TPU v7x, 32 devices: a whole 2x2x4 slice. The times are simulated.
32 devices in a mesh: lon: 4 (over y, x), lat: 8 (over z, core).
Axes of the slice: x: 2, y: 2, z: 4, core: 2. Of those that a mesh axis runs over, the one named last changes fastest.
Arguments:
- sensitivity: float32 [32, 1440, 128], P('lat', 'lon'), may hold values from -6 to 6
- courant_east: float32 [32, 1440, 32], P('lat', 'lon'), may hold values from -0.9 to 0.9
- courant_north: float32 [32, 1440, 32], P('lat', 'lon'), may hold values from -0.9 to 0.9
- mixing: float32 [32, 1440, 31], P('lat', 'lon'), may hold values from 0.05 to 5
- cutoff: int32 [32], P('lat'), may hold values from 4 to 359
- polar_flag: int32 [32], P('lat'), may hold values from 0 to 1, as said below
Outputs:
- adjoint_out: float32 [32, 1440, 128], P('lat', 'lon')
Inputs may be any that keep to these rules, and one draw needn't show every extreme that they name: polar_flag is 1 on a run of rows starting at row 0 and on a run ending at row 31, each of 1 to 8 rows and one of them exactly 8, and 0 elsewhere.
All inputs are finite; a program needn't handle non-finite values.
Results may differ from a plain program's by a relative error of at most 0.0003.
Values sent between devices are 32-bit elements; how exact they have to be, the bound alone decides.
No kernel may reach another device: no remote copies, remote signals or barrier semaphores. Data moves between devices by JAX's collectives and lax.ppermute only.
A program may use at most 64 MiB of HBM per device.

v0:
```python
from functools import partial
import math

import jax
import jax.numpy as jnp
from jax import lax
from jax.sharding import PartitionSpec as P

SUBSTEPS = 2


def partner(block, axis, stride):
    count = lax.axis_size(axis)
    route = []
    for low in range(count):
        high = low | 1 << stride
        if high != low and high < count:
            route += [(low, high), (high, low)]
    return lax.ppermute(block, axis, route)


def padded_2(value, sides, width, wrap):
    for axis, dim in sides:
        count, length = (lax.axis_size(axis), value.shape[dim])
        up = [(i, (i + 1) % count) for i in range(count if wrap else count - 1)]
        down = [(j, i) for i, j in up]
        last = lax.slice_in_dim(value, length - width, length, axis=dim)
        initial = lax.slice_in_dim(value, 0, width, axis=dim)
        before = lax.ppermute(last, axis, up)
        after = lax.ppermute(initial, axis, down)
        value = jnp.concatenate([before, value, after], axis=dim)
    return value


def edge_row(offset):
    row = [0.0] * 6
    row[offset + 2] += 7.0 / 12.0
    row[offset + 3] += 7.0 / 12.0
    row[offset + 1] -= 1.0 / 12.0
    row[offset + 4] -= 1.0 / 12.0
    return row


def flux_weights(courant):
    left_edge = edge_row(-1)
    middle_edge = edge_row(0)
    right_edge = edge_row(1)
    magnitude = jnp.abs(courant)
    result = []
    for position in range(6):
        cell_plus = 1.0 if position == 2 else 0.0
        cell_minus = 1.0 if position == 3 else 0.0
        delta_plus = middle_edge[position] - left_edge[position]
        curve_plus = 6.0 * (cell_plus - 0.5 * (left_edge[position] + middle_edge[position]))
        delta_minus = right_edge[position] - middle_edge[position]
        curve_minus = 6.0 * (cell_minus - 0.5 * (middle_edge[position] + right_edge[position]))
        bend = 1.0 - 2.0 * magnitude / 3.0
        forward_weight = middle_edge[position] - 0.5 * magnitude * (delta_plus - bend * curve_plus)
        backward_weight = middle_edge[position] + 0.5 * magnitude * (
            delta_minus + bend * curve_minus
        )
        result.append(courant * jnp.where(courant >= 0.0, forward_weight, backward_weight))
    return result


def spread_flux(field_ext, courant_ext, axis_dim):
    length = field_ext.shape[axis_dim]
    jump = lax.slice_in_dim(field_ext, 1, length, axis=axis_dim) - lax.slice_in_dim(
        field_ext, 0, length - 1, axis=axis_dim
    )
    weights = flux_weights(lax.slice_in_dim(courant_ext, 0, length - 1, axis=axis_dim))
    padding = [(0, 0)] * jump.ndim
    padding[axis_dim] = (3, 3)
    total = jnp.zeros(field_ext.shape, field_ext.dtype)
    for position in range(6):
        offset = position - 2
        term = jnp.pad(weights[position] * jump, padding)
        total = total + lax.slice_in_dim(term, 3 - offset, 3 - offset + length, axis=axis_dim)
    return total


def solve_setup(mixing, tracers):
    rows, cols, interfaces = mixing.shape
    levels = interfaces + 1
    coef = jnp.moveaxis(mixing, 2, 0)
    nothing = jnp.zeros_like(coef[:1])
    padded = jnp.concatenate([nothing, coef, nothing], axis=0)
    beneath = -padded[:levels]
    overlying = -padded[1:]
    central = 1.0 - beneath - overlying
    factor_prev = jnp.zeros_like(coef[0])
    factor_list = []
    divisor_list = []
    for level in range(levels):
        divisor = central[level] - beneath[level] * factor_prev
        factor = overlying[level] / divisor
        factor_list.append(factor)
        divisor_list.append(divisor)
        factor_prev = factor

    def spread_lanes(values):
        return jnp.broadcast_to(values[..., None], (levels, rows, cols, tracers)).reshape(
            levels, rows * cols * tracers
        )

    return (
        spread_lanes(beneath),
        spread_lanes(jnp.stack(factor_list)),
        spread_lanes(jnp.stack(divisor_list)),
    )


def vertical_apply(field, coeffs, levels):
    rows, cols, channels = field.shape
    tracers = channels // levels
    beneath, factors, divisors = coeffs
    stack = (
        field.reshape(rows, cols, levels, tracers)
        .transpose(2, 0, 1, 3)
        .reshape(levels, rows * cols * tracers)
    )
    partial_prev = jnp.zeros_like(stack[0])
    partials = []
    for level in range(levels):
        partial_now = (stack[level] - beneath[level] * partial_prev) / divisors[level]
        partials.append(partial_now)
        partial_prev = partial_now
    following = jnp.zeros_like(stack[0])
    solved = [None] * levels
    for level in range(levels - 1, -1, -1):
        current = partials[level] - factors[level] * following
        solved[level] = current
        following = current
    result = jnp.stack(solved).reshape(levels, rows, cols, tracers).transpose(1, 2, 0, 3)
    return result.reshape(rows, cols, channels)


def fourier_table(circle):
    halfway = circle // 2
    places = jnp.arange(circle, dtype=jnp.int32)
    columns = jnp.arange(circle, dtype=jnp.int32)
    waves = columns % halfway
    phase = places[:, None] * waves[None, :] % circle
    angle = phase.astype(jnp.float32) * (2.0 * math.pi / circle)
    return jnp.where(columns[None, :] < halfway, jnp.cos(angle), jnp.sin(angle))


def local_setting(cutoff, polar_flag, lat_rows, channels, row_index):
    lat_local = row_index // channels
    chosen = lat_local[:, None] == jnp.arange(lat_rows, dtype=jnp.int32)[None, :]
    row_cut = jnp.sum(jnp.where(chosen, cutoff[None, :], 0), axis=1)
    row_flag = jnp.sum(jnp.where(chosen, polar_flag[None, :], 0), axis=1)
    return (row_cut, row_flag)


def filter_rows(rows, setting, table):
    circles = lax.all_to_all(rows, "lon", split_axis=0, concat_axis=1, tiled=True)
    count = circles.shape[0]
    row_index = lax.axis_index("lon") * count + jnp.arange(count, dtype=jnp.int32)
    row_cut, row_flag = setting(row_index)
    circle = table.shape[0]
    halfway = table.shape[1] // 2
    columns = jnp.arange(table.shape[1], dtype=jnp.int32)
    waves = columns % halfway
    is_sine = columns >= halfway
    scaling = jnp.where(waves == 0, 1.0, 2.0) / circle
    spectra = jnp.dot(
        circles, table, precision=lax.Precision.HIGHEST, preferred_element_type=jnp.float32
    )
    active = (waves[None, :] <= row_cut[:, None]) & jnp.logical_not(is_sine & (waves == 0))[None, :]
    weighted = jnp.where(active, spectra * scaling[None, :], 0.0)
    smooth = lax.dot_general(
        weighted,
        table,
        (((1,), (1,)), ((), ())),
        precision=lax.Precision.HIGHEST,
        preferred_element_type=jnp.float32,
    )
    mixed = jnp.where((row_flag > 0)[:, None], smooth, circles)
    return lax.all_to_all(mixed, "lon", split_axis=1, concat_axis=0, tiled=True)


def widen(courant, tracers):
    return jnp.repeat(courant, tracers, axis=2)


def meridional_core(field_ext, courant_ext, lat_first, lat_total):
    length = field_ext.shape[0]
    face_index = lat_first - 3 + jnp.arange(length, dtype=jnp.int32)
    valid = (face_index >= 0) & (face_index <= lat_total - 2)
    courant_ext = jnp.where(valid[:, None, None], courant_ext, 0.0)
    full = spread_flux(field_ext, courant_ext, 0)
    result = field_ext[3 : length - 3] + full[3 : length - 3]
    ghosts = jnp.concatenate([full[0:3], full[length - 3 :]], axis=0)
    arrived = partner(ghosts, "lon", lax.axis_size("lon").bit_length() - 2)
    lat_index = lax.axis_index("lat")
    south = jnp.where(lat_index == 0, arrived[2::-1], 0.0)
    north = jnp.where(lat_index == lax.axis_size("lat") - 1, arrived[5:2:-1], 0.0)
    result = result.at[0:3].add(south)
    result = result.at[result.shape[0] - 3 :].add(north)
    return result


def on_device(sensitivity, courant_east, courant_north, mixing, cutoff, polar_flag):
    lat_rows, lon_cols, channels = sensitivity.shape
    levels = courant_east.shape[2]
    tracers = channels // levels
    lat_total = lat_rows * lax.axis_size("lat")
    lat_first = lax.axis_index("lat") * lat_rows
    table = fourier_table(lon_cols * lax.axis_size("lon"))
    coeffs = solve_setup(mixing, tracers)
    state = sensitivity
    for substep in range(SUBSTEPS):
        state = vertical_apply(state, coeffs, levels)
        rows = state.transpose(0, 2, 1).reshape(lat_rows * channels, lon_cols)
        setting = partial(local_setting, cutoff, polar_flag, lat_rows, channels)
        state = (
            filter_rows(rows, setting, table)
            .reshape(lat_rows, channels, lon_cols)
            .transpose(0, 2, 1)
        )
        stacked = jnp.concatenate([state, courant_north], axis=2)
        margin = padded_2(stacked, (("lat", 0),), 3, False)
        northward = meridional_core(
            margin[:, :, :channels], widen(margin[:, :, channels:], tracers), lat_first, lat_total
        )
        stacked = jnp.concatenate([northward, courant_east], axis=2)
        margin = padded_2(stacked, (("lon", 1),), 3, True)
        northward = margin[:, :, :channels]
        east_courant = widen(margin[:, :, channels:], tracers)
        state = northward[:, 3:-3] + spread_flux(northward, east_courant, 1)[:, 3:-3]
    return state


def solution(mesh):
    return jax.shard_map(
        on_device,
        mesh=mesh,
        in_specs=(
            P("lat", "lon", None),
            P("lat", "lon", None),
            P("lat", "lon", None),
            P("lat", "lon", None),
            P("lat"),
            P("lat"),
        ),
        out_specs=P("lat", "lon", None),
        check_vma=False,
    )
```

profile of v0, /device:TPU:8, one launch (start us, length us, event | category | flops | bytes accessed | tf_op | source)
XLA Modules:
  0.0 415.4 jit_solution(10514916888348440577)
XLA Ops:
  0.0 1.1 fusion.232
  2.2 0.7 fusion.169
  2.9 0.6 fusion.168
  3.6 0.6 fusion.170
  4.2 0.6 fusion.172
  4.8 0.6 fusion.174
  5.5 0.6 fusion.176
  6.2 1.6 constant_dynamic-update-slice_fusion.31
  8.7 1.2 copy.40
  9.9 3.9 all-to-all-start
  13.8 38.1 %sine_select_fusion.22 = f32[1440,1440]{1,0:T(8,128)} fusion(s32[1440]{0:T(1024)S(1)} %add_select_fusion.1, pred[1440]{0:T(1024)(128)(4,1)S(1)} %get-tuple-element.259), kind=kLoop, calls=%fused_computation.3.clone.3.clone.clone.clone.clone.clone | loop fusion | flops 20736000 | bytes 8301600 | tf_op jit(solution)/shard_map/dot_general | solution.py:167
  52.7 18.1 %fusion.18 = f32[128,1440]{0,1:T(8,128)S(1)} fusion(f32[128,1440]{0,1:T(8,128)S(1)} %bitcast.221, s32[1440]{0:T(1024)S(1)} %add_select_fusion.1, f32[1440]{0:T(1024)S(1)} %select_multiply_fusion, s32[128]{0:T(128)S(1)} %get-tuple-element.54, pred[1440]{0:T(1024)(128)(4,1)S(1)} %get-tuple-element.260, f32[1440,1440]{1,0:T(8,128)} %sine_select_fusion.22), kind=kOutput, calls=%fused_computation.35 | convolution fusion | flops 3185786880 | bytes 9782432 | tf_op jit(solution)/shard_map/dot_general | solution.py:167
  70.8 44.1 %fusion.15 = f32[128,1440]{0,1:T(8,128)S(1)} fusion(f32[128,1440]{0,1:T(8,128)S(1)} %bitcast.222, f32[128,1440]{0,1:T(8,128)S(1)} %fusion.18, s32[1440]{0:T(1024)S(1)} %add_select_fusion.1, pred[1440]{0:T(1024)(128)(4,1)S(1)} %get-tuple-element.259, pred[128]{0:T(512)(128)(4,1)S(1)} %broadcast_compare_fusion.3), kind=kOutput, calls=%fused_computation.32 | convolution fusion | flops 3205969920 | bytes 2219168 | tf_op jit(solution)/shard_map/dot_general | solution.py:172
  114.9 14.5 %all_to_all.58 = f32[128,4,360]{0,2,1:T(8,128)S(1)} all-to-all(f32[128,4,360]{0,2,1:T(8,128)S(1)} %bitcast.228), channel_id=1, replica_groups=mesh['lon'=4,'lat'=8] {'lon'}, dimensions={1} | all-to-all | bytes 1474560 | tf_op jit(solution)/shard_map/all_to_all | solution.py:180
  129.8 2.3 collective-permute-start
  132.2 3.6 collective-permute-start.1
  135.8 0.6 compare_and_fusion.1
  136.4 6.2 %collective-permute-done = f32[3,360,160]{1,2,0:T(8,128)S(1)} collective-permute-done((f32[3,360,160]{1,2,0:T(8,128)S(1)}, f32[3,360,160]{1,2,0:T(8,128)S(1)}, u32[]{:S(2)}, u32[]{:S(2)}) %collective-permute-start) | collective-permute-done | bytes 691232 | tf_op jit(solution)/shard_map/ppermute | solution.py:29
  142.6 0.9 copy-done.7
  143.5 1.3 collective-permute-done.1
  144.8 1.5 fusion.12
  146.3 1.6 broadcast_in_dim.435
  147.9 2.9 reshape.8039
  150.9 2.7 multiply_multiply_fusion.6
  153.5 3.2 multiply_multiply_fusion.7
  157.4 1.2 copy-done.2
  159.2 0.8 collective-permute-start.2
  160.0 1.2 slice_add_fusion.11
  161.2 24.4 %collective-permute-done.2 = f32[6,360,128]{2,1,0:T(8,128)} collective-permute-done((f32[6,360,128]{2,1,0:T(8,128)S(1)}, f32[6,360,128]{2,1,0:T(8,128)}, u32[]{:S(2)}, u32[]{:S(2)}) %collective-permute-start.2) | collective-permute-done | bytes 1105952 | tf_op jit(solution)/shard_map/ppermute | solution.py:19
  185.6 1.3 fusion.231
  187.7 0.6 copy-done.5
  188.4 0.8 collective-permute-start.3
  189.3 2.3 collective-permute-start.4
  191.6 8.4 %collective-permute-done.3 = f32[4,3,160]{1,2,0:T(8,128)S(1)} collective-permute-done((f32[4,3,160]{1,2,0:T(8,128)S(1)}, f32[4,3,160]{1,2,0:T(8,128)S(1)}, u32[]{:S(2)}, u32[]{:S(2)}) %collective-permute-start.3) | collective-permute-done | bytes 7712 | tf_op jit(solution)/shard_map/ppermute | solution.py:29
  200.0 6.2 %collective-permute-done.4 = f32[4,3,160]{1,2,0:T(8,128)S(1)} collective-permute-done((f32[4,3,160]{1,2,0:T(8,128)S(1)}, f32[4,3,160]{1,2,0:T(8,128)S(1)}, u32[]{:S(2)}, u32[]{:S(2)}) %collective-permute-start.4) | collective-permute-done | bytes 7712 | tf_op jit(solution)/shard_map/ppermute | solution.py:30
  207.3 1.4 multiply_multiply_fusion.22
  210.4 1.3 fusion.38
  212.7 1.6 constant_dynamic-update-slice_fusion.63
  214.9 1.2 copy.48
  216.1 3.7 all-to-all-start.2
  219.8 38.1 %sine_select_fusion.21 = f32[1440,1440]{1,0:T(8,128)} fusion(s32[1440]{0:T(1024)S(1)} %copy-done.18, pred[1440]{0:T(1024)(128)(4,1)S(1)} %copy-done.94), kind=kLoop, calls=%fused_computation.3.clone.1.clone.clone.clone.clone.clone.1 | loop fusion | flops 20736000 | bytes 8301600 | tf_op jit(solution)/shard_map/dot_general | solution.py:167
  257.9 18.1 %fusion.17 = f32[128,1440]{0,1:T(8,128)S(1)} fusion(f32[128,1440]{0,1:T(8,128)S(1)} %bitcast.223, s32[1440]{0:T(1024)S(1)} %copy-done.18, f32[1440]{0:T(1024)S(1)} %copy-done.52, s32[128]{0:T(128)S(1)} %copy-done.98, pred[1440]{0:T(1024)(128)(4,1)S(1)} %copy-done.92, f32[1440,1440]{1,0:T(8,128)} %sine_select_fusion.21), kind=kOutput, calls=%fused_computation.34 | convolution fusion | flops 3185786880 | bytes 9782432 | tf_op jit(solution)/shard_map/dot_general | solution.py:167
  276.0 44.3 %fusion.16 = f32[128,1440]{0,1:T(8,128)S(1)} fusion(f32[128,1440]{0,1:T(8,128)S(1)} %bitcast.224, f32[128,1440]{0,1:T(8,128)S(1)} %fusion.17, s32[1440]{0:T(1024)S(1)} %copy-done.18, pred[1440]{0:T(1024)(128)(4,1)S(1)} %copy-done.94, pred[128]{0:T(512)(128)(4,1)S(1)} %copy-done.102), kind=kOutput, calls=%fused_computation.33 | convolution fusion | flops 3205969920 | bytes 2219168 | tf_op jit(solution)/shard_map/dot_general | solution.py:172
  320.4 14.7 %all_to_all.59 = f32[128,4,360]{0,2,1:T(8,128)S(1)} all-to-all(f32[128,4,360]{0,2,1:T(8,128)S(1)} %bitcast.227), channel_id=1, replica_groups=mesh['lon'=4,'lat'=8] {'lon'}, dimensions={1} | all-to-all | bytes 1474560 | tf_op jit(solution)/shard_map/all_to_all | solution.py:180
  335.5 2.1 collective-permute-start.5
  337.6 3.6 collective-permute-start.6
  341.2 7.0 %collective-permute-done.5 = f32[3,360,160]{1,2,0:T(8,128)S(1)} collective-permute-done((f32[3,360,160]{1,2,0:T(8,128)S(1)}, f32[3,360,160]{1,2,0:T(8,128)S(1)}, u32[]{:S(2)}, u32[]{:S(2)}) %collective-permute-start.5) | collective-permute-done | bytes 691232 | tf_op jit(solution)/shard_map/ppermute | solution.py:29
  348.3 1.9 collective-permute-done.6
  350.4 1.6 broadcast_in_dim.439
  352.0 2.9 reshape.8043
  354.9 2.7 multiply_multiply_fusion
  357.6 3.2 multiply_multiply_fusion.1
  361.4 1.2 copy-done.3
  363.2 0.8 collective-permute-start.7
  364.1 1.2 slice_add_fusion.5
  365.3 24.4 %collective-permute-done.7 = f32[6,360,128]{2,1,0:T(8,128)S(1)} collective-permute-done((f32[6,360,128]{2,1,0:T(8,128)S(1)}, f32[6,360,128]{2,1,0:T(8,128)S(1)}, u32[]{:S(2)}, u32[]{:S(2)}) %collective-permute-start.7) | collective-permute-done | bytes 1105952 | tf_op jit(solution)/shard_map/ppermute | solution.py:19
  390.6 0.6 copy-done.6
  391.3 0.8 collective-permute-start.8
  392.2 2.1 collective-permute-start.9
  394.3 8.6 %collective-permute-done.8 = f32[4,3,160]{1,2,0:T(8,128)S(1)} collective-permute-done((f32[4,3,160]{1,2,0:T(8,128)S(1)}, f32[4,3,160]{1,2,0:T(8,128)S(1)}, u32[]{:S(2)}, u32[]{:S(2)}) %collective-permute-start.8) | collective-permute-done | bytes 7712 | tf_op jit(solution)/shard_map/ppermute | solution.py:29
  402.9 6.1 %collective-permute-done.9 = f32[4,3,160]{1,2,0:T(8,128)S(1)} collective-permute-done((f32[4,3,160]{1,2,0:T(8,128)S(1)}, f32[4,3,160]{1,2,0:T(8,128)S(1)}, u32[]{:S(2)}, u32[]{:S(2)}) %collective-permute-start.9) | collective-permute-done | bytes 7712 | tf_op jit(solution)/shard_map/ppermute | solution.py:30
  410.0 1.4 multiply_multiply_fusion.16
  412.8 1.3 fusion.37
  414.1 1.1 copy.55
  (324 shorter events, 13.3 us)
Async XLA Ops:
  1.2 4.9 %copy-start.53 = (f32[4,360]{1,0:T(4,128)}, f32[4,360]{1,0:T(4,128)S(1)}, u32[]{:S(2)}) copy-start(f32[4,360]{1,0:T(4,128)S(1)} %get-tuple-element.243) | copy-start | bytes 17284
  1.2 4.9 %copy-start.55 = (f32[4,360]{1,0:T(4,128)}, f32[4,360]{1,0:T(4,128)S(1)}, u32[]{:S(2)}) copy-start(f32[4,360]{1,0:T(4,128)S(1)} %get-tuple-element.244) | copy-start | bytes 17284
  1.2 4.9 %copy-start.57 = (f32[4,360]{1,0:T(4,128)}, f32[4,360]{1,0:T(4,128)S(1)}, u32[]{:S(2)}) copy-start(f32[4,360]{1,0:T(4,128)S(1)} %get-tuple-element.245) | copy-start | bytes 17284
  1.2 4.9 %copy-start.59 = (f32[4,360]{1,0:T(4,128)}, f32[4,360]{1,0:T(4,128)S(1)}, u32[]{:S(2)}) copy-start(f32[4,360]{1,0:T(4,128)S(1)} %get-tuple-element.246) | copy-start | bytes 17284
  1.2 4.9 %copy-start.61 = (f32[4,360]{1,0:T(4,128)}, f32[4,360]{1,0:T(4,128)S(1)}, u32[]{:S(2)}) copy-start(f32[4,360]{1,0:T(4,128)S(1)} %get-tuple-element.247) | copy-start | bytes 17284
  1.2 4.9 %copy-start.63 = (f32[4,360]{1,0:T(4,128)}, f32[4,360]{1,0:T(4,128)S(1)}, u32[]{:S(2)}) copy-start(f32[4,360]{1,0:T(4,128)S(1)} %get-tuple-element.248) | copy-start | bytes 17284
  1.2 4.9 %copy-start.65 = (f32[4,360]{1,0:T(4,128)}, f32[4,360]{1,0:T(4,128)S(1)}, u32[]{:S(2)}) copy-start(f32[4,360]{1,0:T(4,128)S(1)} %get-tuple-element.249) | copy-start | bytes 17284
  1.2 4.9 %copy-start.67 = (f32[4,360]{1,0:T(4,128)}, f32[4,360]{1,0:T(4,128)S(1)}, u32[]{:S(2)}) copy-start(f32[4,360]{1,0:T(4,128)S(1)} %get-tuple-element.250) | copy-start | bytes 17284
  1.2 4.9 %copy-start.69 = (f32[4,360]{1,0:T(4,128)}, f32[4,360]{1,0:T(4,128)S(1)}, u32[]{:S(2)}) copy-start(f32[4,360]{1,0:T(4,128)S(1)} %get-tuple-element.251) | copy-start | bytes 17284
  1.3 4.9 %copy-start.71 = (f32[4,360]{1,0:T(4,128)}, f32[4,360]{1,0:T(4,128)S(1)}, u32[]{:S(2)}) copy-start(f32[4,360]{1,0:T(4,128)S(1)} %get-tuple-element.252) | copy-start | bytes 17284
  1.3 4.9 %copy-start.73 = (f32[4,360]{1,0:T(4,128)}, f32[4,360]{1,0:T(4,128)S(1)}, u32[]{:S(2)}) copy-start(f32[4,360]{1,0:T(4,128)S(1)} %get-tuple-element.253) | copy-start | bytes 17284
  1.3 4.9 %copy-start.75 = (f32[4,360]{1,0:T(4,128)}, f32[4,360]{1,0:T(4,128)S(1)}, u32[]{:S(2)}) copy-start(f32[4,360]{1,0:T(4,128)S(1)} %get-tuple-element.254) | copy-start | bytes 17284
  1.3 4.9 %copy-start.77 = (f32[4,360]{1,0:T(4,128)}, f32[4,360]{1,0:T(4,128)S(1)}, u32[]{:S(2)}) copy-start(f32[4,360]{1,0:T(4,128)S(1)} %get-tuple-element.255) | copy-start | bytes 17284
  1.3 4.9 %copy-start.79 = (f32[4,360]{1,0:T(4,128)}, f32[4,360]{1,0:T(4,128)S(1)}, u32[]{:S(2)}) copy-start(f32[4,360]{1,0:T(4,128)S(1)} %get-tuple-element.256) | copy-start | bytes 17284
  1.7 6.1 %copy-start.19 = (f32[1,4,360]{2,1,0:T(4,128)}, f32[1,4,360]{2,1,0:T(4,128)S(1)}, u32[]{:S(2)}) copy-start(f32[1,4,360]{2,1,0:T(4,128)S(1)} %get-tuple-element.127) | copy-start | bytes 17284
  1.7 6.1 %copy-start.21 = (f32[1,4,360]{2,1,0:T(4,128)}, f32[1,4,360]{2,1,0:T(4,128)S(1)}, u32[]{:S(2)}) copy-start(f32[1,4,360]{2,1,0:T(4,128)S(1)} %get-tuple-element.129) | copy-start | bytes 17284
  1.7 6.1 %copy-start.23 = (f32[1,4,360]{2,1,0:T(4,128)}, f32[1,4,360]{2,1,0:T(4,128)S(1)}, u32[]{:S(2)}) copy-start(f32[1,4,360]{2,1,0:T(4,128)S(1)} %get-tuple-element.131) | copy-start | bytes 17284
  1.7 6.1 %copy-start.25 = (f32[1,4,360]{2,1,0:T(4,128)}, f32[1,4,360]{2,1,0:T(4,128)S(1)}, u32[]{:S(2)}) copy-start(f32[1,4,360]{2,1,0:T(4,128)S(1)} %get-tuple-element.133) | copy-start | bytes 17284
  1.8 6.1 %copy-start.27 = (f32[1,4,360]{2,1,0:T(4,128)}, f32[1,4,360]{2,1,0:T(4,128)S(1)}, u32[]{:S(2)}) copy-start(f32[1,4,360]{2,1,0:T(4,128)S(1)} %get-tuple-element.135) | copy-start | bytes 17284
  1.8 6.1 %copy-start.29 = (f32[1,4,360]{2,1,0:T(4,128)}, f32[1,4,360]{2,1,0:T(4,128)S(1)}, u32[]{:S(2)}) copy-start(f32[1,4,360]{2,1,0:T(4,128)S(1)} %get-tuple-element.137) | copy-start | bytes 17284
  1.8 6.1 %copy-start.31 = (f32[1,4,360]{2,1,0:T(4,128)}, f32[1,4,360]{2,1,0:T(4,128)S(1)}, u32[]{:S(2)}) copy-start(f32[1,4,360]{2,1,0:T(4,128)S(1)} %get-tuple-element.139) | copy-start | bytes 17284
  1.8 6.1 %copy-start.33 = (f32[1,4,360]{2,1,0:T(4,128)}, f32[1,4,360]{2,1,0:T(4,128)S(1)}, u32[]{:S(2)}) copy-start(f32[1,4,360]{2,1,0:T(4,128)S(1)} %get-tuple-element.141) | copy-start | bytes 17284
  1.8 6.1 %copy-start.35 = (f32[1,4,360]{2,1,0:T(4,128)}, f32[1,4,360]{2,1,0:T(4,128)S(1)}, u32[]{:S(2)}) copy-start(f32[1,4,360]{2,1,0:T(4,128)S(1)} %get-tuple-element.143) | copy-start | bytes 17284
  1.8 6.1 %copy-start.37 = (f32[1,4,360]{2,1,0:T(4,128)}, f32[1,4,360]{2,1,0:T(4,128)S(1)}, u32[]{:S(2)}) copy-start(f32[1,4,360]{2,1,0:T(4,128)S(1)} %get-tuple-element.145) | copy-start | bytes 17284
  1.8 6.1 %copy-start.39 = (f32[1,4,360]{2,1,0:T(4,128)}, f32[1,4,360]{2,1,0:T(4,128)S(1)}, u32[]{:S(2)}) copy-start(f32[1,4,360]{2,1,0:T(4,128)S(1)} %get-tuple-element.147) | copy-start | bytes 17284
  1.8 6.1 %copy-start.41 = (f32[1,4,360]{2,1,0:T(4,128)}, f32[1,4,360]{2,1,0:T(4,128)S(1)}, u32[]{:S(2)}) copy-start(f32[1,4,360]{2,1,0:T(4,128)S(1)} %get-tuple-element.149) | copy-start | bytes 17284
  1.8 6.1 %copy-start.43 = (f32[1,4,360]{2,1,0:T(4,128)}, f32[1,4,360]{2,1,0:T(4,128)S(1)}, u32[]{:S(2)}) copy-start(f32[1,4,360]{2,1,0:T(4,128)S(1)} %get-tuple-element.151) | copy-start | bytes 17284
  1.8 6.1 %copy-start.45 = (f32[1,4,360]{2,1,0:T(4,128)}, f32[1,4,360]{2,1,0:T(4,128)S(1)}, u32[]{:S(2)}) copy-start(f32[1,4,360]{2,1,0:T(4,128)S(1)} %get-tuple-element.153) | copy-start | bytes 17284
  1.9 6.1 %copy-start.47 = (f32[1,4,360]{2,1,0:T(4,128)}, f32[1,4,360]{2,1,0:T(4,128)S(1)}, u32[]{:S(2)}) copy-start(f32[1,4,360]{2,1,0:T(4,128)S(1)} %get-tuple-element.155) | copy-start | bytes 17284
  1.9 6.1 %copy-start.49 = (f32[1,4,360]{2,1,0:T(4,128)}, f32[1,4,360]{2,1,0:T(4,128)S(1)}, u32[]{:S(2)}) copy-start(f32[1,4,360]{2,1,0:T(4,128)S(1)} %get-tuple-element.156) | copy-start | bytes 17284
  1.9 6.1 %copy-start.15 = (f32[1,4,360]{2,1,0:T(4,128)}, f32[1,4,360]{2,1,0:T(4,128)S(1)}, u32[]{:S(2)}) copy-start(f32[1,4,360]{2,1,0:T(4,128)S(1)} %get-tuple-element.154) | copy-start | bytes 17284
  1.9 6.2 %copy-start.13 = (f32[1,4,360]{2,1,0:T(4,128)}, f32[1,4,360]{2,1,0:T(4,128)S(1)}, u32[]{:S(2)}) copy-start(f32[1,4,360]{2,1,0:T(4,128)S(1)} %get-tuple-element.152) | copy-start | bytes 17284
  1.9 6.2 %copy-start.11 = (f32[1,4,360]{2,1,0:T(4,128)}, f32[1,4,360]{2,1,0:T(4,128)S(1)}, u32[]{:S(2)}) copy-start(f32[1,4,360]{2,1,0:T(4,128)S(1)} %get-tuple-element.150) | copy-start | bytes 17284
  1.9 6.3 %copy-start.9 = (f32[1,4,360]{2,1,0:T(4,128)}, f32[1,4,360]{2,1,0:T(4,128)S(1)}, u32[]{:S(2)}) copy-start(f32[1,4,360]{2,1,0:T(4,128)S(1)} %get-tuple-element.148) | copy-start | bytes 17284
  2.9 5.2 %copy-start.81 = (f32[4,360]{1,0:T(4,128)}, f32[4,360]{1,0:T(4,128)S(1)}, u32[]{:S(2)}) copy-start(f32[4,360]{1,0:T(4,128)S(1)} %get-tuple-element.223) | copy-start | bytes 17284
  2.9 5.2 %copy-start.83 = (f32[4,360]{1,0:T(4,128)}, f32[4,360]{1,0:T(4,128)S(1)}, u32[]{:S(2)}) copy-start(f32[4,360]{1,0:T(4,128)S(1)} %get-tuple-element.224) | copy-start | bytes 17284
  2.9 5.2 %copy-start.85 = (f32[4,360]{1,0:T(4,128)}, f32[4,360]{1,0:T(4,128)S(1)}, u32[]{:S(2)}) copy-start(f32[4,360]{1,0:T(4,128)S(1)} %get-tuple-element.230) | copy-start | bytes 17284
  2.9 5.2 %copy-start.87 = (f32[4,360]{1,0:T(4,128)}, f32[4,360]{1,0:T(4,128)S(1)}, u32[]{:S(2)}) copy-start(f32[4,360]{1,0:T(4,128)S(1)} %get-tuple-element.231) | copy-start | bytes 17284
  2.9 5.2 %copy-start.89 = (f32[4,360]{1,0:T(4,128)}, f32[4,360]{1,0:T(4,128)S(1)}, u32[]{:S(2)}) copy-start(f32[4,360]{1,0:T(4,128)S(1)} %get-tuple-element.232) | copy-start | bytes 17284
  9.9 42.3 %all-to-all-start = ((f32[4,128,360]{1,2,0:T(8,128)}), f32[4,128,360]{1,2,0:T(8,128)S(1)}, u32[]{:S(2)}, u32[]{:S(2)}) async-start(f32[4,128,360]{1,2,0:T(8,128)} %copy.40), calls=%async_computation | async-start | bytes 1474560 | tf_op jit(solution)/shard_map/all_to_all | solution.py:157
  13.8 57.0 %copy-start.17 = (s32[1440]{0:T(1024)}, s32[1440]{0:T(1024)S(1)}, u32[]{:S(2)}) copy-start(s32[1440]{0:T(1024)S(1)} %add_select_fusion.1) | copy-start | bytes 17284
  13.8 38.3 %copy-start.91 = (pred[1440]{0:T(1024)(128)(4,1)}, pred[1440]{0:T(1024)(128)(4,1)S(1)}, u32[]{:S(2)}) copy-start(pred[1440]{0:T(1024)(128)(4,1)S(1)} %get-tuple-element.260) | copy-start | bytes 4324
  13.8 56.9 %copy-start.93 = (pred[1440]{0:T(1024)(128)(4,1)}, pred[1440]{0:T(1024)(128)(4,1)S(1)}, u32[]{:S(2)}) copy-start(pred[1440]{0:T(1024)(128)(4,1)S(1)} %get-tuple-element.259) | copy-start | bytes 4324
  13.8 38.1 %copy-start.99 = (s32[4]{0:T(128)S(1)}, s32[4]{0:T(128)}, u32[]{:S(2)}) copy-start(s32[4]{0:T(128)} %param.19) | copy-start | bytes 52
  13.8 38.1 %copy-start.100 = (s32[4]{0:T(128)S(1)}, s32[4]{0:T(128)}, u32[]{:S(2)}) copy-start(s32[4]{0:T(128)} %param.18) | copy-start | bytes 52
  52.1 18.6 %copy-start.101 = (pred[128]{0:T(512)(128)(4,1)}, pred[128]{0:T(512)(128)(4,1)S(1)}, u32[]{:S(2)}) copy-start(pred[128]{0:T(512)(128)(4,1)S(1)} %broadcast_compare_fusion.3) | copy-start | bytes 388
  114.9 14.8 %copy-start.4 = (f32[4,360,32]{1,2,0:T(8,128)S(1)}, f32[4,360,32]{1,2,0:T(8,128)}, u32[]{:S(2)}) copy-start(f32[4,360,32]{1,2,0:T(8,128)} %param.16) | copy-start | bytes 552964
  129.8 12.8 %collective-permute-start = (f32[3,360,160]{1,2,0:T(8,128)S(1)}, f32[3,360,160]{1,2,0:T(8,128)S(1)}, u32[]{:S(2)}, u32[]{:S(2)}) collective-permute-start(f32[3,360,160]{1,2,0:T(8,128)S(1)} %get-tuple-element.191), channel_id=1, source_target_pairs={{0,1},{1,2},{2,3},{3,4},{4,5},{5,6},{6,7},{8,9},{9,10},{10,11},{11... | collective-permute-start | bytes 2073608 | tf_op jit(solution)/shard_map/ppermute | solution.py:29
  132.2 12.6 %collective-permute-start.1 = (f32[3,360,160]{1,2,0:T(8,128)S(1)}, f32[3,360,160]{1,2,0:T(8,128)}, u32[]{:S(2)}, u32[]{:S(2)}) collective-permute-start(f32[3,360,160]{1,2,0:T(8,128)S(1)} %get-tuple-element.192), channel_id=1, source_target_pairs={{1,0},{2,1},{3,2},{4,3},{5,4},{6,5},{7,6},{9,8},{10,9},{11,10},{12... | collective-permute-start | bytes 2073608 | tf_op jit(solution)/shard_map/ppermute | solution.py:30
  159.2 26.4 %collective-permute-start.2 = (f32[6,360,128]{2,1,0:T(8,128)S(1)}, f32[6,360,128]{2,1,0:T(8,128)}, u32[]{:S(2)}, u32[]{:S(2)}) collective-permute-start(f32[6,360,128]{2,1,0:T(8,128)S(1)} %copy.42), channel_id=1, source_target_pairs={{0,16},{16,0},{8,24},{24,8},{1,17},{17,1},{9,25},{25,9},{2,18},{18... | collective-permute-start | bytes 3317768 | tf_op jit(solution)/shard_map/ppermute | solution.py:19
  188.4 11.5 %collective-permute-start.3 = (f32[4,3,160]{1,2,0:T(8,128)S(1)}, f32[4,3,160]{1,2,0:T(8,128)S(1)}, u32[]{:S(2)}, u32[]{:S(2)}) collective-permute-start(f32[4,3,160]{1,2,0:T(8,128)S(1)} %get-tuple-element.189), channel_id=1, source_target_pairs={{0,8},{8,16},{16,24},{24,0},{1,9},{9,17},{17,25},{25,1},{2,10},{10... | collective-permute-start | bytes 23048 | tf_op jit(solution)/shard_map/ppermute | solution.py:29
  189.3 16.9 %collective-permute-start.4 = (f32[4,3,160]{1,2,0:T(8,128)S(1)}, f32[4,3,160]{1,2,0:T(8,128)S(1)}, u32[]{:S(2)}, u32[]{:S(2)}) collective-permute-start(f32[4,3,160]{1,2,0:T(8,128)S(1)} %get-tuple-element.190), channel_id=1, source_target_pairs={{8,0},{16,8},{24,16},{0,24},{9,1},{17,9},{25,17},{1,25},{10,2},{18... | collective-permute-start | bytes 23048 | tf_op jit(solution)/shard_map/ppermute | solution.py:30
  214.7 5.1 %copy-start.18 = (s32[1440]{0:T(1024)S(1)}, s32[1440]{0:T(1024)}, u32[]{:S(2)}) copy-start(s32[1440]{0:T(1024)} %copy-done.17) | copy-start | bytes 17284
  214.7 5.1 %copy-start.94 = (pred[1440]{0:T(1024)(128)(4,1)S(1)}, pred[1440]{0:T(1024)(128)(4,1)}, u32[]{:S(2)}) copy-start(pred[1440]{0:T(1024)(128)(4,1)} %copy-done.93) | copy-start | bytes 4324
  216.1 41.9 %all-to-all-start.2 = ((f32[4,128,360]{1,2,0:T(8,128)}), f32[4,128,360]{1,2,0:T(8,128)S(1)}, u32[]{:S(2)}, u32[]{:S(2)}) async-start(f32[4,128,360]{1,2,0:T(8,128)} %copy.48), calls=%async_computation.2 | async-start | bytes 1474560 | tf_op jit(solution)/shard_map/all_to_all | solution.py:157
  219.8 38.1 %copy-start.52 = (f32[1440]{0:T(1024)S(1)}, f32[1440]{0:T(1024)}, u32[]{:S(2)}) copy-start(f32[1440]{0:T(1024)} %copy-done.51) | copy-start | bytes 17284
  219.8 38.1 %copy-start.92 = (pred[1440]{0:T(1024)(128)(4,1)S(1)}, pred[1440]{0:T(1024)(128)(4,1)}, u32[]{:S(2)}) copy-start(pred[1440]{0:T(1024)(128)(4,1)} %copy-done.91) | copy-start | bytes 4324
  219.8 38.1 %copy-start.98 = (s32[128]{0:T(128)S(1)}, s32[128]{0:T(128)}, u32[]{:S(2)}) copy-start(s32[128]{0:T(128)} %copy-done.97) | copy-start | bytes 1540
  257.9 18.1 %copy-start.102 = (pred[128]{0:T(512)(128)(4,1)S(1)}, pred[128]{0:T(512)(128)(4,1)}, u32[]{:S(2)}) copy-start(pred[128]{0:T(512)(128)(4,1)} %copy-done.101) | copy-start | bytes 388
  335.5 12.8 %collective-permute-start.5 = (f32[3,360,160]{1,2,0:T(8,128)S(1)}, f32[3,360,160]{1,2,0:T(8,128)S(1)}, u32[]{:S(2)}, u32[]{:S(2)}) collective-permute-start(f32[3,360,160]{1,2,0:T(8,128)S(1)} %get-tuple-element.187), channel_id=1, source_target_pairs={{0,1},{1,2},{2,3},{3,4},{4,5},{5,6},{6,7},{8,9},{9,10},{10,11},{11... | collective-permute-start | bytes 2073608 | tf_op jit(solution)/shard_map/ppermute | solution.py:29
  337.6 12.6 %collective-permute-start.6 = (f32[3,360,160]{1,2,0:T(8,128)S(1)}, f32[3,360,160]{1,2,0:T(8,128)S(1)}, u32[]{:S(2)}, u32[]{:S(2)}) collective-permute-start(f32[3,360,160]{1,2,0:T(8,128)S(1)} %get-tuple-element.188), channel_id=1, source_target_pairs={{1,0},{2,1},{3,2},{4,3},{5,4},{6,5},{7,6},{9,8},{10,9},{11,10},{12... | collective-permute-start | bytes 2073608 | tf_op jit(solution)/shard_map/ppermute | solution.py:30
  363.2 26.5 %collective-permute-start.7 = (f32[6,360,128]{2,1,0:T(8,128)S(1)}, f32[6,360,128]{2,1,0:T(8,128)S(1)}, u32[]{:S(2)}, u32[]{:S(2)}) collective-permute-start(f32[6,360,128]{2,1,0:T(8,128)S(1)} %copy.50), channel_id=1, source_target_pairs={{0,16},{16,0},{8,24},{24,8},{1,17},{17,1},{9,25},{25,9},{2,18},{18... | collective-permute-start | bytes 3317768 | tf_op jit(solution)/shard_map/ppermute | solution.py:19
  391.3 11.5 %collective-permute-start.8 = (f32[4,3,160]{1,2,0:T(8,128)S(1)}, f32[4,3,160]{1,2,0:T(8,128)S(1)}, u32[]{:S(2)}, u32[]{:S(2)}) collective-permute-start(f32[4,3,160]{1,2,0:T(8,128)S(1)} %get-tuple-element.185), channel_id=1, source_target_pairs={{0,8},{8,16},{16,24},{24,0},{1,9},{9,17},{17,25},{25,1},{2,10},{10... | collective-permute-start | bytes 23048 | tf_op jit(solution)/shard_map/ppermute | solution.py:29
  392.2 16.7 %collective-permute-start.9 = (f32[4,3,160]{1,2,0:T(8,128)S(1)}, f32[4,3,160]{1,2,0:T(8,128)S(1)}, u32[]{:S(2)}, u32[]{:S(2)}) collective-permute-start(f32[4,3,160]{1,2,0:T(8,128)S(1)} %get-tuple-element.186), channel_id=1, source_target_pairs={{8,0},{16,8},{24,16},{0,24},{9,1},{17,9},{25,17},{1,25},{10,2},{18... | collective-permute-start | bytes 23048 | tf_op jit(solution)/shard_map/ppermute | solution.py:30
  (51 other events, 105.6 us)
where the time goes:
time: 419 us; the launch traced here: 415 us
  matrix products  125 us (30%)
  other arithmetic  110 us (26%)
  waiting for transfers between devices  94.5 us (23%)
  blocking collectives  29.3 us (7%)
  local copies, waits for them, and re-layouts  27.4 us (7%)
  starting transfers between devices  27.1 us (6%)
    dot_general x2, matrix products, filter_rows(): lax.dot_general(weighted, table, (((1,), (1,)), ((), ())), precision=lax....  88.5 us
    dot_general x2, other arithmetic, filter_rows(): jnp.dot(circles, table, precision=lax.Precision.HIGHEST, preferred_elemen...  76.2 us
    ppermute x2, waiting for transfers between devices, partner(): return lax.ppermute(block, axis, route)  48.8 us
    dot_general x2, matrix products, filter_rows(): jnp.dot(circles, table, precision=lax.Precision.HIGHEST, preferred_elemen...  36.1 us
    ppermute x4, waiting for transfers between devices, padded_2(): before = lax.ppermute(last, axis, up)  30.2 us
    all_to_all x2, blocking collectives, filter_rows(): return lax.all_to_all(mixed, 'lon', split_axis=1, concat_axis=0, tiled=True)  29.3 us
    ppermute x4, waiting for transfers between devices, padded_2(): after = lax.ppermute(initial, axis, down)  15.5 us
    mul x8, other arithmetic, spread_flux(): term = jnp.pad(weights[position] * jump, padding)  15.4 us
  transfers between devices with their start and end apart: 12, of which 10 were waited for; matrix products, arithmetic and copies ran while one was open for 19% of the time, Pallas kernels for 0%

commit v1 on v0

v1 whole, which is shorter than its diff:
```python
from functools import partial
import math

import jax
import jax.numpy as jnp
import ml_dtypes
import numpy as np
from jax import lax
from jax.experimental import pallas as pl
from jax.experimental.pallas import tpu as pltpu
from jax.sharding import PartitionSpec as P

SUBSTEPS = 2
QUARTERS = 4
HALO = 3
SUB = 8
f32 = jnp.float32
bf16 = jnp.bfloat16


def round_up(n, k):
    return -(-n // k) * k


def fourier_tables(nlon, wide):
    quarter = nlon // 4
    top = nlon // 4 - 1
    even = list(range(0, top + 1, 2))
    odd = list(range(1, top + 1, 2))
    width = round_up(2 * max(len(even), len(odd)), 128)
    x = np.arange(2 * quarter)
    place = (x // quarter) * wide + x % quarter
    result = []
    for waves in (even, odd):
        k = np.array(waves, np.int64)
        angle = (x[:, None] * k[None, :] % nlon) * (2.0 * math.pi / nlon)
        scale = np.where(k == 0, 1.0, 2.0) / nlon
        ahead = np.zeros((2 * wide, width))
        back = np.zeros((width, 2 * wide))
        index = np.full((1, width), nlon, np.int32)
        n = len(waves)
        ahead[place, :n] = np.cos(angle)
        ahead[place, n : 2 * n] = np.sin(angle)
        back[:n, place] = (np.cos(angle) * scale).T
        back[n : 2 * n, place] = (np.sin(angle) * scale).T
        index[0, :n] = k
        index[0, n : 2 * n] = k
        parts = []
        for table in (ahead, back):
            high = table.astype(np.float32).astype(ml_dtypes.bfloat16)
            low = (table - high.astype(np.float64)).astype(np.float32).astype(ml_dtypes.bfloat16)
            parts += [high, low]
        result += parts + [index]
    return result


def split(x):
    high = x.astype(bf16)
    return high, (x - high.astype(f32)).astype(bf16)


def product(high, low, t_high, t_low):
    total = jnp.dot(high, t_high, preferred_element_type=f32)
    total = total + jnp.dot(low, t_high, preferred_element_type=f32)
    return total + jnp.dot(high, t_low, preferred_element_type=f32)


def column_factors(mix_at, levels, shape, store):
    zero = jnp.zeros(shape, f32)
    h_before = zero
    below = zero
    for level in range(levels):
        above = mix_at(level) if level < levels - 1 else zero
        divisor = 1.0 + below + above - below * h_before
        g = 1.0 / divisor
        h = above * g
        store(level, g, below * g, h)
        h_before = h
        below = above


def column_solve(v, g, a, h):
    n = len(v)
    y = [g[0] * v[0]]
    carry = [a[0]]
    for q in range(1, n):
        y.append(g[q] * v[q] + a[q] * y[q - 1])
        carry.append(a[q] * carry[q - 1])
    z, p = y[n - 1], carry[n - 1]
    step = 1
    while step < SUB:
        z = z + p * pltpu.roll(z, step, 0)
        if 2 * step < SUB:
            p = p * pltpu.roll(p, step, 0)
        step *= 2
    before = pltpu.roll(z, 1, 0)
    y = [y[q] + carry[q] * before for q in range(n - 1)] + [z]
    x = [None] * n
    back = [None] * n
    x[n - 1] = y[n - 1]
    back[n - 1] = h[n - 1]
    for q in range(n - 2, -1, -1):
        x[q] = y[q] + h[q] * x[q + 1]
        back[q] = h[q] * back[q + 1]
    z, p = x[0], back[0]
    step = 1
    while step < SUB:
        z = z + p * pltpu.roll(z, SUB - step, 0)
        if 2 * step < SUB:
            p = p * pltpu.roll(p, SUB - step, 0)
        step *= 2
    after = pltpu.roll(z, SUB - 1, 0)
    return [z] + [x[q] + back[q] * after for q in range(1, n)]


def put(ref, at, value):
    for c in range(ref.shape[0]):
        n = min(128, value.shape[1] - c * 128)
        ref[c, at, :n] = value[:, c * 128 : c * 128 + n]


def get(ref, at):
    return jnp.concatenate([ref[c, at, :] for c in range(ref.shape[0])], axis=1)


def clear(*refs):
    for ref in refs:
        ref[...] = jnp.zeros(ref.shape, f32)


def factor_scratch(rows, levels, wide):
    return [(wide // 128, rows * levels, 128)] * 3


def first_solve_kernel(tiles, order, sens, mix, *refs):
    rows, width, channels = sens.shape
    levels = mix.shape[0] + 1
    tracers = channels // levels
    outs = refs[:tracers]
    turned, mixed, g_s, a_s, h_s = refs[tracers:]
    wide = mixed.shape[2]
    if wide != width:
        clear(turned, mixed)
    mixed[:, :, :width] = mix[...]

    def store(level, g, a, h):
        at = pl.ds((level % tiles) * SUB + level // tiles, rows, stride=levels)
        for s, value in ((g_s, g), (a_s, a), (h_s, h)):
            put(s, at, value)

    column_factors(lambda l: mixed[l], levels, (rows, wide), store)
    for r in range(rows):
        put(turned, slice(0, channels), sens[r].T)
        at = lambda q: slice(r * levels + q * SUB, r * levels + q * SUB + SUB)
        g, a, h = ([get(s, at(q)) for q in range(tiles)] for s in (g_s, a_s, h_s))
        for j in range(tracers):
            t = order[j]
            v = [get(turned, pl.ds(q * tracers + t, SUB, stride=tiles * tracers)) for q in range(tiles)]
            x = column_solve(v, g, a, h)
            for q in range(tiles):
                outs[j][r, q] = x[q]


def pack_rows(src, turned, tiles, emit):
    rows, levels, width = src.shape
    for r in range(rows):
        put(turned, slice(r * levels, (r + 1) * levels), src[r])
    for r in range(rows):
        for q in range(tiles):
            emit(r, q, get(turned, pl.ds(r * levels + q, SUB, stride=tiles)))


def pack_levels_kernel(tiles, src, out, turned):
    clear(turned)

    def emit(r, q, value):
        out[r, q] = value

    pack_rows(src, turned, tiles, emit)


def pack_both_kernel(tiles, src, mix, out, turned):
    rows, levels, width = src.shape
    clear(turned)
    out[1] = jnp.zeros(out.shape[1:], f32)

    def emit(r, q, value):
        out[0, r * tiles + q] = value

    pack_rows(src, turned, tiles, emit)
    per = SUB // rows
    for level in range(levels - 1):
        at = level % per * rows
        out[1, level // per, at : at + rows, :width] = mix[level]


def unpack_kernel(tiles, order, *refs):
    n = len(refs) - 2
    pieces, out, turned = refs[:n], refs[n], refs[n + 1]
    rows, width, channels = out.shape
    for r in range(rows):
        for j in range(n):
            t = order[j]
            for q in range(tiles):
                put(turned, pl.ds(q * n + t, SUB, stride=tiles * n), pieces[j][r, q])
        out[r] = get(turned, slice(0, channels))[:, :width].T


def filter_block(field, tables, cut, flag, emit):
    rows, groups, sub, wide = field.shape
    tiles = groups // QUARTERS
    levels = tiles * sub
    quarter = [
        field[:, q * tiles : (q + 1) * tiles].reshape(rows * levels, wide) for q in range(QUARTERS)
    ]
    halves = []
    for sign in (0, 1):
        ahead_h, ahead_l, back_h, back_l, index = tables[5 * sign : 5 * sign + 5]
        if sign:
            pair = [quarter[0] - quarter[2], quarter[1] - quarter[3]]
        else:
            pair = [quarter[0] + quarter[2], quarter[1] + quarter[3]]
        high, low = split(jnp.concatenate(pair, axis=1))
        spectrum = product(high, low, ahead_h[...], ahead_l[...])
        kept = [
            jnp.where(index[...] <= cut(r), spectrum[r * levels : (r + 1) * levels], 0.0)
            for r in range(rows)
        ]
        high, low = split(jnp.concatenate(kept, axis=0))
        halves.append(product(high, low, back_h[...], back_l[...]))
    even, odd = halves
    for r in range(rows):
        at = slice(r * levels, (r + 1) * levels)
        for q in range(QUARTERS):
            lanes = slice((q % 2) * wide, (q % 2 + 1) * wide)
            e, o = even[at, lanes], odd[at, lanes]
            smooth = e + o if q < 2 else e - o
            emit(r, q, jnp.where(flag(r) > 0, smooth, quarter[q][at]))


def filter_and_edges(field, tables, info, out, edge_z, edge_c):
    rows, groups, sub, wide = field.shape
    tiles = groups // QUARTERS
    cut = lambda r: info[8 + r]
    flag = lambda r: info[8 + rows + r]
    active = flag(0)
    for r in range(1, rows):
        active = active | flag(r)

    @pl.when(active > 0)
    def _():
        def emit(r, q, value):
            out[r, q * tiles : (q + 1) * tiles] = value.reshape(tiles, sub, wide)

        filter_block(field, tables, cut, flag, emit)

    @pl.when(active == 0)
    def _():
        out[...] = field[...]

    write_edges(out, info, edge_z, edge_c)


def write_edges(field, info, edge_z, edge_c):
    shift = field.shape[0] - HALO
    odd = info[4]
    edge_z[...] = field[pl.ds(odd * shift, HALO)]
    edge_c[...] = field[pl.ds((1 - odd) * shift, HALO)]


def place_halo(info, halo, from_z, from_c):
    odd = info[4]
    halo[pl.ds(odd * HALO, HALO)] = from_z[...]
    halo[pl.ds((1 - odd) * HALO, HALO)] = from_c[...]


def flux_terms(courant, jump):
    size = jnp.abs(courant)
    rest = 1.0 - size
    carried = courant * jump
    t = carried * rest
    edge = t * rest
    upwind = -(t * size)
    cell = carried * size * (3.0 - 2.0 * size)
    ahead = courant >= 0.0
    up_plus = jnp.where(ahead, upwind, 0.0)
    cell_plus = jnp.where(ahead, cell, 0.0)
    return edge, up_plus, upwind - up_plus, cell_plus, cell - cell_plus


def meridional_pass(field, halo, north, north_halo, ghosts, out):
    rows, groups, sub, wide = field.shape

    def body(i, _):
        def value(g):
            if g < 0:
                return halo[g + HALO, i]
            return field[g, i] if g < rows else halo[HALO + g - rows, i]

        def courant(g):
            if g < 0:
                return north_halo[g + HALO, i]
            return north[g, i] if g < rows else north_halo[HALO + g - rows, i]

        edge = {}
        cell = {}

        def add(store, at, x, low, high):
            if low <= at <= high:
                store[at] = store[at] + x if at in store else x

        below = value(-HALO)
        for f in range(-HALO, rows + 2):
            above = value(f + 1)
            e, up_plus, up_minus, cell_plus, cell_minus = flux_terms(courant(f), above - below)
            add(edge, f, e, -2, rows)
            add(edge, f - 1, up_plus, -2, rows)
            add(edge, f + 1, up_minus, -2, rows)
            add(cell, f, cell_plus, 0, rows - 1)
            add(cell, f + 1, cell_minus, 0, rows - 1)
            below = above
        for r in range(rows):
            near = edge[r] + edge[r - 1]
            far = edge[r + 1] + edge[r - 2]
            out[r, i] = value(r) + cell[r] + (7.0 / 12.0) * near - (1.0 / 12.0) * far
        ghosts[0, i] = (7.0 / 12.0) * edge[-1] - (1.0 / 12.0) * edge[0]
        ghosts[1, i] = (-1.0 / 12.0) * edge[-1]
        ghosts[2, i] = (7.0 / 12.0) * edge[rows - 1] - (1.0 / 12.0) * edge[rows - 2]
        ghosts[3, i] = (-1.0 / 12.0) * edge[rows - 1]
        return 0

    lax.fori_loop(0, groups, body, 0)


def pole_pass(info, ghosts, out):
    rows, groups, sub, wide = out.shape
    half = groups // 2
    for flag_at, targets in ((5, ((0, 0), (1, 1))), (6, ((2, rows - 1), (3, rows - 2)))):

        @pl.when(info[flag_at] > 0)
        def _():
            for ghost, row in targets:
                out[row, :half] = out[row, :half] + ghosts[ghost, half:]
                out[row, half:] = out[row, half:] + ghosts[ghost, :half]


def widen(values, width):
    wide = values[0].shape[1]
    lane = lax.broadcasted_iota(jnp.int32, values[0].shape, 1)
    result = []
    for q in range(QUARTERS):
        after = pltpu.roll(values[(q + 1) % QUARTERS], width, 1)
        before = pltpu.roll(values[(q - 1) % QUARTERS], wide - width, 1)
        padded = jnp.where(lane < width + HALO, after, before)
        padded = jnp.where((lane >= width + HALO) & (lane < wide - HALO), 0.0, padded)
        result.append(jnp.where(lane < width, values[q], padded))
    return result


def zonal_block(value, courant):
    wide = value.shape[1]
    left = lambda x: pltpu.roll(x, wide - 1, 1)
    right = lambda x: pltpu.roll(x, 1, 1)
    edge, up_plus, up_minus, cell_plus, cell_minus = flux_terms(courant, left(value) - value)
    edge = edge + left(up_plus) + right(up_minus)
    pair = edge + right(edge)
    twelfth = (1.0 / 12.0) * pair
    return value + cell_plus + 8.0 * twelfth - left(twelfth) + right(cell_minus - twelfth)


def zonal_pass(width, field, east, emit):
    rows, groups, sub, wide = field.shape
    tiles = groups // QUARTERS

    def body(i, _):
        r, tile = i // tiles, i % tiles
        values = widen([field[r, q * tiles + tile] for q in range(QUARTERS)], width)
        for q in range(QUARTERS):
            emit(r, q, tile, zonal_block(values[q], east[r, q * tiles + tile]))
        return 0

    lax.fori_loop(0, rows * tiles, body, 0)


def solve_pass(field, g, a, h):
    rows, groups, sub, wide = field.shape
    tiles = groups // QUARTERS

    def body(i, _):
        r, q = i // QUARTERS, i % QUARTERS
        take = lambda ref: [ref[r, q * tiles + tile] for tile in range(tiles)]
        x = column_solve(take(field), take(g), take(a), take(h))
        for tile in range(tiles):
            field[r, q * tiles + tile] = x[tile]
        return 0

    lax.fori_loop(0, rows * QUARTERS, body, 0)


def first_filter_kernel(tiles, info, *refs):
    pieces, tables = refs[:4], refs[4:14]
    out, edge_z, edge_c, field = refs[14:]
    for j in range(QUARTERS):
        field[:, pl.ds(info[j] * tiles, tiles)] = pieces[j][...]
    filter_and_edges(field, tables, info, out, edge_z, edge_c)


def north_kernel(tiles, info, *refs):
    pieces = refs[:4]
    out, edge_z, edge_c = refs[4:]
    rows = out.shape[0]
    for j in range(QUARTERS):
        out[:, pl.ds(info[j] * tiles, tiles)] = pieces[j][...]

    @pl.when(info[6] > 0)
    def _():
        out[rows - 1] = jnp.zeros(out.shape[1:], f32)

    write_edges(out, info, edge_z, edge_c)


def coefficient_kernel(tiles, width, info, *refs):
    pieces = refs[:4]
    east, g_o, a_o, h_o, raw, g_s, a_s, h_s = refs[4:]
    rows, groups, sub, wide = east.shape
    levels = tiles * sub
    per = SUB // rows
    for j in range(QUARTERS):
        q = info[j]
        for r in range(rows):
            raw[r, pl.ds(q * tiles, tiles)] = pieces[j][0, r * tiles : (r + 1) * tiles]

        def store(level, g, a, h):
            at = (level % tiles) * SUB + level // tiles
            for s, value in ((g_s, g), (a_s, a), (h_s, h)):
                put(s, pl.ds(at, rows, stride=levels), value)

        mix_at = lambda l: pieces[j][1, l // per, l % per * rows : l % per * rows + rows, :]
        column_factors(mix_at, levels, (rows, wide), store)
        for s, o in ((g_s, g_o), (a_s, a_o), (h_s, h_o)):
            o[:, pl.ds(q * tiles, tiles)] = get(s, slice(0, rows * levels)).reshape(rows, tiles, sub, wide)

    def body(i, _):
        r, tile = i // tiles, i % tiles
        values = widen([raw[r, q * tiles + tile] for q in range(QUARTERS)], width)
        for q in range(QUARTERS):
            east[r, q * tiles + tile] = values[q]
        return 0

    lax.fori_loop(0, rows * tiles, body, 0)


def middle_kernel(width, info, field, from_z, from_c, north, north_z, north_c, east, g, a, h, *refs):
    tables = refs[:10]
    out, edge_z, edge_c, halo, north_halo, ghosts, work, result = refs[10:]
    tiles = field.shape[1] // QUARTERS
    place_halo(info, halo, from_z, from_c)
    place_halo(info, north_halo, north_z, north_c)
    meridional_pass(field, halo, north, north_halo, ghosts, work)
    pole_pass(info, ghosts, work)

    def emit(r, q, tile, value):
        result[r, q * tiles + tile] = value

    zonal_pass(width, work, east, emit)
    solve_pass(result, g, a, h)
    filter_and_edges(result, tables, info, out, edge_z, edge_c)


def last_kernel(width, info, field, from_z, from_c, north, north_z, north_c, east, *refs):
    outs = refs[:4]
    halo, north_halo, ghosts, work, result = refs[4:]
    tiles = field.shape[1] // QUARTERS
    place_halo(info, halo, from_z, from_c)
    place_halo(info, north_halo, north_z, north_c)
    meridional_pass(field, halo, north, north_halo, ghosts, work)
    pole_pass(info, ghosts, work)

    def emit(r, q, tile, value):
        result[r, q * tiles + tile] = value

    zonal_pass(width, work, east, emit)
    for j in range(QUARTERS):
        outs[j][...] = result[:, pl.ds(info[j] * tiles, tiles)]


def call(kernel, outs, scratch, scalars, *args, cost=(1e6, 1e6)):
    shape = lambda s: jax.ShapeDtypeStruct(s, f32)
    specs = [pl.BlockSpec(memory_space=pltpu.SMEM)] * scalars
    specs += [pl.BlockSpec(memory_space=pltpu.VMEM)] * (len(args) - scalars)
    return pl.pallas_call(
        kernel,
        out_shape=[shape(s) for s in outs],
        in_specs=specs,
        out_specs=[pl.BlockSpec(memory_space=pltpu.VMEM)] * len(outs),
        scratch_shapes=[pltpu.VMEM(s, f32) for s in scratch],
        compiler_params=pltpu.CompilerParams(vmem_limit_bytes=48 * 2**20),
        cost_estimate=pl.CostEstimate(flops=int(cost[0]), bytes_accessed=int(cost[1]), transcendentals=0),
    )(*args)


def lat_exchange(edge_z, edge_c):
    count = lax.axis_size("lat")
    pairs = lambda start: [p for i in range(start, count - 1, 2) for p in ((i, i + 1), (i + 1, i))]
    from_z = lax.ppermute(edge_z, "lat", pairs(1))
    from_c = lax.ppermute(edge_c, "lat", pairs(0))
    return from_z, from_c


def on_device(sensitivity, courant_east, courant_north, mixing, cutoff, polar_flag):
    rows, width, channels = sensitivity.shape
    levels = courant_east.shape[2]
    tracers = channels // levels
    tiles = levels // SUB
    parts = lax.axis_size("lon")
    nlon = width * parts
    quarter = nlon // QUARTERS
    wide = round_up(quarter + 2 * HALO, 128)
    me = lax.axis_index("lon")
    lat = lax.axis_index("lat")
    direct = parts == tracers == QUARTERS
    piece = wide if direct else round_up(width, 128)
    tables = fourier_tables(nlon, wide)

    order = jnp.arange(QUARTERS, dtype=jnp.int32)
    if direct:
        order = order ^ me
    ends = jnp.stack([lat % 2, jnp.where(lat == 0, 1, 0), jnp.where(lat == lax.axis_size("lat") - 1, 1, 0), 0 * lat])
    info = jnp.concatenate([order, ends.astype(jnp.int32), cutoff, polar_flag])

    swap = lambda x, s: lax.ppermute(x, "lon", [(i, i ^ s) for i in range(parts)])

    def quarters_of(blocks):
        whole = jnp.moveaxis(blocks[..., :width], 0, -2)
        whole = whole.reshape(whole.shape[:-2] + (QUARTERS, quarter))
        whole = jnp.pad(whole, [(0, 0)] * (whole.ndim - 1) + [(0, wide - quarter)])
        return [whole[..., q, :] for q in range(QUARTERS)]

    def gather(x):
        if direct:
            return [x] + [swap(x, s) for s in range(1, parts)]
        return quarters_of(lax.all_gather(x, "lon"))

    def to_tracers(ys):
        if direct:
            return [ys[0]] + [swap(ys[s], s) for s in range(1, parts)]
        sent = jnp.stack([ys[d % tracers] for d in range(parts)])
        return quarters_of(lax.all_to_all(sent, "lon", split_axis=0, concat_axis=0, tiled=True))

    def to_longitudes(zs):
        if direct:
            return [zs[0]] + [swap(zs[s], s) for s in range(1, parts)]
        whole = jnp.concatenate([z[..., :quarter] for z in zs], axis=-1)
        blocks = jnp.moveaxis(whole.reshape(whole.shape[:-1] + (parts, width)), -2, 0)
        came = lax.all_to_all(blocks, "lon", split_axis=0, concat_axis=0, tiled=True)
        came = jnp.pad(came, [(0, 0)] * (came.ndim - 1) + [(0, piece - width)])
        return [came[t] for t in range(tracers)]

    north_t = courant_north.transpose(0, 2, 1)
    east_t = courant_east.transpose(0, 2, 1)
    mix_t = mixing.transpose(2, 0, 1)
    block = (rows, tiles, SUB, piece)
    full = (rows, QUARTERS * tiles, SUB, wide)
    edge = (HALO,) + full[1:]
    turned = (piece // 128, rows * levels, 128)

    (north_piece,) = call(partial(pack_levels_kernel, tiles), [block], [turned], 0, north_t)
    north_pieces = gather(north_piece)
    ys = call(
        partial(first_solve_kernel, tiles),
        [block] * tracers,
        [(piece // 128, channels, 128), (levels - 1, rows, piece)] + factor_scratch(rows, levels, piece),
        1,
        info,
        sensitivity,
        mix_t,
    )
    pieces = to_tracers(ys)
    (both,) = call(partial(pack_both_kernel, tiles), [(2, rows * tiles, SUB, piece)], [turned], 0, east_t, mix_t)
    both_pieces = gather(both)
    north, north_z, north_c = call(partial(north_kernel, tiles), [full, edge, edge], [], 1, info, *north_pieces)
    north_z, north_c = lat_exchange(north_z, north_c)
    state, edge_z, edge_c = call(
        partial(first_filter_kernel, tiles), [full, edge, edge], [full], 1, info, *pieces, *tables
    )
    edge_z, edge_c = lat_exchange(edge_z, edge_c)
    east, g, a, h = call(
        partial(coefficient_kernel, tiles, quarter),
        [full] * 4,
        [full] + factor_scratch(rows, levels, wide),
        1,
        info,
        *both_pieces,
    )
    halos = [(2 * HALO,) + full[1:]] * 2 + [(4,) + full[1:]] + [full] * 2
    for substep in range(SUBSTEPS - 1):
        state, edge_z, edge_c = call(
            partial(middle_kernel, quarter),
            [full, edge, edge],
            halos,
            1,
            info, state, edge_z, edge_c, north, north_z, north_c, east, g, a, h, *tables,
        )
        edge_z, edge_c = lat_exchange(edge_z, edge_c)
    quarter_block = (rows, tiles, SUB, wide)
    zs = call(
        partial(last_kernel, quarter),
        [quarter_block] * QUARTERS,
        halos,
        1,
        info, state, edge_z, edge_c, north, north_z, north_c, east,
    )
    pieces = to_longitudes(zs)
    (out,) = call(
        partial(unpack_kernel, tiles), [sensitivity.shape], [(piece // 128, channels, 128)], 1, info, *pieces
    )
    return out


def solution(mesh):
    return jax.shard_map(
        on_device,
        mesh=mesh,
        in_specs=(
            P("lat", "lon", None),
            P("lat", "lon", None),
            P("lat", "lon", None),
            P("lat", "lon", None),
            P("lat"),
            P("lat"),
        ),
        out_specs=P("lat", "lon", None),
        check_vma=False,
    )
```

time: 419 us -> 117 us (0.28)
  matrix products: 125 us -> 0 us
  other arithmetic: 110 us -> 0.01 us
  waiting for transfers between devices: 94.5 us -> 42.4 us
  Pallas kernels: 0 us -> 32.4 us
  blocking collectives: 29.3 us -> 0 us
  local copies, waits for them, and re-layouts: 27.4 us -> 13.6 us
    dot_general x4 -> x0, matrix products: 125 us -> none  [the longest x2 88.5 us: filter_rows(): lax.dot_general(weighted, table, (((1,), (1,)), ((), ())), precision=lax....]
    dot_general x2 -> x0, other arithmetic: 76.2 us -> none  [filter_rows(): jnp.dot(circles, table, precision=lax.Precision.HIGHEST, preferred_elemen...]
    ppermute x10 -> x18, waiting for transfers between devices: 94.5 us -> 42.4 us  [the longest x12 33.6 us: on_device(): lax.ppermute(x, 'lon', [(i, i ^ s) for i in range(parts)])]
    pallas_call x0 -> x9, Pallas kernels: none -> 32.4 us  [call(): pl.pallas_call(kernel, out_shape=[shape(s) for s in outs], in_specs=specs...]
    all_to_all x2 -> x0, blocking collectives: 29.3 us -> none  [filter_rows(): return lax.all_to_all(mixed, 'lon', split_axis=1, concat_axis=0, tiled=True)]
    mul x8 -> x0, other arithmetic: 15.4 us -> none  [spread_flux(): term = jnp.pad(weights[position] * jump, padding)]
    ppermute x10 -> x18, starting transfers between devices: 19.5 us -> 27.7 us  [the longest x12 16.2 us: on_device(): lax.ppermute(x, 'lon', [(i, i ^ s) for i in range(parts)])]
    all_to_all x2 -> x0, starting transfers between devices: 7.59 us -> none  [filter_rows(): lax.all_to_all(rows, 'lon', split_axis=0, concat_axis=1, tiled=True)]
  transfers between devices with their start and end apart: 12 -> 18, of which waited for: 10 -> 6; matrix products, arithmetic and copies ran while one was open for 19% -> 0% of each run, Pallas kernels for 0% -> 6%
where the time goes in v1:
time: 117 us; the launch traced here: 116 us
  waiting for transfers between devices  42.4 us (36%)
  Pallas kernels  32.4 us (28%)
  starting transfers between devices  27.7 us (24%)
  local copies, waits for them, and re-layouts  13.6 us (12%)
    ppermute x12, waiting for transfers between devices, on_device(): lax.ppermute(x, 'lon', [(i, i ^ s) for i in range(parts)])  33.6 us
    pallas_call x9, Pallas kernels, call(): pl.pallas_call(kernel, out_shape=[shape(s) for s in outs], in_specs=specs...  32.4 us
    ppermute x12, starting transfers between devices, on_device(): lax.ppermute(x, 'lon', [(i, i ^ s) for i in range(parts)])  16.2 us
    unnamed x54, local copies, waits for them, and re-layouts  13.5 us
    ppermute x3, waiting for transfers between devices, lat_exchange(): from_z = lax.ppermute(edge_z, 'lat', pairs(1))  8.79 us
    ppermute x3, starting transfers between devices, lat_exchange(): from_z = lax.ppermute(edge_z, 'lat', pairs(1))  5.81 us
    ppermute x3, starting transfers between devices, lat_exchange(): from_c = lax.ppermute(edge_c, 'lat', pairs(0))  5.66 us
  transfers between devices with their start and end apart: 18, of which 6 were waited for; matrix products, arithmetic and copies ran while one was open for 0% of the time, Pallas kernels for 6%

profile of v1, /device:TPU:8, one launch (start us, length us, event | category | flops | bytes accessed | tf_op | source)
XLA Modules:
  0.0 116.3 jit_solution(10676348492269322859)
XLA Ops:
  0.0 0.6 copy-done.25
  0.7 0.0 copy-done.26
  0.7 0.1 concatenate.3.order.info
  0.8 0.9 copy-done.19
  1.7 1.1 copy-done.20
  2.8 1.9 %shard_map.154 = (f32[4,4,8,384]{3,2,1,0:T(8,128)S(1)}, f32[4,4,8,384]{3,2,1,0:T(8,128)S(1)}, f32[4,4,8,384]{3,2,1,0:T(8,128)S(1)}, f32[4,4,8,384]{3,2,1,0:T(8,128)S(1)}) custom-call(s32[16]{0:T(128)S(1)} %concatenate.3.order.info, f32[4,360,128]{2,1,0:T(8,128)S(1)} %copy-done.20, f32[31,4,360]{2,1,0:T(4,128)S(1)} %bitcast.6), custom_call_target="tpu_custom_call" | custom-call | flops 1000000 | bytes 1000000 | tf_op jit(solution)/shard_map/pallas_call | solution.py:491
  4.7 1.6 %collective-permute-start = (f32[4,4,8,384]{3,2,1,0:T(8,128)S(1)}, f32[4,4,8,384]{3,2,1,0:T(8,128)S(1)}, u32[]{:S(2)}, u32[]{:S(2)}) collective-permute-start(f32[4,4,8,384]{3,2,1,0:T(8,128)S(1)} %get-tuple-element.27), channel_id=1, source_target_pairs={{0,8},{8,0},{16,24},{24,16},{1,9},{9,1},{17,25},{25,17},{2,10},{10... | collective-permute-start | bytes 589832 | tf_op jit(solution)/shard_map/ppermute | solution.py:531
  6.3 1.5 %collective-permute-start.1 = (f32[4,4,8,384]{3,2,1,0:T(8,128)S(1)}, f32[4,4,8,384]{3,2,1,0:T(8,128)S(1)}, u32[]{:S(2)}, u32[]{:S(2)}) collective-permute-start(f32[4,4,8,384]{3,2,1,0:T(8,128)S(1)} %get-tuple-element.28), channel_id=1, source_target_pairs={{0,16},{8,24},{16,0},{24,8},{1,17},{9,25},{17,1},{25,9},{2,18},{10... | collective-permute-start | bytes 589832 | tf_op jit(solution)/shard_map/ppermute | solution.py:531
  7.8 0.5 collective-permute-start.2
  8.3 0.9 copy-done.22
  9.2 0.1 shard_map.158.refs_0_
  9.3 2.5 %collective-permute-start.12 = (f32[2,16,8,384]{3,2,1,0:T(8,128)S(1)}, f32[2,16,8,384]{3,2,1,0:T(8,128)S(1)}, u32[]{:S(2)}, u32[]{:S(2)}) collective-permute-start(f32[2,16,8,384]{3,2,1,0:T(8,128)S(1)} %shard_map.158.refs_0_), channel_id=1, source_target_pairs={{0,24},{8,16},{16,8},{24,0},{1,25},{9,17},{17,9},{25,1},{2,26},{10... | collective-permute-start | bytes 1179656 | tf_op jit(solution)/shard_map/ppermute | solution.py:531
  11.8 0.0 copy-start.23
  11.8 0.5 collective-permute-start.7
  12.4 0.2 collective-permute-done.refs_1_
  12.6 1.5 %collective-permute-start.6 = (f32[4,4,8,384]{3,2,1,0:T(8,128)S(1)}, f32[4,4,8,384]{3,2,1,0:T(8,128)S(1)}, u32[]{:S(2)}, u32[]{:S(2)}) collective-permute-start(f32[4,4,8,384]{3,2,1,0:T(8,128)S(1)} %shard_map.156.refs_0_), channel_id=1, source_target_pairs={{0,16},{8,24},{16,0},{24,8},{1,17},{9,25},{17,1},{25,9},{2,18},{10... | collective-permute-start | bytes 589832 | tf_op jit(solution)/shard_map/ppermute | solution.py:531
  14.1 15.5 %collective-permute-done.1.refs_2_ = f32[4,4,8,384]{3,2,1,0:T(8,128)S(1)} collective-permute-done((f32[4,4,8,384]{3,2,1,0:T(8,128)S(1)}, f32[4,4,8,384]{3,2,1,0:T(8,128)S(1)}, u32[]{:S(2)}, u32[]{:S(2)}) %collective-permute-start.1) | collective-permute-done | bytes 196640 | tf_op jit(solution)/shard_map/ppermute | solution.py:531
  29.6 0.0 collective-permute-start.5
  29.6 0.0 collective-permute-done.2.refs_3_
  29.6 2.5 %collective-permute-start.11 = (f32[2,16,8,384]{3,2,1,0:T(8,128)S(1)}, f32[2,16,8,384]{3,2,1,0:T(8,128)S(1)}, u32[]{:S(2)}, u32[]{:S(2)}) collective-permute-start(f32[2,16,8,384]{3,2,1,0:T(8,128)S(1)} %shard_map.158.refs_0_), channel_id=1, source_target_pairs={{0,16},{8,24},{16,0},{24,8},{1,17},{9,25},{17,1},{25,9},{2,18},{10... | collective-permute-start | bytes 1179656 | tf_op jit(solution)/shard_map/ppermute | solution.py:531
  32.1 0.0 copy-start.7
  32.1 1.1 copy-done.7
  33.2 1.1 copy-done.9
  34.3 1.1 copy-done.11
  35.3 1.1 copy-done.13
  36.4 2.1 %shard_map.155 = (f32[4,16,8,384]{3,2,1,0:T(8,128)}, f32[3,16,8,384]{3,2,1,0:T(8,128)S(1)}, f32[3,16,8,384]{3,2,1,0:T(8,128)S(1)}) custom-call(s32[16]{0:T(128)S(1)} %concatenate.3.order.info, f32[4,4,8,384]{3,2,1,0:T(8,128)S(1)} %get-tuple-element.26.refs_0_, f32[4,4,8,384]{3,2,1,0:T(8,128)S(1)} %collective-permute-done.refs_1_, ...), custom_call_target="tpu_custom_call" | custom-call | flops 1000000 | bytes 1000000 | tf_op jit(solution)/shard_map/pallas_call | solution.py:491
  38.5 0.0 collective-permute-done.7.refs_3_
  38.5 1.9 %collective-permute-start.3 = (f32[3,16,8,384]{3,2,1,0:T(8,128)S(1)}, f32[3,16,8,384]{3,2,1,0:T(8,128)S(1)}, u32[]{:S(2)}, u32[]{:S(2)}) collective-permute-start(f32[3,16,8,384]{3,2,1,0:T(8,128)S(1)} %get-tuple-element.31), channel_id=1, source_target_pairs={{1,2},{2,1},{3,4},{4,3},{5,6},{6,5},{9,10},{10,9},{11,12},{12,11},... | collective-permute-start | bytes 1769480 | tf_op jit(solution)/shard_map/ppermute | solution.py:505
  40.4 0.0 collective-permute-done.6.refs_2_
  40.4 1.7 %collective-permute-start.4 = (f32[3,16,8,384]{3,2,1,0:T(8,128)S(1)}, f32[3,16,8,384]{3,2,1,0:T(8,128)S(1)}, u32[]{:S(2)}, u32[]{:S(2)}) collective-permute-start(f32[3,16,8,384]{3,2,1,0:T(8,128)S(1)} %get-tuple-element.32), channel_id=1, source_target_pairs={{0,1},{1,0},{2,3},{3,2},{4,5},{5,4},{6,7},{7,6},{8,9},{9,8},{10,11... | collective-permute-start | bytes 1769480 | tf_op jit(solution)/shard_map/ppermute | solution.py:506
  42.1 0.0 collective-permute-done.5.refs_1_
  42.2 0.7 shard_map.157
  42.8 0.9 copy-done
  43.7 2.0 %collective-permute-start.8 = (f32[3,16,8,384]{3,2,1,0:T(8,128)S(1)}, f32[3,16,8,384]{3,2,1,0:T(8,128)S(1)}, u32[]{:S(2)}, u32[]{:S(2)}) collective-permute-start(f32[3,16,8,384]{3,2,1,0:T(8,128)S(1)} %get-tuple-element.34), channel_id=1, source_target_pairs={{1,2},{2,1},{3,4},{4,3},{5,6},{6,5},{9,10},{10,9},{11,12},{12,11},... | collective-permute-start | bytes 1769480 | tf_op jit(solution)/shard_map/ppermute | solution.py:505
  45.7 0.0 collective-permute-done.12.refs_3_
  45.8 0.0 copy-start.8
  45.8 0.0 copy-start.10
  45.8 3.4 %collective-permute-start.9 = (f32[3,16,8,384]{3,2,1,0:T(8,128)S(1)}, f32[3,16,8,384]{3,2,1,0:T(8,128)S(1)}, u32[]{:S(2)}, u32[]{:S(2)}) collective-permute-start(f32[3,16,8,384]{3,2,1,0:T(8,128)S(1)} %get-tuple-element.35), channel_id=1, source_target_pairs={{0,1},{1,0},{2,3},{3,2},{4,5},{5,4},{6,7},{7,6},{8,9},{9,8},{10,11... | collective-permute-start | bytes 1769480 | tf_op jit(solution)/shard_map/ppermute | solution.py:506
  49.2 0.0 collective-permute-done.11.refs_2_
  49.2 2.0 %collective-permute-start.10 = (f32[2,16,8,384]{3,2,1,0:T(8,128)S(1)}, f32[2,16,8,384]{3,2,1,0:T(8,128)S(1)}, u32[]{:S(2)}, u32[]{:S(2)}) collective-permute-start(f32[2,16,8,384]{3,2,1,0:T(8,128)S(1)} %shard_map.158.refs_0_), channel_id=1, source_target_pairs={{0,8},{8,0},{16,24},{24,16},{1,9},{9,1},{17,25},{25,17},{2,10},{10... | collective-permute-start | bytes 1179656 | tf_op jit(solution)/shard_map/ppermute | solution.py:531
  51.2 9.4 %collective-permute-done.10.refs_1_ = f32[2,16,8,384]{3,2,1,0:T(8,128)S(1)} collective-permute-done((f32[2,16,8,384]{3,2,1,0:T(8,128)S(1)}, f32[2,16,8,384]{3,2,1,0:T(8,128)S(1)}, u32[]{:S(2)}, u32[]{:S(2)}) %collective-permute-start.10) | collective-permute-done | bytes 393248 | tf_op jit(solution)/shard_map/ppermute | solution.py:531
  60.6 4.3 %shard_map.159 = (f32[4,16,8,384]{3,2,1,0:T(8,128)S(1)}, f32[4,16,8,384]{3,2,1,0:T(8,128)S(1)}, f32[4,16,8,384]{3,2,1,0:T(8,128)S(1)}, f32[4,16,8,384]{3,2,1,0:T(8,128)S(1)}) custom-call(s32[16]{0:T(128)S(1)} %concatenate.3.order.info, f32[2,16,8,384]{3,2,1,0:T(8,128)S(1)} %shard_map.158.refs_0_, f32[2,16,8,384]{3,2,1,0:T(8,128)S(1)} %collective-permute-done.10.refs_1_, ...), custom_call_target="tpu_custom_call" | custom-call | flops 1000000 | bytes 1000000 | tf_op jit(solution)/shard_map/pallas_call | solution.py:491
  64.9 0.9 copy-done.2
  65.8 0.9 copy-done.16
  66.6 0.9 copy-done.17
  67.5 0.9 copy-done.18
  68.5 0.0 collective-permute-done.3.from_z
  68.5 0.0 collective-permute-done.4.from_c
  68.5 0.0 collective-permute-done.8.north_z
  68.5 0.0 collective-permute-done.9.north_c
  68.5 12.9 %shard_map.160 = (f32[4,16,8,384]{3,2,1,0:T(8,128)}, f32[3,16,8,384]{3,2,1,0:T(8,128)S(1)}, f32[3,16,8,384]{3,2,1,0:T(8,128)S(1)}) custom-call(s32[16]{0:T(128)S(1)} %concatenate.3.order.info, f32[4,16,8,384]{3,2,1,0:T(8,128)} %get-tuple-element.30.field, f32[3,16,8,384]{3,2,1,0:T(8,128)S(1)} %collective-permute-done.3.from_z, ...), custom_call_target="tpu_custom_call" | custom-call | flops 1000000 | bytes 1000000 | tf_op jit(solution)/shard_map/pallas_call | solution.py:491
  81.4 1.9 %collective-permute-start.13 = (f32[3,16,8,384]{3,2,1,0:T(8,128)S(1)}, f32[3,16,8,384]{3,2,1,0:T(8,128)S(1)}, u32[]{:S(2)}, u32[]{:S(2)}) collective-permute-start(f32[3,16,8,384]{3,2,1,0:T(8,128)S(1)} %get-tuple-element.41), channel_id=1, source_target_pairs={{1,2},{2,1},{3,4},{4,3},{5,6},{6,5},{9,10},{10,9},{11,12},{12,11},... | collective-permute-start | bytes 1769480 | tf_op jit(solution)/shard_map/ppermute | solution.py:505
  83.3 0.5 collective-permute-start.14
  83.8 8.8 %collective-permute-done.13.from_z = f32[3,16,8,384]{3,2,1,0:T(8,128)S(1)} collective-permute-done((f32[3,16,8,384]{3,2,1,0:T(8,128)S(1)}, f32[3,16,8,384]{3,2,1,0:T(8,128)S(1)}, u32[]{:S(2)}, u32[]{:S(2)}) %collective-permute-start.13) | collective-permute-done | bytes 589856 | tf_op jit(solution)/shard_map/ppermute | solution.py:505
  92.6 0.0 collective-permute-done.14.from_c
  92.6 1.1 copy-done.15
  93.7 8.6 %shard_map.161 = (f32[4,4,8,384]{3,2,1,0:T(8,128)S(1)}, f32[4,4,8,384]{3,2,1,0:T(8,128)S(1)}, f32[4,4,8,384]{3,2,1,0:T(8,128)S(1)}, f32[4,4,8,384]{3,2,1,0:T(8,128)S(1)}) custom-call(s32[16]{0:T(128)S(1)} %concatenate.3.order.info, f32[4,16,8,384]{3,2,1,0:T(8,128)S(1)} %copy-done.15, f32[3,16,8,384]{3,2,1,0:T(8,128)S(1)} %collective-permute-done.13.from_z, ...), custom_call_target="tpu_custom_call" | custom-call | flops 1000000 | bytes 1000000 | tf_op jit(solution)/shard_map/pallas_call | solution.py:491
  102.3 1.8 %collective-permute-start.15 = (f32[4,4,8,384]{3,2,1,0:T(8,128)S(1)}, f32[4,4,8,384]{3,2,1,0:T(8,128)S(1)}, u32[]{:S(2)}, u32[]{:S(2)}) collective-permute-start(f32[4,4,8,384]{3,2,1,0:T(8,128)S(1)} %get-tuple-element.44), channel_id=1, source_target_pairs={{0,8},{8,0},{16,24},{24,16},{1,9},{9,1},{17,25},{25,17},{2,10},{10... | collective-permute-start | bytes 589832 | tf_op jit(solution)/shard_map/ppermute | solution.py:531
  104.1 0.0 collective-permute-start.16
  104.2 1.7 %collective-permute-start.17 = (f32[4,4,8,384]{3,2,1,0:T(8,128)S(1)}, f32[4,4,8,384]{3,2,1,0:T(8,128)S(1)}, u32[]{:S(2)}, u32[]{:S(2)}) collective-permute-start(f32[4,4,8,384]{3,2,1,0:T(8,128)S(1)} %get-tuple-element.46), channel_id=1, source_target_pairs={{0,24},{8,16},{16,8},{24,0},{1,25},{9,17},{17,9},{25,1},{2,26},{10... | collective-permute-start | bytes 589832 | tf_op jit(solution)/shard_map/ppermute | solution.py:531
  105.9 4.3 %collective-permute-done.15.refs_1_ = f32[4,4,8,384]{3,2,1,0:T(8,128)S(1)} collective-permute-done((f32[4,4,8,384]{3,2,1,0:T(8,128)S(1)}, f32[4,4,8,384]{3,2,1,0:T(8,128)S(1)}, u32[]{:S(2)}, u32[]{:S(2)}) %collective-permute-start.15) | collective-permute-done | bytes 196640 | tf_op jit(solution)/shard_map/ppermute | solution.py:531
  110.2 4.2 %collective-permute-done.16.refs_2_ = f32[4,4,8,384]{3,2,1,0:T(8,128)S(1)} collective-permute-done((f32[4,4,8,384]{3,2,1,0:T(8,128)S(1)}, f32[4,4,8,384]{3,2,1,0:T(8,128)S(1)}, u32[]{:S(2)}, u32[]{:S(2)}) %collective-permute-start.16) | collective-permute-done | bytes 196640 | tf_op jit(solution)/shard_map/ppermute | solution.py:531
  114.4 0.0 collective-permute-done.17.refs_3_
  114.4 1.9 %shard_map.162 = f32[4,360,128]{2,1,0:T(8,128)} custom-call(s32[16]{0:T(128)S(1)} %concatenate.3.order.info, f32[4,4,8,384]{3,2,1,0:T(8,128)S(1)} %get-tuple-element.43.refs_0_, f32[4,4,8,384]{3,2,1,0:T(8,128)S(1)} %collective-permute-done.15.refs_1_, f32[4,4,8,384]{3,2,1,0:T(8,128)S(1)} %collective-permute-done.16.refs_2_, ...), custom_call_target="tpu_custom_call" | custom-call | flops 1000000 | bytes 1000000 | tf_op jit(solution)/shard_map/pallas_call | solution.py:491
  (37 shorter events, 0.1 us)
Async XLA Ops:
  0.0 0.7 copy-start.25
  0.0 0.7 copy-start.26
  0.8 0.9 copy-start.19
  1.7 1.1 copy-start.20
  2.8 9.0 %copy-start.21 = (f32[4,360,32]{1,2,0:T(8,128)S(1)}, f32[4,360,32]{1,2,0:T(8,128)}, u32[]{:S(2)}) copy-start(f32[4,360,32]{1,2,0:T(8,128)} %param.18) | copy-start | bytes 552964
  2.8 29.3 %copy-start.6 = (bf16[768,384]{1,0:T(8,128)(2,1)S(1)}, bf16[768,384]{1,0:T(8,128)(2,1)}, u32[]{:S(2)}) copy-start(bf16[768,384]{1,0:T(8,128)(2,1)} %constant.52.clone.refs_9_.refs_5_) | copy-start | bytes 1769476
  2.8 29.3 %copy-start.24 = (s32[1,384]{1,0:T(1,128)S(1)}, s32[1,384]{1,0:T(1,128)}, u32[]{:S(2)}) copy-start(s32[1,384]{1,0:T(1,128)} %constant.51.clone.refs_8_.refs_4_) | copy-start | bytes 4612
  4.7 7.9 %collective-permute-start = (f32[4,4,8,384]{3,2,1,0:T(8,128)S(1)}, f32[4,4,8,384]{3,2,1,0:T(8,128)S(1)}, u32[]{:S(2)}, u32[]{:S(2)}) collective-permute-start(f32[4,4,8,384]{3,2,1,0:T(8,128)S(1)} %get-tuple-element.27), channel_id=1, source_target_pairs={{0,8},{8,0},{16,24},{24,16},{1,9},{9,1},{17,25},{25,17},{2,10},{10... | collective-permute-start | bytes 589832 | tf_op jit(solution)/shard_map/ppermute | solution.py:531
  6.3 23.4 %collective-permute-start.1 = (f32[4,4,8,384]{3,2,1,0:T(8,128)S(1)}, f32[4,4,8,384]{3,2,1,0:T(8,128)S(1)}, u32[]{:S(2)}, u32[]{:S(2)}) collective-permute-start(f32[4,4,8,384]{3,2,1,0:T(8,128)S(1)} %get-tuple-element.28), channel_id=1, source_target_pairs={{0,16},{8,24},{16,0},{24,8},{1,17},{9,25},{17,1},{25,9},{2,18},{10... | collective-permute-start | bytes 589832 | tf_op jit(solution)/shard_map/ppermute | solution.py:531
  7.8 24.3 %copy-start.5 = (bf16[768,384]{1,0:T(8,128)(2,1)S(1)}, bf16[768,384]{1,0:T(8,128)(2,1)}, u32[]{:S(2)}) copy-start(bf16[768,384]{1,0:T(8,128)(2,1)} %constant.53.clone.refs_10_.refs_6_) | copy-start | bytes 1769476
  7.8 24.3 %copy-start.4 = (bf16[384,768]{1,0:T(8,128)(2,1)S(1)}, bf16[384,768]{1,0:T(8,128)(2,1)}, u32[]{:S(2)}) copy-start(bf16[384,768]{1,0:T(8,128)(2,1)} %constant.54.clone.refs_11_.refs_7_) | copy-start | bytes 1769476
  7.8 21.8 %collective-permute-start.2 = (f32[4,4,8,384]{3,2,1,0:T(8,128)S(1)}, f32[4,4,8,384]{3,2,1,0:T(8,128)S(1)}, u32[]{:S(2)}, u32[]{:S(2)}) collective-permute-start(f32[4,4,8,384]{3,2,1,0:T(8,128)S(1)} %get-tuple-element.29), channel_id=1, source_target_pairs={{0,24},{8,16},{16,8},{24,0},{1,25},{9,17},{17,9},{25,1},{2,26},{10... | collective-permute-start | bytes 589832 | tf_op jit(solution)/shard_map/ppermute | solution.py:531
  8.3 0.9 copy-start.22
  9.3 36.5 %collective-permute-start.12 = (f32[2,16,8,384]{3,2,1,0:T(8,128)S(1)}, f32[2,16,8,384]{3,2,1,0:T(8,128)S(1)}, u32[]{:S(2)}, u32[]{:S(2)}) collective-permute-start(f32[2,16,8,384]{3,2,1,0:T(8,128)S(1)} %shard_map.158.refs_0_), channel_id=1, source_target_pairs={{0,24},{8,16},{16,8},{24,0},{1,25},{9,17},{17,9},{25,1},{2,26},{10... | collective-permute-start | bytes 1179656 | tf_op jit(solution)/shard_map/ppermute | solution.py:531
  11.8 20.3 %copy-start.23 = (s32[1,384]{1,0:T(1,128)S(1)}, s32[1,384]{1,0:T(1,128)}, u32[]{:S(2)}) copy-start(s32[1,384]{1,0:T(1,128)} %constant.56.clone.refs_13_.refs_9_) | copy-start | bytes 4612
  11.8 26.6 %collective-permute-start.7 = (f32[4,4,8,384]{3,2,1,0:T(8,128)S(1)}, f32[4,4,8,384]{3,2,1,0:T(8,128)S(1)}, u32[]{:S(2)}, u32[]{:S(2)}) collective-permute-start(f32[4,4,8,384]{3,2,1,0:T(8,128)S(1)} %shard_map.156.refs_0_), channel_id=1, source_target_pairs={{0,24},{8,16},{16,8},{24,0},{1,25},{9,17},{17,9},{25,1},{2,26},{10... | collective-permute-start | bytes 589832 | tf_op jit(solution)/shard_map/ppermute | solution.py:531
  12.6 27.8 %collective-permute-start.6 = (f32[4,4,8,384]{3,2,1,0:T(8,128)S(1)}, f32[4,4,8,384]{3,2,1,0:T(8,128)S(1)}, u32[]{:S(2)}, u32[]{:S(2)}) collective-permute-start(f32[4,4,8,384]{3,2,1,0:T(8,128)S(1)} %shard_map.156.refs_0_), channel_id=1, source_target_pairs={{0,16},{8,24},{16,0},{24,8},{1,17},{9,25},{17,1},{25,9},{2,18},{10... | collective-permute-start | bytes 589832 | tf_op jit(solution)/shard_map/ppermute | solution.py:531
  29.6 12.5 %collective-permute-start.5 = (f32[4,4,8,384]{3,2,1,0:T(8,128)S(1)}, f32[4,4,8,384]{3,2,1,0:T(8,128)S(1)}, u32[]{:S(2)}, u32[]{:S(2)}) collective-permute-start(f32[4,4,8,384]{3,2,1,0:T(8,128)S(1)} %shard_map.156.refs_0_), channel_id=1, source_target_pairs={{0,8},{8,0},{16,24},{24,16},{1,9},{9,1},{17,25},{25,17},{2,10},{10... | collective-permute-start | bytes 589832 | tf_op jit(solution)/shard_map/ppermute | solution.py:531
  29.6 19.6 %collective-permute-start.11 = (f32[2,16,8,384]{3,2,1,0:T(8,128)S(1)}, f32[2,16,8,384]{3,2,1,0:T(8,128)S(1)}, u32[]{:S(2)}, u32[]{:S(2)}) collective-permute-start(f32[2,16,8,384]{3,2,1,0:T(8,128)S(1)} %shard_map.158.refs_0_), channel_id=1, source_target_pairs={{0,16},{8,24},{16,0},{24,8},{1,17},{9,25},{17,1},{25,9},{2,18},{10... | collective-permute-start | bytes 1179656 | tf_op jit(solution)/shard_map/ppermute | solution.py:531
  32.1 1.1 copy-start.7
  33.2 1.1 copy-start.9
  34.3 1.1 copy-start.11
  35.3 1.1 copy-start.13
  38.5 30.0 %collective-permute-start.3 = (f32[3,16,8,384]{3,2,1,0:T(8,128)S(1)}, f32[3,16,8,384]{3,2,1,0:T(8,128)S(1)}, u32[]{:S(2)}, u32[]{:S(2)}) collective-permute-start(f32[3,16,8,384]{3,2,1,0:T(8,128)S(1)} %get-tuple-element.31), channel_id=1, source_target_pairs={{1,2},{2,1},{3,4},{4,3},{5,6},{6,5},{9,10},{10,9},{11,12},{12,11},... | collective-permute-start | bytes 1769480 | tf_op jit(solution)/shard_map/ppermute | solution.py:505
  40.4 28.1 %collective-permute-start.4 = (f32[3,16,8,384]{3,2,1,0:T(8,128)S(1)}, f32[3,16,8,384]{3,2,1,0:T(8,128)S(1)}, u32[]{:S(2)}, u32[]{:S(2)}) collective-permute-start(f32[3,16,8,384]{3,2,1,0:T(8,128)S(1)} %get-tuple-element.32), channel_id=1, source_target_pairs={{0,1},{1,0},{2,3},{3,2},{4,5},{5,4},{6,7},{7,6},{8,9},{9,8},{10,11... | collective-permute-start | bytes 1769480 | tf_op jit(solution)/shard_map/ppermute | solution.py:506
  42.2 26.3 %copy-start.12 = (bf16[768,384]{1,0:T(8,128)(2,1)S(1)}, bf16[768,384]{1,0:T(8,128)(2,1)}, u32[]{:S(2)}) copy-start(bf16[768,384]{1,0:T(8,128)(2,1)} %constant.48.clone.refs_5_.refs_1_) | copy-start | bytes 1769476
  42.2 26.3 %copy-start.14 = (bf16[768,384]{1,0:T(8,128)(2,1)S(1)}, bf16[768,384]{1,0:T(8,128)(2,1)}, u32[]{:S(2)}) copy-start(bf16[768,384]{1,0:T(8,128)(2,1)} %constant.47.clone.refs_4_.refs_0_) | copy-start | bytes 1769476
  42.8 0.9 copy-start
  43.7 24.7 %collective-permute-start.8 = (f32[3,16,8,384]{3,2,1,0:T(8,128)S(1)}, f32[3,16,8,384]{3,2,1,0:T(8,128)S(1)}, u32[]{:S(2)}, u32[]{:S(2)}) collective-permute-start(f32[3,16,8,384]{3,2,1,0:T(8,128)S(1)} %get-tuple-element.34), channel_id=1, source_target_pairs={{1,2},{2,1},{3,4},{4,3},{5,6},{6,5},{9,10},{10,9},{11,12},{12,11},... | collective-permute-start | bytes 1769480 | tf_op jit(solution)/shard_map/ppermute | solution.py:505
  45.8 22.7 %copy-start.8 = (bf16[384,768]{1,0:T(8,128)(2,1)S(1)}, bf16[384,768]{1,0:T(8,128)(2,1)}, u32[]{:S(2)}) copy-start(bf16[384,768]{1,0:T(8,128)(2,1)} %constant.50.clone.refs_7_.refs_3_) | copy-start | bytes 1769476
  45.8 22.7 %copy-start.10 = (bf16[384,768]{1,0:T(8,128)(2,1)S(1)}, bf16[384,768]{1,0:T(8,128)(2,1)}, u32[]{:S(2)}) copy-start(bf16[384,768]{1,0:T(8,128)(2,1)} %constant.49.clone.refs_6_.refs_2_) | copy-start | bytes 1769476
  45.8 22.7 %collective-permute-start.9 = (f32[3,16,8,384]{3,2,1,0:T(8,128)S(1)}, f32[3,16,8,384]{3,2,1,0:T(8,128)S(1)}, u32[]{:S(2)}, u32[]{:S(2)}) collective-permute-start(f32[3,16,8,384]{3,2,1,0:T(8,128)S(1)} %get-tuple-element.35), channel_id=1, source_target_pairs={{0,1},{1,0},{2,3},{3,2},{4,5},{5,4},{6,7},{7,6},{8,9},{9,8},{10,11... | collective-permute-start | bytes 1769480 | tf_op jit(solution)/shard_map/ppermute | solution.py:506
  49.2 11.4 %collective-permute-start.10 = (f32[2,16,8,384]{3,2,1,0:T(8,128)S(1)}, f32[2,16,8,384]{3,2,1,0:T(8,128)S(1)}, u32[]{:S(2)}, u32[]{:S(2)}) collective-permute-start(f32[2,16,8,384]{3,2,1,0:T(8,128)S(1)} %shard_map.158.refs_0_), channel_id=1, source_target_pairs={{0,8},{8,0},{16,24},{24,16},{1,9},{9,1},{17,25},{25,17},{2,10},{10... | collective-permute-start | bytes 1179656 | tf_op jit(solution)/shard_map/ppermute | solution.py:531
  64.9 0.9 copy-start.2
  65.8 0.9 copy-start.16
  66.6 0.9 copy-start.17
  67.5 0.9 copy-start.18
  68.5 24.1 %copy-start.1 = (f32[4,16,8,384]{3,2,1,0:T(8,128)S(1)}, f32[4,16,8,384]{3,2,1,0:T(8,128)}, u32[]{:S(2)}) copy-start(f32[4,16,8,384]{3,2,1,0:T(8,128)} %copy-done) | copy-start | bytes 2359300
  68.5 24.1 %copy-start.3 = (f32[4,16,8,384]{3,2,1,0:T(8,128)S(1)}, f32[4,16,8,384]{3,2,1,0:T(8,128)}, u32[]{:S(2)}) copy-start(f32[4,16,8,384]{3,2,1,0:T(8,128)} %copy-done.2) | copy-start | bytes 2359300
  81.4 11.2 %collective-permute-start.13 = (f32[3,16,8,384]{3,2,1,0:T(8,128)S(1)}, f32[3,16,8,384]{3,2,1,0:T(8,128)S(1)}, u32[]{:S(2)}, u32[]{:S(2)}) collective-permute-start(f32[3,16,8,384]{3,2,1,0:T(8,128)S(1)} %get-tuple-element.41), channel_id=1, source_target_pairs={{1,2},{2,1},{3,4},{4,3},{5,6},{6,5},{9,10},{10,9},{11,12},{12,11},... | collective-permute-start | bytes 1769480 | tf_op jit(solution)/shard_map/ppermute | solution.py:505
  83.3 9.3 %collective-permute-start.14 = (f32[3,16,8,384]{3,2,1,0:T(8,128)S(1)}, f32[3,16,8,384]{3,2,1,0:T(8,128)S(1)}, u32[]{:S(2)}, u32[]{:S(2)}) collective-permute-start(f32[3,16,8,384]{3,2,1,0:T(8,128)S(1)} %get-tuple-element.42), channel_id=1, source_target_pairs={{0,1},{1,0},{2,3},{3,2},{4,5},{5,4},{6,7},{7,6},{8,9},{9,8},{10,11... | collective-permute-start | bytes 1769480 | tf_op jit(solution)/shard_map/ppermute | solution.py:506
  92.6 1.1 copy-start.15
  102.3 7.9 %collective-permute-start.15 = (f32[4,4,8,384]{3,2,1,0:T(8,128)S(1)}, f32[4,4,8,384]{3,2,1,0:T(8,128)S(1)}, u32[]{:S(2)}, u32[]{:S(2)}) collective-permute-start(f32[4,4,8,384]{3,2,1,0:T(8,128)S(1)} %get-tuple-element.44), channel_id=1, source_target_pairs={{0,8},{8,0},{16,24},{24,16},{1,9},{9,1},{17,25},{25,17},{2,10},{10... | collective-permute-start | bytes 589832 | tf_op jit(solution)/shard_map/ppermute | solution.py:531
  104.1 10.3 %collective-permute-start.16 = (f32[4,4,8,384]{3,2,1,0:T(8,128)S(1)}, f32[4,4,8,384]{3,2,1,0:T(8,128)S(1)}, u32[]{:S(2)}, u32[]{:S(2)}) collective-permute-start(f32[4,4,8,384]{3,2,1,0:T(8,128)S(1)} %get-tuple-element.45), channel_id=1, source_target_pairs={{0,16},{8,24},{16,0},{24,8},{1,17},{9,25},{17,1},{25,9},{2,18},{10... | collective-permute-start | bytes 589832 | tf_op jit(solution)/shard_map/ppermute | solution.py:531
  104.2 10.3 %collective-permute-start.17 = (f32[4,4,8,384]{3,2,1,0:T(8,128)S(1)}, f32[4,4,8,384]{3,2,1,0:T(8,128)S(1)}, u32[]{:S(2)}, u32[]{:S(2)}) collective-permute-start(f32[4,4,8,384]{3,2,1,0:T(8,128)S(1)} %get-tuple-element.46), channel_id=1, source_target_pairs={{0,24},{8,16},{16,8},{24,0},{1,25},{9,17},{17,9},{25,1},{2,26},{10... | collective-permute-start | bytes 589832 | tf_op jit(solution)/shard_map/ppermute | solution.py:531

commit v2 on v1

v2 whole, which is shorter than its diff:
```python
from functools import partial
import math

import jax
import jax.numpy as jnp
import ml_dtypes
import numpy as np
from jax import lax
from jax.experimental import pallas as pl
from jax.experimental.pallas import tpu as pltpu
from jax.sharding import PartitionSpec as P

SUBSTEPS = 2
QUARTERS = 4
HALO = 3
MIDDLE_ROOM = 24
SUB = 8
f32 = jnp.float32
bf16 = jnp.bfloat16


def round_up(n, k):
    return -(-n // k) * k


def fourier_tables(nlon, wide):
    quarter = nlon // 4
    x = np.arange(2 * quarter)
    place = (x // quarter) * wide + x % quarter
    table = np.zeros((2, 2 * wide, round_up(quarter, 128)))
    for odd in (0, 1):
        k = np.arange(odd, quarter, 2)
        n = len(k)
        angle = (x[:, None] * k[None, :] % nlon) * (2.0 * math.pi / nlon)
        table[odd, place, :n] = np.cos(angle)
        table[odd, place, n : 2 * n] = np.sin(angle)
    high = table.astype(np.float32).astype(ml_dtypes.bfloat16)
    low = (table - high.astype(np.float64)).astype(np.float32).astype(ml_dtypes.bfloat16)
    return [high, low]


def wave_index(odd, count, shape):
    n = (count - odd + 1) // 2
    column = lax.broadcasted_iota(jnp.int32, shape, 1)
    wave = 2 * jnp.where(column < n, column, column - n) + odd
    return jnp.where(column < 2 * n, wave, 4 * count)


def split(x):
    high = x.astype(bf16)
    return high, (x - high.astype(f32)).astype(bf16)


def product(high, low, t_high, t_low, side):
    dot = lambda x, t: lax.dot_general(x, t, (((1,), (side,)), ((), ())), preferred_element_type=f32)
    return dot(high, t_high) + dot(low, t_high) + dot(high, t_low)


def column_factors(mix_at, levels, shape, store):
    zero = jnp.zeros(shape, f32)
    h_before = zero
    below = zero
    for level in range(levels):
        above = mix_at(level) if level < levels - 1 else zero
        divisor = 1.0 + below + above - below * h_before
        g = 1.0 / divisor
        h = above * g
        store(level, g, below * g, h)
        h_before = h
        below = above


def column_solve(v, g, a, h):
    n = len(v)
    y = [g[0] * v[0]]
    carry = [a[0]]
    for q in range(1, n):
        y.append(g[q] * v[q] + a[q] * y[q - 1])
        carry.append(a[q] * carry[q - 1])
    z, p = y[n - 1], carry[n - 1]
    step = 1
    while step < SUB:
        z = z + p * pltpu.roll(z, step, 0)
        if 2 * step < SUB:
            p = p * pltpu.roll(p, step, 0)
        step *= 2
    before = pltpu.roll(z, 1, 0)
    y = [y[q] + carry[q] * before for q in range(n - 1)] + [z]
    x = [None] * n
    back = [None] * n
    x[n - 1] = y[n - 1]
    back[n - 1] = h[n - 1]
    for q in range(n - 2, -1, -1):
        x[q] = y[q] + h[q] * x[q + 1]
        back[q] = h[q] * back[q + 1]
    z, p = x[0], back[0]
    step = 1
    while step < SUB:
        z = z + p * pltpu.roll(z, SUB - step, 0)
        if 2 * step < SUB:
            p = p * pltpu.roll(p, SUB - step, 0)
        step *= 2
    after = pltpu.roll(z, SUB - 1, 0)
    return [z] + [x[q] + back[q] * after for q in range(1, n)]


def put(ref, at, value):
    for c in range(ref.shape[0]):
        n = min(128, value.shape[1] - c * 128)
        ref[c, at, :n] = value[:, c * 128 : c * 128 + n]


def get(ref, at):
    return jnp.concatenate([ref[c, at, :] for c in range(ref.shape[0])], axis=1)


def order_of(j, direct):
    return lax.axis_index("lon") ^ j if direct else j


def at_odd():
    return lax.axis_index("lat") % 2


def at_end(end):
    return lax.axis_index("lat") == (lax.axis_size("lat") - 1 if end else 0)


def clear(*refs):
    for ref in refs:
        ref[...] = jnp.zeros(ref.shape, f32)


def factor_scratch(rows, levels, wide):
    return [(wide // 128, rows * levels, 128)] * 3


def first_solve_kernel(tiles, direct, tracers, *refs):
    sens, mix = refs[-(9 + tracers) : -(7 + tracers)]
    outs = refs[-(7 + tracers) : -7]
    turned, g_s, a_s, h_s, sens_v, mix_v, sems = refs[-7:]
    rows, width, channels = sens.shape
    levels = mix.shape[0] + 1
    loads = [pltpu.make_async_copy(mix, mix_v, sems.at[rows])]
    loads += [pltpu.make_async_copy(sens.at[r], sens_v.at[r], sems.at[r]) for r in range(rows)]
    for load in loads:
        load.start()
    clear(turned, g_s, a_s, h_s)
    loads[0].wait()

    def store(level, g, a, h):
        at = pl.ds((level % tiles) * SUB + level // tiles, rows, stride=levels)
        for s, value in ((g_s, g), (a_s, a), (h_s, h)):
            put(s, at, value)

    column_factors(lambda l: mix_v[l], levels, (rows, width), store)
    for r in range(rows):
        loads[r + 1].wait()
        put(turned, slice(0, channels), sens_v[r].T)
        at = lambda q: slice(r * levels + q * SUB, r * levels + q * SUB + SUB)
        g, a, h = ([get(s, at(q)) for q in range(tiles)] for s in (g_s, a_s, h_s))
        for j in range(tracers):
            t = order_of(j, direct)
            v = [get(turned, pl.ds(q * tracers + t, SUB, stride=tiles * tracers)) for q in range(tiles)]
            x = column_solve(v, g, a, h)
            for q in range(tiles):
                outs[j][r, q] = x[q]


def pack_levels_kernel(tiles, *refs):
    src, out, src_v, turned, sems = refs[-5:]
    rows, levels, width = src.shape
    loads = [pltpu.make_async_copy(src.at[r], src_v.at[r], sems.at[r]) for r in range(rows)]
    for load in loads:
        load.start()
    clear(turned)
    for r in range(rows):
        loads[r].wait()
        put(turned, slice(r * levels, (r + 1) * levels), src_v[r])
        for q in range(tiles):
            out[r, q] = get(turned, pl.ds(r * levels + q, SUB, stride=tiles))


def pack_mixing_kernel(*refs):
    mix, out, mix_v, sem = refs[-4:]
    rows, width = mix.shape[1:]
    load = pltpu.make_async_copy(mix, mix_v, sem)
    load.start()
    out[...] = jnp.zeros(out.shape, f32)
    load.wait()
    per = SUB // rows
    for level in range(mix.shape[0]):
        at = level % per * rows
        out[level // per, at : at + rows, :width] = mix_v[level]


def unpack_kernel(tiles, direct, *refs):
    n = len(refs) - 2
    pieces, out, turned = refs[:n], refs[n], refs[n + 1]
    rows, width, channels = out.shape
    for r in range(rows):
        for j in range(n):
            t = order_of(j, direct)
            for q in range(tiles):
                put(turned, pl.ds(q * n + t, SUB, stride=tiles * n), pieces[j][r, q])
        out[r] = get(turned, slice(0, channels))[:, :width].T


def filter_block(count, field, tables, cut, flag, emit):
    rows, groups, sub, wide = field.shape
    tiles = groups // QUARTERS
    levels = tiles * sub
    quarter = [
        field[:, q * tiles : (q + 1) * tiles].reshape(rows * levels, wide) for q in range(QUARTERS)
    ]
    halves = []
    for sign in (0, 1):
        t_high, t_low = (t[sign] for t in tables)
        index = wave_index(sign, count, (levels, t_high.shape[1]))
        scale = jnp.where(index == 0, 1.0, 2.0) / (4 * count)
        if sign:
            pair = [quarter[0] - quarter[2], quarter[1] - quarter[3]]
        else:
            pair = [quarter[0] + quarter[2], quarter[1] + quarter[3]]
        high, low = split(jnp.concatenate(pair, axis=1))
        spectrum = product(high, low, t_high, t_low, 0)
        kept = [
            jnp.where(index <= cut(r), spectrum[r * levels : (r + 1) * levels] * scale, 0.0)
            for r in range(rows)
        ]
        high, low = split(jnp.concatenate(kept, axis=0))
        halves.append(product(high, low, t_high, t_low, 1))
    even, odd = halves
    for r in range(rows):
        at = slice(r * levels, (r + 1) * levels)
        for q in range(QUARTERS):
            lanes = slice((q % 2) * wide, (q % 2 + 1) * wide)
            e, o = even[at, lanes], odd[at, lanes]
            smooth = e + o if q < 2 else e - o
            emit(r, q, jnp.where(flag(r) > 0, smooth, quarter[q][at]))


def load_settings(cutoff, polar_flag, cut_s, flag_s, sems):
    loads = [pltpu.make_async_copy(cutoff, cut_s, sems.at[0]), pltpu.make_async_copy(polar_flag, flag_s, sems.at[1])]
    for load in loads:
        load.start()
    return loads


def settings_scratch(rows):
    return [pltpu.SMEM((rows,), jnp.int32)] * 2 + [pltpu.SemaphoreType.DMA((2,))]


def filter_and_edges(count, field, tables, cutoff, polar_flag, out, edge_z, edge_c):
    rows, groups, sub, wide = field.shape
    tiles = groups // QUARTERS
    active = polar_flag[0]
    for r in range(1, rows):
        active = active | polar_flag[r]

    @pl.when(active > 0)
    def _():
        def emit(r, q, value):
            out[r, q * tiles : (q + 1) * tiles] = value.reshape(tiles, sub, wide)

        filter_block(count, field, tables, lambda r: cutoff[r], lambda r: polar_flag[r], emit)

    @pl.when(active == 0)
    def _():
        out[...] = field[...]

    write_edges(out, edge_z, edge_c)


def write_edges(field, edge_z, edge_c):
    shift = field.shape[0] - HALO
    odd = at_odd()
    edge_z[...] = field[pl.ds(odd * shift, HALO)]
    edge_c[...] = field[pl.ds((1 - odd) * shift, HALO)]


def by_parity(from_z, from_c, body):
    odd = at_odd()

    @pl.when(odd == 1)
    def _():
        body(from_c, from_z)

    @pl.when(odd == 0)
    def _():
        body(from_z, from_c)


def face_weights(courant):
    size = jnp.abs(courant)
    rest = 1.0 - size
    t = courant * rest
    edge = t * rest
    upwind = t * size
    cell = courant * size * (3.0 - 2.0 * size)
    ahead = courant >= 0.0
    small = (1.0 / 12.0) * upwind
    small_plus = jnp.where(ahead, small, 0.0)
    small_minus = small - small_plus
    near = (7.0 / 12.0) * edge
    far = (-1.0 / 12.0) * edge
    large = cell - 7.0 * small
    return {
        -2: small_plus,
        -1: far - 7.0 * small_plus,
        0: near + jnp.where(ahead, large, small),
        1: near + jnp.where(ahead, small, large),
        2: far - 7.0 * small_minus,
        3: small_minus,
    }


def stencil(before, now, m):
    if m == 3:
        return before
    if m == -3:
        return -now
    return before - now + 1.0 if m == 0 else before - now


def north_factors(courant, ghosts, out):
    rows, groups = out.shape[1:3]

    def body(i, _):
        before = None
        for f in range(-HALO, rows + HALO):
            now = face_weights(courant(f, i)) if f < rows + HALO - 1 else None
            for r in range(rows):
                m = f - r
                if -HALO <= m <= HALO:
                    out[m + HALO, r, i] = stencil(
                        before[1 - m] if m > -HALO else None, now[-m] if m < HALO else None, m
                    )
            for end, pole_face, step in ((0, 0, 1), (1, rows - 2, -1)):
                for face, k, slot in ((pole_face, 1, 0), (pole_face + step, 2, 1), (pole_face, 2, 2)):
                    if f == face:

                        @pl.when(at_end(end))
                        def _():
                            ghosts[slot, i] = now[k + 1 if end else -k]

            before = now
        return 0

    lax.fori_loop(0, groups, body, 0)


def meridional_pass(field, before, after, north, out):
    rows, groups, sub, wide = field.shape

    def body(i, _):
        total = [None] * rows
        for g in range(-HALO, rows + HALO):
            if g < 0:
                v = before[g + HALO, i]
            else:
                v = field[g, i] if g < rows else after[g - rows, i]
            for r in range(rows):
                if -HALO <= g - r <= HALO:
                    term = north[g - r + HALO, r, i] * v
                    total[r] = term if total[r] is None else total[r] + term
        for r in range(rows):
            out[r, i] = total[r]
        return 0

    lax.fori_loop(0, groups, body, 0)


def pole_pass(field, ghosts, out):
    rows, groups, sub, wide = out.shape
    half = groups // 2
    for end in (0, 1):

        @pl.when(at_end(end))
        def _():
            first, second, third = (rows - 1, rows - 2, rows - 3) if end else (0, 1, 2)

            def body(i, _):
                j = (i + half) % groups
                v0, v1, v2 = field[first, j], field[second, j], field[third, j]
                near = v0 - v1 if end else v1 - v0
                far = v1 - v2 if end else v2 - v1
                out[first, i] = out[first, i] + ghosts[0, j] * near + ghosts[1, j] * far
                out[second, i] = out[second, i] + ghosts[2, j] * near
                return 0

            lax.fori_loop(0, groups, body, 0)


def widen(values, width):
    wide = values[0].shape[1]
    lane = lax.broadcasted_iota(jnp.int32, values[0].shape, 1)
    result = []
    for q in range(QUARTERS):
        after = pltpu.roll(values[(q + 1) % QUARTERS], width, 1)
        before = pltpu.roll(values[(q - 1) % QUARTERS], wide - width, 1)
        padded = jnp.where(lane < width + HALO, after, before)
        padded = jnp.where((lane >= width + HALO) & (lane < wide - HALO), 0.0, padded)
        result.append(jnp.where(lane < width, values[q], padded))
    return result


def shifted(x, m):
    return x if m == 0 else pltpu.roll(x, -m % x.shape[1], 1)


def zonal_pass(width, field, east, emit):
    rows, groups, sub, wide = field.shape
    tiles = groups // QUARTERS

    def body(i, _):
        r, tile = i // tiles, i % tiles
        values = widen([field[r, q * tiles + tile] for q in range(QUARTERS)], width)
        for q in range(QUARTERS):
            total = None
            for m in range(-HALO, HALO + 1):
                term = east[m + HALO, r, q * tiles + tile] * shifted(values[q], m)
                total = term if total is None else total + term
            emit(r, q, tile, total)
        return 0

    lax.fori_loop(0, rows * tiles, body, 0)


def east_factors(width, courant, out):
    rows, groups, sub, wide = courant.shape
    tiles = groups // QUARTERS

    def body(i, _):
        r, tile = i // tiles, i % tiles
        values = widen([courant[r, q * tiles + tile] for q in range(QUARTERS)], width)
        for q in range(QUARTERS):
            w = {k: shifted(x, -k) for k, x in face_weights(values[q]).items()}
            for m in range(-HALO, HALO + 1):
                out[m + HALO, r, q * tiles + tile] = stencil(w.get(1 - m), w.get(-m), m)
        return 0

    lax.fori_loop(0, rows * tiles, body, 0)


def solve_pass(field, g, a, h):
    rows, groups, sub, wide = field.shape
    tiles = groups // QUARTERS

    def body(i, _):
        r, q = i // QUARTERS, i % QUARTERS
        take = lambda ref: [ref[r, q * tiles + tile] for tile in range(tiles)]
        x = column_solve(take(field), take(g), take(a), take(h))
        for tile in range(tiles):
            field[r, q * tiles + tile] = x[tile]
        return 0

    lax.fori_loop(0, rows * QUARTERS, body, 0)


def place(pieces, tiles, direct, out):
    for j in range(QUARTERS):
        out[:, pl.ds(order_of(j, direct) * tiles, tiles)] = pieces[j][...]


def first_filter_kernel(tiles, direct, count, *refs):
    pieces, tables = refs[:4], refs[4:6]
    cutoff, polar_flag, out, edge_z, edge_c, field, cut_s, flag_s, sems = refs[-9:]
    loads = load_settings(cutoff, polar_flag, cut_s, flag_s, sems)
    place(pieces, tiles, direct, field)
    for load in loads:
        load.wait()
    filter_and_edges(count, field, tables, cut_s, flag_s, out, edge_z, edge_c)


def north_kernel(tiles, direct, *refs):
    pieces = refs[:4]
    out, edge_z, edge_c = refs[-3:]
    place(pieces, tiles, direct, out)

    @pl.when(at_end(1))
    def _():
        out[out.shape[0] - 1] = jnp.zeros(out.shape[1:], f32)

    write_edges(out, edge_z, edge_c)


def north_factor_kernel(north, from_z, from_c, *refs):
    out, ghosts = refs[-2:]
    rows = north.shape[0]

    def body(before, after):
        def courant(g, i):
            if g < 0:
                return before[g + HALO, i]
            return north[g, i] if g < rows else after[g - rows, i]

        north_factors(courant, ghosts, out)

    by_parity(from_z, from_c, body)


def east_factor_kernel(tiles, direct, width, *refs):
    pieces, out, raw = refs[:4], refs[4], refs[5]
    place(pieces, tiles, direct, raw)
    east_factors(width, raw, out)


def column_factor_kernel(tiles, direct, *refs):
    pieces = refs[:4]
    g_o, a_o, h_o, g_s, a_s, h_s = refs[4:]
    rows, groups, sub, wide = g_o.shape
    levels = tiles * sub
    per = SUB // rows
    for j in range(QUARTERS):

        def store(level, g, a, h):
            at = (level % tiles) * SUB + level // tiles
            for s, value in ((g_s, g), (a_s, a), (h_s, h)):
                put(s, pl.ds(at, rows, stride=levels), value)

        mix_at = lambda l: pieces[j][l // per, l % per * rows : l % per * rows + rows, :]
        column_factors(mix_at, levels, (rows, wide), store)
        for s, o in ((g_s, g_o), (a_s, a_o), (h_s, h_o)):
            value = get(s, slice(0, rows * levels)).reshape(rows, tiles, sub, wide)
            o[:, pl.ds(order_of(j, direct) * tiles, tiles)] = value


def advect(width, field, from_z, from_c, north, ghosts, east, work, emit):
    by_parity(from_z, from_c, lambda before, after: meridional_pass(field, before, after, north, work))
    pole_pass(field, ghosts, work)
    zonal_pass(width, work, east, emit)


def middle_kernel(width, field, from_z, from_c, north, ghosts, east, g, a, h, *refs):
    tables = refs[:2]
    cutoff, polar_flag, out, edge_z, edge_c, work, result, cut_s, flag_s, sems = refs[2:]
    loads = load_settings(cutoff, polar_flag, cut_s, flag_s, sems)
    tiles = field.shape[1] // QUARTERS

    def emit(r, q, tile, value):
        result[r, q * tiles + tile] = value

    advect(width, field, from_z, from_c, north, ghosts, east, work, emit)
    solve_pass(result, g, a, h)
    for load in loads:
        load.wait()
    filter_and_edges(width, result, tables, cut_s, flag_s, out, edge_z, edge_c)


def last_kernel(width, direct, field, from_z, from_c, north, ghosts, east, *refs):
    outs = refs[:4]
    work, result = refs[4:]
    tiles = field.shape[1] // QUARTERS

    def emit(r, q, tile, value):
        result[r, q * tiles + tile] = value

    advect(width, field, from_z, from_c, north, ghosts, east, work, emit)
    for j in range(QUARTERS):
        outs[j][...] = result[:, pl.ds(order_of(j, direct) * tiles, tiles)]


def call(kernel, outs, scratch, *args, us=1.0, room=16, outside=()):
    specs = [pl.BlockSpec(memory_space=pltpu.VMEM)] * len(args)
    specs += [pl.BlockSpec(memory_space=pltpu.HBM)] * len(outside)
    return pl.pallas_call(
        kernel,
        out_shape=[jax.ShapeDtypeStruct(s, f32) if isinstance(s, tuple) else s for s in outs],
        in_specs=specs,
        out_specs=[pl.BlockSpec(memory_space=pltpu.VMEM)] * len(outs),
        scratch_shapes=[pltpu.VMEM(s, f32) if isinstance(s, tuple) else s for s in scratch],
        compiler_params=pltpu.CompilerParams(vmem_limit_bytes=room * 2**20),
        cost_estimate=pl.CostEstimate(flops=int(us * 10**9), bytes_accessed=10**5, transcendentals=0),
    )(*args, *outside)


def lat_exchange(edge_z, edge_c):
    count = lax.axis_size("lat")
    pairs = lambda start: [p for i in range(start, count - 1, 2) for p in ((i, i + 1), (i + 1, i))]
    from_z = lax.ppermute(edge_z, "lat", pairs(1))
    from_c = lax.ppermute(edge_c, "lat", pairs(0))
    return from_z, from_c


def on_device(sensitivity, courant_east, courant_north, mixing, cutoff, polar_flag):
    rows, width, channels = sensitivity.shape
    levels = courant_east.shape[2]
    tracers = channels // levels
    tiles = levels // SUB
    parts = lax.axis_size("lon")
    nlon = width * parts
    quarter = nlon // QUARTERS
    wide = round_up(quarter + 2 * HALO, 128)
    direct = parts == tracers == QUARTERS
    piece = wide if direct else round_up(width, 128)
    tables = fourier_tables(nlon, wide)

    swap = lambda x, s: lax.ppermute(x, "lon", [(i, i ^ s) for i in range(parts)])

    def quarters_of(blocks):
        whole = jnp.moveaxis(blocks[..., :width], 0, -2)
        whole = whole.reshape(whole.shape[:-2] + (QUARTERS, quarter))
        whole = jnp.pad(whole, [(0, 0)] * (whole.ndim - 1) + [(0, wide - quarter)])
        return [whole[..., q, :] for q in range(QUARTERS)]

    def gather(x):
        if direct:
            return [x] + [swap(x, s) for s in range(1, parts)]
        return quarters_of(lax.all_gather(x, "lon"))

    def to_tracers(ys):
        if direct:
            return [ys[0]] + [swap(ys[s], s) for s in range(1, parts)]
        sent = jnp.stack([ys[d % tracers] for d in range(parts)])
        return quarters_of(lax.all_to_all(sent, "lon", split_axis=0, concat_axis=0, tiled=True))

    def to_longitudes(zs):
        if direct:
            return [zs[0]] + [swap(zs[s], s) for s in range(1, parts)]
        whole = jnp.concatenate([z[..., :quarter] for z in zs], axis=-1)
        blocks = jnp.moveaxis(whole.reshape(whole.shape[:-1] + (parts, width)), -2, 0)
        came = lax.all_to_all(blocks, "lon", split_axis=0, concat_axis=0, tiled=True)
        came = jnp.pad(came, [(0, 0)] * (came.ndim - 1) + [(0, piece - width)])
        return [came[t] for t in range(tracers)]

    north_t = courant_north.transpose(0, 2, 1)
    east_t = courant_east.transpose(0, 2, 1)
    mix_t = mixing.transpose(2, 0, 1)
    block = (rows, tiles, SUB, piece)
    full = (rows, QUARTERS * tiles, SUB, wide)
    edge = (HALO,) + full[1:]
    turned = (piece // 128, rows * levels, 128)

    def pack(x, *after):
        scratch = [x.shape, turned, pltpu.SemaphoreType.DMA((rows,))]
        return call(partial(pack_levels_kernel, tiles), [block], scratch, *after, outside=[x], us=0.4)[0]

    north_piece = pack(north_t)
    north_pieces = gather(north_piece)
    ys = call(
        partial(first_solve_kernel, tiles, direct, tracers),
        [block] * tracers,
        [(piece // 128, channels, 128)]
        + factor_scratch(rows, levels, piece)
        + [sensitivity.shape, mix_t.shape, pltpu.SemaphoreType.DMA((rows + 1,))],
        north_piece,
        outside=[sensitivity, mix_t],
        us=3.0,
    )
    pieces = to_tracers(ys)
    north, north_z, north_c = call(partial(north_kernel, tiles, direct), [full, edge, edge], [], *north_pieces, ys[0])
    north_z, north_c = lat_exchange(north_z, north_c)
    east_pieces = gather(pack(east_t, *north_pieces[1:]))
    state, edge_z, edge_c = call(
        partial(first_filter_kernel, tiles, direct, quarter),
        [full, edge, edge],
        [full] + settings_scratch(rows),
        *pieces, *tables, north,
        us=2.5,
        outside=[cutoff, polar_flag],
    )
    (mix_piece,) = call(
        pack_mixing_kernel,
        [(rows * tiles, SUB, piece)],
        [mix_t.shape, pltpu.SemaphoreType.DMA(())],
        edge_z,
        outside=[mix_t],
    )
    mix_pieces = gather(mix_piece)
    edges = lat_exchange(edge_z, edge_c)
    north, ghosts = call(
        north_factor_kernel, [(2 * HALO + 1,) + full, (3,) + full[1:]], [], north, north_z, north_c, edge_z
    )
    (east,) = call(
        partial(east_factor_kernel, tiles, direct, quarter), [(2 * HALO + 1,) + full], [full], *east_pieces, us=3.0
    )
    g, a, h = call(
        partial(column_factor_kernel, tiles, direct), [full] * 3, factor_scratch(rows, levels, wide), *mix_pieces, us=2.2
    )
    for substep in range(SUBSTEPS - 1):
        state, edge_z, edge_c = call(
            partial(middle_kernel, quarter),
            [full, edge, edge],
            [full, full] + settings_scratch(rows),
            state, *edges, north, ghosts, east, g, a, h, *tables,
            room=MIDDLE_ROOM,
        us=6.0,
            outside=[cutoff, polar_flag],
        )
        edges = lat_exchange(edge_z, edge_c)
    zs = call(
        partial(last_kernel, quarter, direct),
        [(rows, tiles, SUB, wide)] * QUARTERS,
        [full, full],
        state, *edges, north, ghosts, east,
        us=3.5,
    )
    pieces = to_longitudes(zs)
    (out,) = call(
        partial(unpack_kernel, tiles, direct), [sensitivity.shape], [(piece // 128, channels, 128)], *pieces
    )
    return out


def solution(mesh):
    return jax.shard_map(
        on_device,
        mesh=mesh,
        in_specs=(
            P("lat", "lon", None),
            P("lat", "lon", None),
            P("lat", "lon", None),
            P("lat", "lon", None),
            P("lat"),
            P("lat"),
        ),
        out_specs=P("lat", "lon", None),
        check_vma=False,
    )
```

time: 117 us -> 85.8 us (0.73)
  Pallas kernels: 32.4 us -> 20.7 us
  local copies, waits for them, and re-layouts: 13.6 us -> 2.99 us
  waiting for transfers between devices: 42.4 us -> 33.6 us
    pallas_call x9 -> x12, Pallas kernels: 32.4 us -> 20.7 us  [call(): pl.pallas_call(kernel, out_shape=[jax.ShapeDtypeStruct(s, f32) if isinsta...]
    unnamed x54 -> x18, local copies, waits for them, and re-layouts: 13.5 us -> 2.99 us
    ppermute x12 -> x15, waiting for transfers between devices: 33.6 us -> 26.1 us  [on_device(): lax.ppermute(x, 'lon', [(i, i ^ s) for i in range(parts)])]
    ppermute x3, starting transfers between devices: 5.66 us -> 2.28 us  [lat_exchange(): from_c = lax.ppermute(edge_c, 'lat', pairs(0))]
    ppermute x12 -> x15, starting transfers between devices: 16.2 us -> 18.7 us  [on_device(): lax.ppermute(x, 'lon', [(i, i ^ s) for i in range(parts)])]
    ppermute x3, waiting for transfers between devices: 8.79 us -> 7.53 us  [lat_exchange(): from_z = lax.ppermute(edge_z, 'lat', pairs(1))]
    ppermute x3, starting transfers between devices: 5.81 us -> 7.03 us  [lat_exchange(): from_z = lax.ppermute(edge_z, 'lat', pairs(1))]
  transfers between devices with their start and end apart: 18 -> 21, of which waited for: 6 -> 8; matrix products, arithmetic and copies ran while one was open for 0% -> 0% of each run, Pallas kernels for 6% -> 13%
where the time goes in v2:
time: 85.8 us; the launch traced here: 85.6 us
  waiting for transfers between devices  33.6 us (39%)
  starting transfers between devices  28.1 us (33%)
  Pallas kernels  20.7 us (24%)
  local copies, waits for them, and re-layouts  2.99 us (3%)
    ppermute x15, waiting for transfers between devices, on_device(): lax.ppermute(x, 'lon', [(i, i ^ s) for i in range(parts)])  26.1 us
    pallas_call x12, Pallas kernels, call(): pl.pallas_call(kernel, out_shape=[jax.ShapeDtypeStruct(s, f32) if isinsta...  20.7 us
    ppermute x15, starting transfers between devices, on_device(): lax.ppermute(x, 'lon', [(i, i ^ s) for i in range(parts)])  18.7 us
    ppermute x3, waiting for transfers between devices, lat_exchange(): from_z = lax.ppermute(edge_z, 'lat', pairs(1))  7.53 us
    ppermute x3, starting transfers between devices, lat_exchange(): from_z = lax.ppermute(edge_z, 'lat', pairs(1))  7.03 us
    unnamed x18, local copies, waits for them, and re-layouts  2.99 us
    ppermute x3, starting transfers between devices, lat_exchange(): from_c = lax.ppermute(edge_c, 'lat', pairs(0))  2.28 us
  transfers between devices with their start and end apart: 21, of which 8 were waited for; matrix products, arithmetic and copies ran while one was open for 0% of the time, Pallas kernels for 13%

profile of v2, /device:TPU:8, one launch (start us, length us, event | category | flops | bytes accessed | tf_op | source)
XLA Modules:
  0.0 85.6 jit_solution(8980666528011006579)
XLA Ops:
  0.0 0.9 %copy-done.1 = f32[4,360,32]{1,2,0:T(8,128)S(1)} copy-done((f32[4,360,32]{1,2,0:T(8,128)S(1)}, f32[4,360,32]{1,2,0:T(8,128)}, u32[]{:S(2)}) %copy-start.1) | copy-done | bytes 184344
  0.9 0.3 shard_map.82.refs_0_
  1.3 2.5 %collective-permute-start.5 = (f32[4,4,8,384]{3,2,1,0:T(8,128)S(1)}, f32[4,4,8,384]{3,2,1,0:T(8,128)S(1)}, u32[]{:S(2)}, u32[]{:S(2)}) collective-permute-start(f32[4,4,8,384]{3,2,1,0:T(8,128)S(1)} %shard_map.82.refs_0_), channel_id=1, source_target_pairs={{0,24},{8,16},{16,8},{24,0},{1,25},{9,17},{17,9},{25,1},{2,26},{10... | collective-permute-start | bytes 589832 | tf_op jit(solution)/shard_map/ppermute | solution.py:599
  3.8 0.5 collective-permute-start.4
  4.3 0.5 collective-permute-start.3
  4.8 1.1 %copy-done = f32[4,360,128]{2,1,0:T(8,128)S(1)} copy-done((f32[4,360,128]{2,1,0:T(8,128)S(1)}, f32[4,360,128]{2,1,0:T(8,128)}, u32[]{:S(2)}) %copy-start) | copy-done | bytes 737304
  5.9 0.9 %copy-done.3 = f32[4,360,31]{1,0,2:T(4,128)S(1)} copy-done((f32[4,360,31]{1,0,2:T(4,128)S(1)}, f32[4,360,31]{1,0,2:T(4,128)}, u32[]{:S(2)}) %copy-start.3) | copy-done | bytes 178584
  6.9 0.0 copy-start.8
  6.9 2.9 %shard_map.83 = (f32[4,4,8,384]{3,2,1,0:T(8,128)S(1)}, f32[4,4,8,384]{3,2,1,0:T(8,128)S(1)}, f32[4,4,8,384]{3,2,1,0:T(8,128)S(1)}, f32[4,4,8,384]{3,2,1,0:T(8,128)S(1)}) custom-call(f32[4,4,8,384]{3,2,1,0:T(8,128)S(1)} %shard_map.82.refs_0_, f32[4,360,128]{2,1,0:T(8,128)S(1)} %copy-done, f32[31,4,360]{2,1,0:T(4,128)S(1)} %bitcast.5), custom_call_target="tpu_custom_call" | custom-call | flops 3000000000 | bytes 100000 | tf_op jit(solution)/shard_map/pallas_call | solution.py:567
  9.8 1.6 %collective-permute-start = (f32[4,4,8,384]{3,2,1,0:T(8,128)S(1)}, f32[4,4,8,384]{3,2,1,0:T(8,128)S(1)}, u32[]{:S(2)}, u32[]{:S(2)}) collective-permute-start(f32[4,4,8,384]{3,2,1,0:T(8,128)S(1)} %get-tuple-element.28), channel_id=1, source_target_pairs={{0,8},{8,0},{16,24},{24,16},{1,9},{9,1},{17,25},{25,17},{2,10},{10... | collective-permute-start | bytes 589832 | tf_op jit(solution)/shard_map/ppermute | solution.py:599
  11.4 1.5 %collective-permute-start.1 = (f32[4,4,8,384]{3,2,1,0:T(8,128)S(1)}, f32[4,4,8,384]{3,2,1,0:T(8,128)S(1)}, u32[]{:S(2)}, u32[]{:S(2)}) collective-permute-start(f32[4,4,8,384]{3,2,1,0:T(8,128)S(1)} %get-tuple-element.29), channel_id=1, source_target_pairs={{0,16},{8,24},{16,0},{24,8},{1,17},{9,25},{17,1},{25,9},{2,18},{10... | collective-permute-start | bytes 589832 | tf_op jit(solution)/shard_map/ppermute | solution.py:599
  12.9 0.0 collective-permute-done.5.refs_3_.refs_2_
  12.9 0.5 collective-permute-start.2
  13.4 0.0 collective-permute-done.4.refs_2_.refs_1_
  13.4 0.9 %collective-permute-done.3.refs_1_.refs_0_ = f32[4,4,8,384]{3,2,1,0:T(8,128)S(1)} collective-permute-done((f32[4,4,8,384]{3,2,1,0:T(8,128)S(1)}, f32[4,4,8,384]{3,2,1,0:T(8,128)S(1)}, u32[]{:S(2)}, u32[]{:S(2)}) %collective-permute-start.3) | collective-permute-done | bytes 196640 | tf_op jit(solution)/shard_map/ppermute | solution.py:599
  14.3 0.0 copy-done.2
  14.3 0.3 shard_map.87.refs_0_
  14.7 1.6 %collective-permute-start.12 = (f32[4,4,8,384]{3,2,1,0:T(8,128)S(1)}, f32[4,4,8,384]{3,2,1,0:T(8,128)S(1)}, u32[]{:S(2)}, u32[]{:S(2)}) collective-permute-start(f32[4,4,8,384]{3,2,1,0:T(8,128)S(1)} %shard_map.87.refs_0_), channel_id=1, source_target_pairs={{0,24},{8,16},{16,8},{24,0},{1,25},{9,17},{17,9},{25,1},{2,26},{10... | collective-permute-start | bytes 589832 | tf_op jit(solution)/shard_map/ppermute | solution.py:599
  16.3 1.4 %collective-permute-start.11 = (f32[4,4,8,384]{3,2,1,0:T(8,128)S(1)}, f32[4,4,8,384]{3,2,1,0:T(8,128)S(1)}, u32[]{:S(2)}, u32[]{:S(2)}) collective-permute-start(f32[4,4,8,384]{3,2,1,0:T(8,128)S(1)} %shard_map.87.refs_0_), channel_id=1, source_target_pairs={{0,16},{8,24},{16,0},{24,8},{1,17},{9,25},{17,1},{25,9},{2,18},{10... | collective-permute-start | bytes 589832 | tf_op jit(solution)/shard_map/ppermute | solution.py:599
  17.6 0.1 shard_map.84
  17.8 0.0 copy-start.4
  17.8 0.7 collective-permute-done.refs_1_
  18.5 10.0 %collective-permute-done.1.refs_2_ = f32[4,4,8,384]{3,2,1,0:T(8,128)S(1)} collective-permute-done((f32[4,4,8,384]{3,2,1,0:T(8,128)S(1)}, f32[4,4,8,384]{3,2,1,0:T(8,128)S(1)}, u32[]{:S(2)}, u32[]{:S(2)}) %collective-permute-start.1) | collective-permute-done | bytes 196640 | tf_op jit(solution)/shard_map/ppermute | solution.py:599
  28.5 0.0 collective-permute-done.2.refs_3_
  28.5 0.0 copy-done.5
  28.5 0.0 copy-done.6
  28.5 0.0 copy-done.7
  28.6 0.0 copy-done.8
  28.6 0.7 shard_map.85
  29.3 0.3 shard_map.89.refs_0_
  29.6 0.2 collective-permute-start.15
  29.8 2.6 %collective-permute-start.14 = (f32[16,8,384]{2,1,0:T(8,128)S(1)}, f32[16,8,384]{2,1,0:T(8,128)S(1)}, u32[]{:S(2)}, u32[]{:S(2)}) collective-permute-start(f32[16,8,384]{2,1,0:T(8,128)S(1)} %shard_map.89.refs_0_), channel_id=1, source_target_pairs={{0,16},{8,24},{16,0},{24,8},{1,17},{9,25},{17,1},{25,9},{2,18},{10... | collective-permute-start | bytes 589832 | tf_op jit(solution)/shard_map/ppermute | solution.py:599
  32.5 0.7 collective-permute-start.13
  33.2 0.0 collective-permute-done.12.refs_3_
  33.2 1.9 %collective-permute-start.8 = (f32[3,16,8,384]{3,2,1,0:T(8,128)S(1)}, f32[3,16,8,384]{3,2,1,0:T(8,128)S(1)}, u32[]{:S(2)}, u32[]{:S(2)}) collective-permute-start(f32[3,16,8,384]{3,2,1,0:T(8,128)S(1)} %get-tuple-element.35), channel_id=1, source_target_pairs={{1,2},{2,1},{3,4},{4,3},{5,6},{6,5},{9,10},{10,9},{11,12},{12,11},... | collective-permute-start | bytes 1769480 | tf_op jit(solution)/shard_map/ppermute | solution.py:581
  35.1 0.0 collective-permute-done.11.refs_2_
  35.1 1.7 %collective-permute-start.9 = (f32[3,16,8,384]{3,2,1,0:T(8,128)S(1)}, f32[3,16,8,384]{3,2,1,0:T(8,128)S(1)}, u32[]{:S(2)}, u32[]{:S(2)}) collective-permute-start(f32[3,16,8,384]{3,2,1,0:T(8,128)S(1)} %get-tuple-element.36), channel_id=1, source_target_pairs={{0,1},{1,0},{2,3},{3,2},{4,5},{5,4},{6,7},{7,6},{8,9},{9,8},{10,11... | collective-permute-start | bytes 1769480 | tf_op jit(solution)/shard_map/ppermute | solution.py:582
  36.8 0.0 collective-permute-done.15.refs_3_
  36.8 0.1 collective-permute-start.7
  36.9 1.4 %collective-permute-done.14.refs_2_ = f32[16,8,384]{2,1,0:T(8,128)S(1)} collective-permute-done((f32[16,8,384]{2,1,0:T(8,128)S(1)}, f32[16,8,384]{2,1,0:T(8,128)S(1)}, u32[]{:S(2)}, u32[]{:S(2)}) %collective-permute-start.14) | collective-permute-done | bytes 196640 | tf_op jit(solution)/shard_map/ppermute | solution.py:599
  38.4 1.9 %collective-permute-start.6 = (f32[3,16,8,384]{3,2,1,0:T(8,128)S(1)}, f32[3,16,8,384]{3,2,1,0:T(8,128)S(1)}, u32[]{:S(2)}, u32[]{:S(2)}) collective-permute-start(f32[3,16,8,384]{3,2,1,0:T(8,128)S(1)} %get-tuple-element.33.refs_0_), channel_id=1, source_target_pairs={{1,2},{2,1},{3,4},{4,3},{5,6},{6,5},{9,10},{10,9},{11,12},{12,11},... | collective-permute-start | bytes 1769480 | tf_op jit(solution)/shard_map/ppermute | solution.py:581
  40.3 0.0 collective-permute-done.13.refs_1_
  40.3 1.6 %collective-permute-start.10 = (f32[4,4,8,384]{3,2,1,0:T(8,128)S(1)}, f32[4,4,8,384]{3,2,1,0:T(8,128)S(1)}, u32[]{:S(2)}, u32[]{:S(2)}) collective-permute-start(f32[4,4,8,384]{3,2,1,0:T(8,128)S(1)} %shard_map.87.refs_0_), channel_id=1, source_target_pairs={{0,8},{8,0},{16,24},{24,16},{1,9},{9,1},{17,25},{25,17},{2,10},{10... | collective-permute-start | bytes 589832 | tf_op jit(solution)/shard_map/ppermute | solution.py:599
  41.8 2.2 %shard_map.90 = (f32[4,16,8,384]{3,2,1,0:T(8,128)S(1)}, f32[4,16,8,384]{3,2,1,0:T(8,128)S(1)}, f32[4,16,8,384]{3,2,1,0:T(8,128)S(1)}) custom-call(f32[16,8,384]{2,1,0:T(8,128)S(1)} %shard_map.89.refs_0_, f32[16,8,384]{2,1,0:T(8,128)S(1)} %collective-permute-done.13.refs_1_, f32[16,8,384]{2,1,0:T(8,128)S(1)} %collective-permute-done.14.refs_2_, ...), custom_call_target="tpu_custom_call" | custom-call | flops 2200000000 | bytes 100000 | tf_op jit(solution)/shard_map/pallas_call | solution.py:567
  44.0 3.4 %collective-permute-done.10.refs_1_ = f32[4,4,8,384]{3,2,1,0:T(8,128)S(1)} collective-permute-done((f32[4,4,8,384]{3,2,1,0:T(8,128)S(1)}, f32[4,4,8,384]{3,2,1,0:T(8,128)S(1)}, u32[]{:S(2)}, u32[]{:S(2)}) %collective-permute-start.10) | collective-permute-done | bytes 196640 | tf_op jit(solution)/shard_map/ppermute | solution.py:599
  47.5 3.0 %shard_map.88.east = f32[7,4,16,8,384]{4,3,2,1,0:T(8,128)S(1)} custom-call(f32[4,4,8,384]{3,2,1,0:T(8,128)S(1)} %shard_map.87.refs_0_, f32[4,4,8,384]{3,2,1,0:T(8,128)S(1)} %collective-permute-done.10.refs_1_, f32[4,4,8,384]{3,2,1,0:T(8,128)S(1)} %collective-permute-done.11.refs_2_, f32[4,4,8,384]{3,2,1,0:T(8,128)S(1)} %collective-permute-done.12.refs_3_), custom_call_target="tpu_custom_call" | custom-call | flops 3000000000 | bytes 100000 | tf_op jit(solution)/shard_map/pallas_call | solution.py:567
  50.4 0.0 collective-permute-done.8.from_z
  50.5 0.0 collective-permute-done.9.from_c
  50.5 1.5 %shard_map.86 = (f32[7,4,16,8,384]{4,3,2,1,0:T(8,128)S(1)}, f32[3,16,8,384]{3,2,1,0:T(8,128)S(1)}) custom-call(f32[4,16,8,384]{3,2,1,0:T(8,128)S(1)} %get-tuple-element.31.refs_6_.north, f32[3,16,8,384]{3,2,1,0:T(8,128)S(1)} %collective-permute-done.8.from_z, f32[3,16,8,384]{3,2,1,0:T(8,128)S(1)} %collective-permute-done.9.from_c, ...), custom_call_target="tpu_custom_call" | custom-call | flops 1000000000 | bytes 100000 | tf_op jit(solution)/shard_map/pallas_call | solution.py:567
  52.0 0.0 collective-permute-done.7.from_c
  52.0 0.0 collective-permute-done.6.from_z
  52.0 4.4 %shard_map.91 = (f32[4,16,8,384]{3,2,1,0:T(8,128)S(1)}, f32[3,16,8,384]{3,2,1,0:T(8,128)S(1)}, f32[3,16,8,384]{3,2,1,0:T(8,128)S(1)}) custom-call(f32[4,16,8,384]{3,2,1,0:T(8,128)S(1)} %get-tuple-element.32.field, f32[3,16,8,384]{3,2,1,0:T(8,128)S(1)} %collective-permute-done.6.from_z, f32[3,16,8,384]{3,2,1,0:T(8,128)S(1)} %collective-permute-done.7.from_c, ...), custom_call_target="tpu_custom_call" | custom-call | flops 6000000000 | bytes 100000 | tf_op jit(solution)/shard_map/pallas_call | solution.py:567
  56.4 3.2 %collective-permute-start.16 = (f32[3,16,8,384]{3,2,1,0:T(8,128)S(1)}, f32[3,16,8,384]{3,2,1,0:T(8,128)S(1)}, u32[]{:S(2)}, u32[]{:S(2)}) collective-permute-start(f32[3,16,8,384]{3,2,1,0:T(8,128)S(1)} %get-tuple-element.43), channel_id=1, source_target_pairs={{1,2},{2,1},{3,4},{4,3},{5,6},{6,5},{9,10},{10,9},{11,12},{12,11},... | collective-permute-start | bytes 1769480 | tf_op jit(solution)/shard_map/ppermute | solution.py:581
  59.7 0.4 collective-permute-start.17
  60.1 7.5 %collective-permute-done.16.from_z = f32[3,16,8,384]{3,2,1,0:T(8,128)S(1)} collective-permute-done((f32[3,16,8,384]{3,2,1,0:T(8,128)S(1)}, f32[3,16,8,384]{3,2,1,0:T(8,128)S(1)}, u32[]{:S(2)}, u32[]{:S(2)}) %collective-permute-start.16) | collective-permute-done | bytes 589856 | tf_op jit(solution)/shard_map/ppermute | solution.py:581
  67.6 0.0 collective-permute-done.17.from_c
  67.6 3.4 %shard_map.92 = (f32[4,4,8,384]{3,2,1,0:T(8,128)S(1)}, f32[4,4,8,384]{3,2,1,0:T(8,128)S(1)}, f32[4,4,8,384]{3,2,1,0:T(8,128)S(1)}, f32[4,4,8,384]{3,2,1,0:T(8,128)S(1)}) custom-call(f32[4,16,8,384]{3,2,1,0:T(8,128)S(1)} %get-tuple-element.42.field, f32[3,16,8,384]{3,2,1,0:T(8,128)S(1)} %collective-permute-done.16.from_z, ...), custom_call_target="tpu_custom_call" | custom-call | flops 3500000000 | bytes 100000 | tf_op jit(solution)/shard_map/pallas_call | solution.py:567
  71.1 1.6 %collective-permute-start.18 = (f32[4,4,8,384]{3,2,1,0:T(8,128)S(1)}, f32[4,4,8,384]{3,2,1,0:T(8,128)S(1)}, u32[]{:S(2)}, u32[]{:S(2)}) collective-permute-start(f32[4,4,8,384]{3,2,1,0:T(8,128)S(1)} %get-tuple-element.46), channel_id=1, source_target_pairs={{0,8},{8,0},{16,24},{24,16},{1,9},{9,1},{17,25},{25,17},{2,10},{10... | collective-permute-start | bytes 589832 | tf_op jit(solution)/shard_map/ppermute | solution.py:599
  72.6 0.8 collective-permute-start.19
  73.4 1.2 %collective-permute-start.20 = (f32[4,4,8,384]{3,2,1,0:T(8,128)S(1)}, f32[4,4,8,384]{3,2,1,0:T(8,128)S(1)}, u32[]{:S(2)}, u32[]{:S(2)}) collective-permute-start(f32[4,4,8,384]{3,2,1,0:T(8,128)S(1)} %get-tuple-element.48), channel_id=1, source_target_pairs={{0,24},{8,16},{16,8},{24,0},{1,25},{9,17},{17,9},{25,1},{2,26},{10... | collective-permute-start | bytes 589832 | tf_op jit(solution)/shard_map/ppermute | solution.py:599
  74.6 4.3 %collective-permute-done.18.refs_1_ = f32[4,4,8,384]{3,2,1,0:T(8,128)S(1)} collective-permute-done((f32[4,4,8,384]{3,2,1,0:T(8,128)S(1)}, f32[4,4,8,384]{3,2,1,0:T(8,128)S(1)}, u32[]{:S(2)}, u32[]{:S(2)}) %collective-permute-start.18) | collective-permute-done | bytes 196640 | tf_op jit(solution)/shard_map/ppermute | solution.py:599
  78.9 5.2 %collective-permute-done.19.refs_2_ = f32[4,4,8,384]{3,2,1,0:T(8,128)S(1)} collective-permute-done((f32[4,4,8,384]{3,2,1,0:T(8,128)S(1)}, f32[4,4,8,384]{3,2,1,0:T(8,128)S(1)}, u32[]{:S(2)}, u32[]{:S(2)}) %collective-permute-start.19) | collective-permute-done | bytes 196640 | tf_op jit(solution)/shard_map/ppermute | solution.py:599
  84.1 0.0 collective-permute-done.20.refs_3_
  84.1 1.4 %shard_map.93 = f32[4,360,128]{2,1,0:T(8,128)} custom-call(f32[4,4,8,384]{3,2,1,0:T(8,128)S(1)} %get-tuple-element.45.refs_0_, f32[4,4,8,384]{3,2,1,0:T(8,128)S(1)} %collective-permute-done.18.refs_1_, f32[4,4,8,384]{3,2,1,0:T(8,128)S(1)} %collective-permute-done.19.refs_2_, f32[4,4,8,384]{3,2,1,0:T(8,128)S(1)} %collective-permute-done.20.refs_3_), custom_call_target="tpu_custom_call" | custom-call | flops 1000000000 | bytes 100000 | tf_op jit(solution)/shard_map/pallas_call | solution.py:567
  (8 shorter events, 0.0 us)
Async XLA Ops:
  0.0 0.9 %copy-start.1 = (f32[4,360,32]{1,2,0:T(8,128)S(1)}, f32[4,360,32]{1,2,0:T(8,128)}, u32[]{:S(2)}) copy-start(f32[4,360,32]{1,2,0:T(8,128)} %param.10) | copy-start | bytes 552964
  1.3 11.6 %collective-permute-start.5 = (f32[4,4,8,384]{3,2,1,0:T(8,128)S(1)}, f32[4,4,8,384]{3,2,1,0:T(8,128)S(1)}, u32[]{:S(2)}, u32[]{:S(2)}) collective-permute-start(f32[4,4,8,384]{3,2,1,0:T(8,128)S(1)} %shard_map.82.refs_0_), channel_id=1, source_target_pairs={{0,24},{8,16},{16,8},{24,0},{1,25},{9,17},{17,9},{25,1},{2,26},{10... | collective-permute-start | bytes 589832 | tf_op jit(solution)/shard_map/ppermute | solution.py:599
  3.8 9.6 %collective-permute-start.4 = (f32[4,4,8,384]{3,2,1,0:T(8,128)S(1)}, f32[4,4,8,384]{3,2,1,0:T(8,128)S(1)}, u32[]{:S(2)}, u32[]{:S(2)}) collective-permute-start(f32[4,4,8,384]{3,2,1,0:T(8,128)S(1)} %shard_map.82.refs_0_), channel_id=1, source_target_pairs={{0,16},{8,24},{16,0},{24,8},{1,17},{9,25},{17,1},{25,9},{2,18},{10... | collective-permute-start | bytes 589832 | tf_op jit(solution)/shard_map/ppermute | solution.py:599
  4.3 10.0 %collective-permute-start.3 = (f32[4,4,8,384]{3,2,1,0:T(8,128)S(1)}, f32[4,4,8,384]{3,2,1,0:T(8,128)S(1)}, u32[]{:S(2)}, u32[]{:S(2)}) collective-permute-start(f32[4,4,8,384]{3,2,1,0:T(8,128)S(1)} %shard_map.82.refs_0_), channel_id=1, source_target_pairs={{0,8},{8,0},{16,24},{24,16},{1,9},{9,1},{17,25},{25,17},{2,10},{10... | collective-permute-start | bytes 589832 | tf_op jit(solution)/shard_map/ppermute | solution.py:599
  4.8 1.1 %copy-start = (f32[4,360,128]{2,1,0:T(8,128)S(1)}, f32[4,360,128]{2,1,0:T(8,128)}, u32[]{:S(2)}) copy-start(f32[4,360,128]{2,1,0:T(8,128)} %refs_1_.2) | copy-start | bytes 2211844
  5.9 0.9 %copy-start.3 = (f32[4,360,31]{1,0,2:T(4,128)S(1)}, f32[4,360,31]{1,0,2:T(4,128)}, u32[]{:S(2)}) copy-start(f32[4,360,31]{1,0,2:T(4,128)} %param.11) | copy-start | bytes 535684
  6.9 7.5 %copy-start.2 = (f32[4,360,32]{1,2,0:T(8,128)S(1)}, f32[4,360,32]{1,2,0:T(8,128)}, u32[]{:S(2)}) copy-start(f32[4,360,32]{1,2,0:T(8,128)} %param.9) | copy-start | bytes 552964
  6.9 21.7 %copy-start.5 = (s32[4]{0:T(128)S(1)}, s32[4]{0:T(128)}, u32[]{:S(2)}) copy-start(s32[4]{0:T(128)} %refs_2_.1) | copy-start | bytes 52
  6.9 21.7 %copy-start.6 = (s32[4]{0:T(128)S(1)}, s32[4]{0:T(128)}, u32[]{:S(2)}) copy-start(s32[4]{0:T(128)} %refs_3_.1) | copy-start | bytes 52
  6.9 21.7 %copy-start.7 = (bf16[2,768,384]{2,1,0:T(8,128)(2,1)S(1)}, bf16[2,768,384]{2,1,0:T(8,128)(2,1)}, u32[]{:S(2)}) copy-start(bf16[2,768,384]{2,1,0:T(8,128)(2,1)} %constant.5.clone.refs_5_.refs_1_) | copy-start | bytes 3538948
  6.9 21.7 %copy-start.8 = (bf16[2,768,384]{2,1,0:T(8,128)(2,1)S(1)}, bf16[2,768,384]{2,1,0:T(8,128)(2,1)}, u32[]{:S(2)}) copy-start(bf16[2,768,384]{2,1,0:T(8,128)(2,1)} %constant.4.clone.refs_4_.refs_0_) | copy-start | bytes 3538948
  9.8 8.7 %collective-permute-start = (f32[4,4,8,384]{3,2,1,0:T(8,128)S(1)}, f32[4,4,8,384]{3,2,1,0:T(8,128)S(1)}, u32[]{:S(2)}, u32[]{:S(2)}) collective-permute-start(f32[4,4,8,384]{3,2,1,0:T(8,128)S(1)} %get-tuple-element.28), channel_id=1, source_target_pairs={{0,8},{8,0},{16,24},{24,16},{1,9},{9,1},{17,25},{25,17},{2,10},{10... | collective-permute-start | bytes 589832 | tf_op jit(solution)/shard_map/ppermute | solution.py:599
  11.4 17.2 %collective-permute-start.1 = (f32[4,4,8,384]{3,2,1,0:T(8,128)S(1)}, f32[4,4,8,384]{3,2,1,0:T(8,128)S(1)}, u32[]{:S(2)}, u32[]{:S(2)}) collective-permute-start(f32[4,4,8,384]{3,2,1,0:T(8,128)S(1)} %get-tuple-element.29), channel_id=1, source_target_pairs={{0,16},{8,24},{16,0},{24,8},{1,17},{9,25},{17,1},{25,9},{2,18},{10... | collective-permute-start | bytes 589832 | tf_op jit(solution)/shard_map/ppermute | solution.py:599
  12.9 15.6 %collective-permute-start.2 = (f32[4,4,8,384]{3,2,1,0:T(8,128)S(1)}, f32[4,4,8,384]{3,2,1,0:T(8,128)S(1)}, u32[]{:S(2)}, u32[]{:S(2)}) collective-permute-start(f32[4,4,8,384]{3,2,1,0:T(8,128)S(1)} %get-tuple-element.30), channel_id=1, source_target_pairs={{0,24},{8,16},{16,8},{24,0},{1,25},{9,17},{17,9},{25,1},{2,26},{10... | collective-permute-start | bytes 589832 | tf_op jit(solution)/shard_map/ppermute | solution.py:599
  14.7 18.5 %collective-permute-start.12 = (f32[4,4,8,384]{3,2,1,0:T(8,128)S(1)}, f32[4,4,8,384]{3,2,1,0:T(8,128)S(1)}, u32[]{:S(2)}, u32[]{:S(2)}) collective-permute-start(f32[4,4,8,384]{3,2,1,0:T(8,128)S(1)} %shard_map.87.refs_0_), channel_id=1, source_target_pairs={{0,24},{8,16},{16,8},{24,0},{1,25},{9,17},{17,9},{25,1},{2,26},{10... | collective-permute-start | bytes 589832 | tf_op jit(solution)/shard_map/ppermute | solution.py:599
  16.3 18.8 %collective-permute-start.11 = (f32[4,4,8,384]{3,2,1,0:T(8,128)S(1)}, f32[4,4,8,384]{3,2,1,0:T(8,128)S(1)}, u32[]{:S(2)}, u32[]{:S(2)}) collective-permute-start(f32[4,4,8,384]{3,2,1,0:T(8,128)S(1)} %shard_map.87.refs_0_), channel_id=1, source_target_pairs={{0,16},{8,24},{16,0},{24,8},{1,17},{9,25},{17,1},{25,9},{2,18},{10... | collective-permute-start | bytes 589832 | tf_op jit(solution)/shard_map/ppermute | solution.py:599
  17.8 11.5 %copy-start.4 = (f32[4,360,31]{1,0,2:T(4,128)S(1)}, f32[4,360,31]{1,0,2:T(4,128)}, u32[]{:S(2)}) copy-start(f32[4,360,31]{1,0,2:T(4,128)} %param.11) | copy-start | bytes 535684
  29.6 7.2 %collective-permute-start.15 = (f32[16,8,384]{2,1,0:T(8,128)S(1)}, f32[16,8,384]{2,1,0:T(8,128)S(1)}, u32[]{:S(2)}, u32[]{:S(2)}) collective-permute-start(f32[16,8,384]{2,1,0:T(8,128)S(1)} %shard_map.89.refs_0_), channel_id=1, source_target_pairs={{0,24},{8,16},{16,8},{24,0},{1,25},{9,17},{17,9},{25,1},{2,26},{10... | collective-permute-start | bytes 589832 | tf_op jit(solution)/shard_map/ppermute | solution.py:599
  29.8 8.5 %collective-permute-start.14 = (f32[16,8,384]{2,1,0:T(8,128)S(1)}, f32[16,8,384]{2,1,0:T(8,128)S(1)}, u32[]{:S(2)}, u32[]{:S(2)}) collective-permute-start(f32[16,8,384]{2,1,0:T(8,128)S(1)} %shard_map.89.refs_0_), channel_id=1, source_target_pairs={{0,16},{8,24},{16,0},{24,8},{1,17},{9,25},{17,1},{25,9},{2,18},{10... | collective-permute-start | bytes 589832 | tf_op jit(solution)/shard_map/ppermute | solution.py:599
  32.5 7.8 %collective-permute-start.13 = (f32[16,8,384]{2,1,0:T(8,128)S(1)}, f32[16,8,384]{2,1,0:T(8,128)S(1)}, u32[]{:S(2)}, u32[]{:S(2)}) collective-permute-start(f32[16,8,384]{2,1,0:T(8,128)S(1)} %shard_map.89.refs_0_), channel_id=1, source_target_pairs={{0,8},{8,0},{16,24},{24,16},{1,9},{9,1},{17,25},{25,17},{2,10},{10... | collective-permute-start | bytes 589832 | tf_op jit(solution)/shard_map/ppermute | solution.py:599
  33.2 17.3 %collective-permute-start.8 = (f32[3,16,8,384]{3,2,1,0:T(8,128)S(1)}, f32[3,16,8,384]{3,2,1,0:T(8,128)S(1)}, u32[]{:S(2)}, u32[]{:S(2)}) collective-permute-start(f32[3,16,8,384]{3,2,1,0:T(8,128)S(1)} %get-tuple-element.35), channel_id=1, source_target_pairs={{1,2},{2,1},{3,4},{4,3},{5,6},{6,5},{9,10},{10,9},{11,12},{12,11},... | collective-permute-start | bytes 1769480 | tf_op jit(solution)/shard_map/ppermute | solution.py:581
  35.1 15.4 %collective-permute-start.9 = (f32[3,16,8,384]{3,2,1,0:T(8,128)S(1)}, f32[3,16,8,384]{3,2,1,0:T(8,128)S(1)}, u32[]{:S(2)}, u32[]{:S(2)}) collective-permute-start(f32[3,16,8,384]{3,2,1,0:T(8,128)S(1)} %get-tuple-element.36), channel_id=1, source_target_pairs={{0,1},{1,0},{2,3},{3,2},{4,5},{5,4},{6,7},{7,6},{8,9},{9,8},{10,11... | collective-permute-start | bytes 1769480 | tf_op jit(solution)/shard_map/ppermute | solution.py:582
  36.8 15.2 %collective-permute-start.7 = (f32[3,16,8,384]{3,2,1,0:T(8,128)S(1)}, f32[3,16,8,384]{3,2,1,0:T(8,128)S(1)}, u32[]{:S(2)}, u32[]{:S(2)}) collective-permute-start(f32[3,16,8,384]{3,2,1,0:T(8,128)S(1)} %get-tuple-element.34), channel_id=1, source_target_pairs={{0,1},{1,0},{2,3},{3,2},{4,5},{5,4},{6,7},{7,6},{8,9},{9,8},{10,11... | collective-permute-start | bytes 1769480 | tf_op jit(solution)/shard_map/ppermute | solution.py:582
  38.4 13.7 %collective-permute-start.6 = (f32[3,16,8,384]{3,2,1,0:T(8,128)S(1)}, f32[3,16,8,384]{3,2,1,0:T(8,128)S(1)}, u32[]{:S(2)}, u32[]{:S(2)}) collective-permute-start(f32[3,16,8,384]{3,2,1,0:T(8,128)S(1)} %get-tuple-element.33.refs_0_), channel_id=1, source_target_pairs={{1,2},{2,1},{3,4},{4,3},{5,6},{6,5},{9,10},{10,9},{11,12},{12,11},... | collective-permute-start | bytes 1769480 | tf_op jit(solution)/shard_map/ppermute | solution.py:581
  40.3 7.2 %collective-permute-start.10 = (f32[4,4,8,384]{3,2,1,0:T(8,128)S(1)}, f32[4,4,8,384]{3,2,1,0:T(8,128)S(1)}, u32[]{:S(2)}, u32[]{:S(2)}) collective-permute-start(f32[4,4,8,384]{3,2,1,0:T(8,128)S(1)} %shard_map.87.refs_0_), channel_id=1, source_target_pairs={{0,8},{8,0},{16,24},{24,16},{1,9},{9,1},{17,25},{25,17},{2,10},{10... | collective-permute-start | bytes 589832 | tf_op jit(solution)/shard_map/ppermute | solution.py:599
  56.4 11.2 %collective-permute-start.16 = (f32[3,16,8,384]{3,2,1,0:T(8,128)S(1)}, f32[3,16,8,384]{3,2,1,0:T(8,128)S(1)}, u32[]{:S(2)}, u32[]{:S(2)}) collective-permute-start(f32[3,16,8,384]{3,2,1,0:T(8,128)S(1)} %get-tuple-element.43), channel_id=1, source_target_pairs={{1,2},{2,1},{3,4},{4,3},{5,6},{6,5},{9,10},{10,9},{11,12},{12,11},... | collective-permute-start | bytes 1769480 | tf_op jit(solution)/shard_map/ppermute | solution.py:581
  59.7 8.0 %collective-permute-start.17 = (f32[3,16,8,384]{3,2,1,0:T(8,128)S(1)}, f32[3,16,8,384]{3,2,1,0:T(8,128)S(1)}, u32[]{:S(2)}, u32[]{:S(2)}) collective-permute-start(f32[3,16,8,384]{3,2,1,0:T(8,128)S(1)} %get-tuple-element.44), channel_id=1, source_target_pairs={{0,1},{1,0},{2,3},{3,2},{4,5},{5,4},{6,7},{7,6},{8,9},{9,8},{10,11... | collective-permute-start | bytes 1769480 | tf_op jit(solution)/shard_map/ppermute | solution.py:582
  71.1 7.8 %collective-permute-start.18 = (f32[4,4,8,384]{3,2,1,0:T(8,128)S(1)}, f32[4,4,8,384]{3,2,1,0:T(8,128)S(1)}, u32[]{:S(2)}, u32[]{:S(2)}) collective-permute-start(f32[4,4,8,384]{3,2,1,0:T(8,128)S(1)} %get-tuple-element.46), channel_id=1, source_target_pairs={{0,8},{8,0},{16,24},{24,16},{1,9},{9,1},{17,25},{25,17},{2,10},{10... | collective-permute-start | bytes 589832 | tf_op jit(solution)/shard_map/ppermute | solution.py:599
  72.6 11.5 %collective-permute-start.19 = (f32[4,4,8,384]{3,2,1,0:T(8,128)S(1)}, f32[4,4,8,384]{3,2,1,0:T(8,128)S(1)}, u32[]{:S(2)}, u32[]{:S(2)}) collective-permute-start(f32[4,4,8,384]{3,2,1,0:T(8,128)S(1)} %get-tuple-element.47), channel_id=1, source_target_pairs={{0,16},{8,24},{16,0},{24,8},{1,17},{9,25},{17,1},{25,9},{2,18},{10... | collective-permute-start | bytes 589832 | tf_op jit(solution)/shard_map/ppermute | solution.py:599
  73.4 10.7 %collective-permute-start.20 = (f32[4,4,8,384]{3,2,1,0:T(8,128)S(1)}, f32[4,4,8,384]{3,2,1,0:T(8,128)S(1)}, u32[]{:S(2)}, u32[]{:S(2)}) collective-permute-start(f32[4,4,8,384]{3,2,1,0:T(8,128)S(1)} %get-tuple-element.48), channel_id=1, source_target_pairs={{0,24},{8,16},{16,8},{24,0},{1,25},{9,17},{17,9},{25,1},{2,26},{10... | collective-permute-start | bytes 589832 | tf_op jit(solution)/shard_map/ppermute | solution.py:599

commit v3 on v2

--- a/solution.py
+++ b/solution.py
@@ -13,7 +13,9 @@
 SUBSTEPS = 2
 QUARTERS = 4
 HALO = 3
-MIDDLE_ROOM = 24
+MIDDLE_ROOM = 16
+PACK_US = 0.5
+FILTER_US = 2.5
 SUB = 8
 f32 = jnp.float32
 bf16 = jnp.bfloat16
@@ -68,6 +70,29 @@
         store(level, g, below * g, h)
         h_before = h
         below = above
+
+
+def column_rest(h):
+    n = len(h)
+    before = lambda x: [pltpu.roll(x[n - 1], 1, 0)] + x[: n - 1]
+    ratio = before(h)
+    s = [jnp.ones(h[0].shape, f32)]
+    carry = [ratio[0]]
+    for q in range(1, n):
+        s.append(1.0 + ratio[q] * s[q - 1])
+        carry.append(ratio[q] * carry[q - 1])
+    z, p = s[n - 1], carry[n - 1]
+    step = 1
+    while step < SUB:
+        z = z + p * pltpu.roll(z, step, 0)
+        if 2 * step < SUB:
+            p = p * pltpu.roll(p, step, 0)
+        step *= 2
+    start = pltpu.roll(z, 1, 0)
+    s = [s[q] + carry[q] * start for q in range(n - 1)] + [z]
+    g = [(1.0 - h[q]) / s[q] for q in range(n)]
+    mixing = before([h[q] * s[q] / (1.0 - h[q]) for q in range(n)])
+    return g, [mixing[q] * g[q] for q in range(n)]
 
 
 def column_solve(v, g, a, h):
@@ -135,17 +160,18 @@
     return [(wide // 128, rows * levels, 128)] * 3
 
 
-def first_solve_kernel(tiles, direct, tracers, *refs):
-    sens, mix = refs[-(9 + tracers) : -(7 + tracers)]
-    outs = refs[-(7 + tracers) : -7]
-    turned, g_s, a_s, h_s, sens_v, mix_v, sems = refs[-7:]
+def first_solve_kernel(tiles, direct, sens, mix, north, *refs):
     rows, width, channels = sens.shape
     levels = mix.shape[0] + 1
-    loads = [pltpu.make_async_copy(mix, mix_v, sems.at[rows])]
+    tracers = channels // levels
+    outs, h_out = refs[:tracers], refs[tracers]
+    turned, packed, g_s, a_s, h_s, sens_v, mix_v, north_v, sems = refs[tracers + 1 :]
+    loads = [pltpu.make_async_copy(mix, mix_v, sems.at[2 * rows])]
     loads += [pltpu.make_async_copy(sens.at[r], sens_v.at[r], sems.at[r]) for r in range(rows)]
+    loads += [pltpu.make_async_copy(north.at[r], north_v.at[r], sems.at[rows + r]) for r in range(rows)]
     for load in loads:
         load.start()
-    clear(turned, g_s, a_s, h_s)
+    clear(turned, packed, g_s, a_s, h_s)
     loads[0].wait()
 
     def store(level, g, a, h):
@@ -155,19 +181,28 @@
 
     column_factors(lambda l: mix_v[l], levels, (rows, width), store)
     for r in range(rows):
-        loads[r + 1].wait()
+        loads[1 + r].wait()
         put(turned, slice(0, channels), sens_v[r].T)
         at = lambda q: slice(r * levels + q * SUB, r * levels + q * SUB + SUB)
         g, a, h = ([get(s, at(q)) for q in range(tiles)] for s in (g_s, a_s, h_s))
+        for q in range(tiles):
+            h_out[r, q] = h[q]
         for j in range(tracers):
             t = order_of(j, direct)
             v = [get(turned, pl.ds(q * tracers + t, SUB, stride=tiles * tracers)) for q in range(tiles)]
             x = column_solve(v, g, a, h)
             for q in range(tiles):
                 outs[j][r, q] = x[q]
-
-
-def pack_levels_kernel(tiles, *refs):
+    for r in range(rows):
+        loads[1 + rows + r].wait()
+        put(packed, slice(r * levels, (r + 1) * levels), north_v[r])
+        for q in range(tiles):
+            value = get(packed, pl.ds(r * levels + q, SUB, stride=tiles))
+            for j in range(tracers):
+                outs[j][rows + r, q] = value
+
+
+def pack_both_kernel(tiles, h, *refs):
     src, out, src_v, turned, sems = refs[-5:]
     rows, levels, width = src.shape
     loads = [pltpu.make_async_copy(src.at[r], src_v.at[r], sems.at[r]) for r in range(rows)]
@@ -175,23 +210,13 @@
         load.start()
     clear(turned)
     for r in range(rows):
+        for q in range(tiles):
+            out[1, r * tiles + q] = h[r, q]
+    for r in range(rows):
         loads[r].wait()
         put(turned, slice(r * levels, (r + 1) * levels), src_v[r])
         for q in range(tiles):
-            out[r, q] = get(turned, pl.ds(r * levels + q, SUB, stride=tiles))
-
-
-def pack_mixing_kernel(*refs):
-    mix, out, mix_v, sem = refs[-4:]
-    rows, width = mix.shape[1:]
-    load = pltpu.make_async_copy(mix, mix_v, sem)
-    load.start()
-    out[...] = jnp.zeros(out.shape, f32)
-    load.wait()
-    per = SUB // rows
-    for level in range(mix.shape[0]):
-        at = level % per * rows
-        out[level // per, at : at + rows, :width] = mix_v[level]
+            out[0, r * tiles + q] = get(turned, pl.ds(r * levels + q, SUB, stride=tiles))
 
 
 def unpack_kernel(tiles, direct, *refs):
@@ -269,14 +294,14 @@
     def _():
         out[...] = field[...]
 
-    write_edges(out, edge_z, edge_c)
-
-
-def write_edges(field, edge_z, edge_c):
+    write_edges(out, edge_z, edge_c, 0)
+
+
+def write_edges(field, edge_z, edge_c, at):
     shift = field.shape[0] - HALO
     odd = at_odd()
-    edge_z[...] = field[pl.ds(odd * shift, HALO)]
-    edge_c[...] = field[pl.ds((1 - odd) * shift, HALO)]
+    edge_z[at : at + HALO] = field[pl.ds(odd * shift, HALO)]
+    edge_c[at : at + HALO] = field[pl.ds((1 - odd) * shift, HALO)]
 
 
 def by_parity(from_z, from_c, body):
@@ -347,7 +372,7 @@
             before = now
         return 0
 
-    lax.fori_loop(0, groups, body, 0)
+    lax.fori_loop(0, groups, body, 0, unroll=2)
 
 
 def meridional_pass(field, before, after, north, out):
@@ -368,7 +393,7 @@
             out[r, i] = total[r]
         return 0
 
-    lax.fori_loop(0, groups, body, 0)
+    lax.fori_loop(0, groups, body, 0, unroll=2)
 
 
 def pole_pass(field, ghosts, out):
@@ -389,7 +414,7 @@
                 out[second, i] = out[second, i] + ghosts[2, j] * near
                 return 0
 
-            lax.fori_loop(0, groups, body, 0)
+            lax.fori_loop(0, groups, body, 0, unroll=2)
 
 
 def widen(values, width):
@@ -424,7 +449,7 @@
             emit(r, q, tile, total)
         return 0
 
-    lax.fori_loop(0, rows * tiles, body, 0)
+    lax.fori_loop(0, rows * tiles, body, 0, unroll=2)
 
 
 def east_factors(width, courant, out):
@@ -440,7 +465,7 @@
                 out[m + HALO, r, q * tiles + tile] = stencil(w.get(1 - m), w.get(-m), m)
         return 0
 
-    lax.fori_loop(0, rows * tiles, body, 0)
+    lax.fori_loop(0, rows * tiles, body, 0, unroll=2)
 
 
 def solve_pass(field, g, a, h):
@@ -455,7 +480,7 @@
             field[r, q * tiles + tile] = x[tile]
         return 0
 
-    lax.fori_loop(0, rows * QUARTERS, body, 0)
+    lax.fori_loop(0, rows * QUARTERS, body, 0, unroll=2)
 
 
 def place(pieces, tiles, direct, out):
@@ -465,26 +490,24 @@
 
 def first_filter_kernel(tiles, direct, count, *refs):
     pieces, tables = refs[:4], refs[4:6]
-    cutoff, polar_flag, out, edge_z, edge_c, field, cut_s, flag_s, sems = refs[-9:]
+    cutoff, polar_flag, out, north, edge_z, edge_c, field, cut_s, flag_s, sems = refs[-10:]
+    rows = field.shape[0]
     loads = load_settings(cutoff, polar_flag, cut_s, flag_s, sems)
-    place(pieces, tiles, direct, field)
+    for j in range(QUARTERS):
+        at = pl.ds(order_of(j, direct) * tiles, tiles)
+        field[:, at] = pieces[j][:rows]
+        north[:, at] = pieces[j][rows:]
+
+    @pl.when(at_end(1))
+    def _():
+        north[rows - 1] = jnp.zeros(north.shape[1:], f32)
+
+    write_edges(north, edge_z, edge_c, HALO)
     for load in loads:
         load.wait()
     filter_and_edges(count, field, tables, cut_s, flag_s, out, edge_z, edge_c)
 
 
-def north_kernel(tiles, direct, *refs):
-    pieces = refs[:4]
-    out, edge_z, edge_c = refs[-3:]
-    place(pieces, tiles, direct, out)
-
-    @pl.when(at_end(1))
-    def _():
-        out[out.shape[0] - 1] = jnp.zeros(out.shape[1:], f32)
-
-    write_edges(out, edge_z, edge_c)
-
-
 def north_factor_kernel(north, from_z, from_c, *refs):
     out, ghosts = refs[-2:]
     rows = north.shape[0]
@@ -492,8 +515,8 @@
     def body(before, after):
         def courant(g, i):
             if g < 0:
-                return before[g + HALO, i]
-            return north[g, i] if g < rows else after[g - rows, i]
+                return before[HALO + g + HALO, i]
+            return north[g, i] if g < rows else after[HALO + g - rows, i]
 
         north_factors(courant, ghosts, out)
 
@@ -501,29 +524,30 @@
 
 
 def east_factor_kernel(tiles, direct, width, *refs):
-    pieces, out, raw = refs[:4], refs[4], refs[5]
-    place(pieces, tiles, direct, raw)
+    pieces, out, raw = refs[:4], refs[-2], refs[-1]
+    for j in range(QUARTERS):
+        at = pl.ds(order_of(j, direct) * tiles, tiles)
+        for r in range(raw.shape[0]):
+            raw[r, at] = pieces[j][0, r * tiles : (r + 1) * tiles]
     east_factors(width, raw, out)
 
 
 def column_factor_kernel(tiles, direct, *refs):
     pieces = refs[:4]
-    g_o, a_o, h_o, g_s, a_s, h_s = refs[4:]
-    rows, groups, sub, wide = g_o.shape
-    levels = tiles * sub
-    per = SUB // rows
-    for j in range(QUARTERS):
-
-        def store(level, g, a, h):
-            at = (level % tiles) * SUB + level // tiles
-            for s, value in ((g_s, g), (a_s, a), (h_s, h)):
-                put(s, pl.ds(at, rows, stride=levels), value)
-
-        mix_at = lambda l: pieces[j][l // per, l % per * rows : l % per * rows + rows, :]
-        column_factors(mix_at, levels, (rows, wide), store)
-        for s, o in ((g_s, g_o), (a_s, a_o), (h_s, h_o)):
-            value = get(s, slice(0, rows * levels)).reshape(rows, tiles, sub, wide)
-            o[:, pl.ds(order_of(j, direct) * tiles, tiles)] = value
+    g_o, a_o, h_o = refs[-3:]
+
+    def body(r, _):
+        for j in range(QUARTERS):
+            h = [pieces[j][1, r * tiles + q] for q in range(tiles)]
+            g, a = column_rest(h)
+            for q in range(tiles):
+                at = order_of(j, direct) * tiles + q
+                g_o[r, at] = g[q]
+                a_o[r, at] = a[q]
+                h_o[r, at] = h[q]
+        return 0
+
+    lax.fori_loop(0, g_o.shape[0], body, 0)
 
 
 def advect(width, field, from_z, from_c, north, ghosts, east, work, emit):
@@ -564,6 +588,7 @@
 def call(kernel, outs, scratch, *args, us=1.0, room=16, outside=()):
     specs = [pl.BlockSpec(memory_space=pltpu.VMEM)] * len(args)
     specs += [pl.BlockSpec(memory_space=pltpu.HBM)] * len(outside)
+    outside = [pltpu.with_memory_space_constraint(x, pltpu.HBM) for x in outside]
     return pl.pallas_call(
         kernel,
         out_shape=[jax.ShapeDtypeStruct(s, f32) if isinstance(s, tuple) else s for s in outs],
@@ -632,51 +657,47 @@
     edge = (HALO,) + full[1:]
     turned = (piece // 128, rows * levels, 128)
 
-    def pack(x, *after):
-        scratch = [x.shape, turned, pltpu.SemaphoreType.DMA((rows,))]
-        return call(partial(pack_levels_kernel, tiles), [block], scratch, *after, outside=[x], us=0.4)[0]
-
-    north_piece = pack(north_t)
-    north_pieces = gather(north_piece)
-    ys = call(
-        partial(first_solve_kernel, tiles, direct, tracers),
-        [block] * tracers,
-        [(piece // 128, channels, 128)]
+    *ys, h_piece = call(
+        partial(first_solve_kernel, tiles, direct),
+        [(2 * rows,) + block[1:]] * tracers + [block],
+        [(piece // 128, channels, 128), turned]
         + factor_scratch(rows, levels, piece)
-        + [sensitivity.shape, mix_t.shape, pltpu.SemaphoreType.DMA((rows + 1,))],
-        north_piece,
-        outside=[sensitivity, mix_t],
+        + [sensitivity.shape, mix_t.shape, north_t.shape, pltpu.SemaphoreType.DMA((2 * rows + 1,))],
+        outside=[sensitivity, mix_t, north_t],
         us=3.0,
     )
     pieces = to_tracers(ys)
-    north, north_z, north_c = call(partial(north_kernel, tiles, direct), [full, edge, edge], [], *north_pieces, ys[0])
-    north_z, north_c = lat_exchange(north_z, north_c)
-    east_pieces = gather(pack(east_t, *north_pieces[1:]))
-    state, edge_z, edge_c = call(
+    (both,) = call(
+        partial(pack_both_kernel, tiles),
+        [(2, rows * tiles, SUB, piece)],
+        [east_t.shape, turned, pltpu.SemaphoreType.DMA((rows,))],
+        h_piece, *pieces[1:],
+        outside=[east_t],
+        us=PACK_US,
+    )
+    both_pieces = gather(both)
+    both_edge = (2 * HALO,) + full[1:]
+    state, north, edge_z, edge_c = call(
         partial(first_filter_kernel, tiles, direct, quarter),
-        [full, edge, edge],
+        [full, full, both_edge, both_edge],
         [full] + settings_scratch(rows),
-        *pieces, *tables, north,
-        us=2.5,
+        *pieces, *tables, both,
+        us=FILTER_US,
         outside=[cutoff, polar_flag],
     )
-    (mix_piece,) = call(
-        pack_mixing_kernel,
-        [(rows * tiles, SUB, piece)],
-        [mix_t.shape, pltpu.SemaphoreType.DMA(())],
-        edge_z,
-        outside=[mix_t],
-    )
-    mix_pieces = gather(mix_piece)
     edges = lat_exchange(edge_z, edge_c)
+    (east,) = call(
+        partial(east_factor_kernel, tiles, direct, quarter), [(2 * HALO + 1,) + full], [full], *both_pieces, us=10.0
+    )
+    g, a, h = call(
+        partial(column_factor_kernel, tiles, direct),
+        [full] * 3,
+        [],
+        *both_pieces,
+        us=10.0,
+    )
     north, ghosts = call(
-        north_factor_kernel, [(2 * HALO + 1,) + full, (3,) + full[1:]], [], north, north_z, north_c, edge_z
-    )
-    (east,) = call(
-        partial(east_factor_kernel, tiles, direct, quarter), [(2 * HALO + 1,) + full], [full], *east_pieces, us=3.0
-    )
-    g, a, h = call(
-        partial(column_factor_kernel, tiles, direct), [full] * 3, factor_scratch(rows, levels, wide), *mix_pieces, us=2.2
+        north_factor_kernel, [(2 * HALO + 1,) + full, (3,) + full[1:]], [], north, *edges, us=1.5
     )
     for substep in range(SUBSTEPS - 1):
         state, edge_z, edge_c = call(

time: 85.8 us -> 80.4 us (0.937)
  waiting for transfers between devices: 33.6 us -> 43.8 us
  starting transfers between devices: 28.1 us -> 18.5 us
  Pallas kernels: 20.7 us -> 17.4 us
  local copies, waits for them, and re-layouts: 2.99 us -> 0.01 us
    ppermute x15 -> x9, waiting for transfers between devices: 26.1 us -> 36.3 us  [on_device(): lax.ppermute(x, 'lon', [(i, i ^ s) for i in range(parts)])]
    ppermute x15 -> x9, starting transfers between devices: 18.7 us -> 10.7 us  [on_device(): lax.ppermute(x, 'lon', [(i, i ^ s) for i in range(parts)])]
    pallas_call x12 -> x9, Pallas kernels: 20.7 us -> 17.4 us  [call(): pl.pallas_call(kernel, out_shape=[jax.ShapeDtypeStruct(s, f32) if isinsta...]
    unnamed x18 -> x4, local copies, waits for them, and re-layouts: 2.99 us -> 0.01 us
    ppermute x3 -> x2, starting transfers between devices: 7.03 us -> 6.11 us  [lat_exchange(): from_z = lax.ppermute(edge_z, 'lat', pairs(1))]
    ppermute x3 -> x2, starting transfers between devices: 2.28 us -> 1.73 us  [lat_exchange(): from_c = lax.ppermute(edge_c, 'lat', pairs(0))]
    ppermute x3 -> x2, waiting for transfers between devices: 7.53 us -> 7.48 us  [lat_exchange(): from_z = lax.ppermute(edge_z, 'lat', pairs(1))]
  transfers between devices with their start and end apart: 21 -> 13, of which waited for: 8 -> 8; matrix products, arithmetic and copies ran while one was open for 0% -> 0% of each run, Pallas kernels for 13% -> 5%
where the time goes in v3:
time: 80.4 us; the launch traced here: 79.8 us
  waiting for transfers between devices  43.8 us (54%)
  starting transfers between devices  18.5 us (23%)
  Pallas kernels  17.4 us (22%)
    ppermute x9, waiting for transfers between devices, on_device(): lax.ppermute(x, 'lon', [(i, i ^ s) for i in range(parts)])  36.3 us
    pallas_call x9, Pallas kernels, call(): pl.pallas_call(kernel, out_shape=[jax.ShapeDtypeStruct(s, f32) if isinsta...  17.4 us
    ppermute x9, starting transfers between devices, on_device(): lax.ppermute(x, 'lon', [(i, i ^ s) for i in range(parts)])  10.7 us
    ppermute x2, waiting for transfers between devices, lat_exchange(): from_z = lax.ppermute(edge_z, 'lat', pairs(1))  7.48 us
    ppermute x2, starting transfers between devices, lat_exchange(): from_z = lax.ppermute(edge_z, 'lat', pairs(1))  6.11 us
    ppermute x2, starting transfers between devices, lat_exchange(): from_c = lax.ppermute(edge_c, 'lat', pairs(0))  1.73 us
  transfers between devices with their start and end apart: 13, of which 8 were waited for; matrix products, arithmetic and copies ran while one was open for 0% of the time, Pallas kernels for 5%

profile of v3, /device:TPU:8, one launch (start us, length us, event | category | flops | bytes accessed | tf_op | source)
XLA Modules:
  0.0 79.8 jit_solution(777752995072990259)
XLA Ops:
  0.0 0.0 copy-start.1
  0.0 2.8 %shard_map.82 = (f32[8,4,8,384]{3,2,1,0:T(8,128)S(1)}, f32[8,4,8,384]{3,2,1,0:T(8,128)S(1)}, f32[8,4,8,384]{3,2,1,0:T(8,128)S(1)}, f32[8,4,8,384]{3,2,1,0:T(8,128)S(1)}, f32[4,4,8,384]{3,2,1,0:T(8,128)S(1)}) custom-call(f32[4,360,128]{2,1,0:T(8,128)} %sens.1, f32[31,4,360]{2,1,0:T(4,128)} %bitcast.5, f32[4,32,360]{2,1,0:T(8,128)} %bitcast.4), custom_call_target="tpu_custom_call" | custom-call | flops 3000000000 | bytes 100000 | tf_op jit(solution)/shard_map/pallas_call | solution.py:592
  2.8 0.0 copy-start
  2.8 1.6 %collective-permute-start = (f32[8,4,8,384]{3,2,1,0:T(8,128)S(1)}, f32[8,4,8,384]{3,2,1,0:T(8,128)S(1)}, u32[]{:S(2)}, u32[]{:S(2)}) collective-permute-start(f32[8,4,8,384]{3,2,1,0:T(8,128)S(1)} %get-tuple-element.27), channel_id=1, source_target_pairs={{0,8},{8,0},{16,24},{24,16},{1,9},{9,1},{17,25},{25,17},{2,10},{10... | collective-permute-start | bytes 1179656 | tf_op jit(solution)/shard_map/ppermute | solution.py:624
  4.4 1.5 %collective-permute-start.1 = (f32[8,4,8,384]{3,2,1,0:T(8,128)S(1)}, f32[8,4,8,384]{3,2,1,0:T(8,128)S(1)}, u32[]{:S(2)}, u32[]{:S(2)}) collective-permute-start(f32[8,4,8,384]{3,2,1,0:T(8,128)S(1)} %get-tuple-element.28), channel_id=1, source_target_pairs={{0,16},{8,24},{16,0},{24,8},{1,17},{9,25},{17,1},{25,9},{2,18},{10... | collective-permute-start | bytes 1179656 | tf_op jit(solution)/shard_map/ppermute | solution.py:624
  5.9 0.5 collective-permute-start.2
  6.4 8.5 %collective-permute-done.refs_0_.refs_1_ = f32[8,4,8,384]{3,2,1,0:T(8,128)S(1)} collective-permute-done((f32[8,4,8,384]{3,2,1,0:T(8,128)S(1)}, f32[8,4,8,384]{3,2,1,0:T(8,128)S(1)}, u32[]{:S(2)}, u32[]{:S(2)}) %collective-permute-start) | collective-permute-done | bytes 393248 | tf_op jit(solution)/shard_map/ppermute | solution.py:624
  14.9 8.5 %collective-permute-done.1.refs_1_.refs_2_ = f32[8,4,8,384]{3,2,1,0:T(8,128)S(1)} collective-permute-done((f32[8,4,8,384]{3,2,1,0:T(8,128)S(1)}, f32[8,4,8,384]{3,2,1,0:T(8,128)S(1)}, u32[]{:S(2)}, u32[]{:S(2)}) %collective-permute-start.1) | collective-permute-done | bytes 393248 | tf_op jit(solution)/shard_map/ppermute | solution.py:624
  23.4 0.0 collective-permute-done.2.refs_2_.refs_3_
  23.4 0.9 %shard_map.83.refs_6_.refs_0_ = f32[2,16,8,384]{3,2,1,0:T(8,128)S(1)} custom-call(f32[4,4,8,384]{3,2,1,0:T(8,128)S(1)} %get-tuple-element.30.h, f32[8,4,8,384]{3,2,1,0:T(8,128)S(1)} %collective-permute-done.refs_0_.refs_1_, f32[8,4,8,384]{3,2,1,0:T(8,128)S(1)} %collective-permute-done.1.refs_1_.refs_2_, ...), custom_call_target="tpu_custom_call" | custom-call | flops 500000000 | bytes 100000 | tf_op jit(solution)/shard_map/pallas_call | solution.py:592
  24.3 1.6 %collective-permute-start.7 = (f32[2,16,8,384]{3,2,1,0:T(8,128)S(1)}, f32[2,16,8,384]{3,2,1,0:T(8,128)S(1)}, u32[]{:S(2)}, u32[]{:S(2)}) collective-permute-start(f32[2,16,8,384]{3,2,1,0:T(8,128)S(1)} %shard_map.83.refs_6_.refs_0_), channel_id=1, source_target_pairs={{0,24},{8,16},{16,8},{24,0},{1,25},{9,17},{17,9},{25,1},{2,26},{10... | collective-permute-start | bytes 1179656 | tf_op jit(solution)/shard_map/ppermute | solution.py:624
  25.9 1.2 %collective-permute-start.6 = (f32[2,16,8,384]{3,2,1,0:T(8,128)S(1)}, f32[2,16,8,384]{3,2,1,0:T(8,128)S(1)}, u32[]{:S(2)}, u32[]{:S(2)}) collective-permute-start(f32[2,16,8,384]{3,2,1,0:T(8,128)S(1)} %shard_map.83.refs_6_.refs_0_), channel_id=1, source_target_pairs={{0,16},{8,24},{16,0},{24,8},{1,17},{9,25},{17,1},{25,9},{2,18},{10... | collective-permute-start | bytes 1179656 | tf_op jit(solution)/shard_map/ppermute | solution.py:624
  27.1 0.8 collective-permute-start.5
  27.9 0.0 copy-done.1
  27.9 0.0 copy-done
  27.9 0.8 %shard_map.84 = (f32[4,16,8,384]{3,2,1,0:T(8,128)S(1)}, f32[4,16,8,384]{3,2,1,0:T(8,128)S(1)}, f32[6,16,8,384]{3,2,1,0:T(8,128)S(1)}, f32[6,16,8,384]{3,2,1,0:T(8,128)S(1)}) custom-call(f32[8,4,8,384]{3,2,1,0:T(8,128)S(1)} %get-tuple-element.26.refs_0_, f32[8,4,8,384]{3,2,1,0:T(8,128)S(1)} %collective-permute-done.refs_0_.refs_1_, ...), custom_call_target="tpu_custom_call" | custom-call | flops 2500000000 | bytes 100000 | tf_op jit(solution)/shard_map/pallas_call | solution.py:592
  28.7 2.0 %collective-permute-start.3 = (f32[6,16,8,384]{3,2,1,0:T(8,128)S(1)}, f32[6,16,8,384]{3,2,1,0:T(8,128)S(1)}, u32[]{:S(2)}, u32[]{:S(2)}) collective-permute-start(f32[6,16,8,384]{3,2,1,0:T(8,128)S(1)} %get-tuple-element.32), channel_id=1, source_target_pairs={{1,2},{2,1},{3,4},{4,3},{5,6},{6,5},{9,10},{10,9},{11,12},{12,11},... | collective-permute-start | bytes 3538952 | tf_op jit(solution)/shard_map/ppermute | solution.py:606
  30.7 1.7 %collective-permute-start.4 = (f32[6,16,8,384]{3,2,1,0:T(8,128)S(1)}, f32[6,16,8,384]{3,2,1,0:T(8,128)S(1)}, u32[]{:S(2)}, u32[]{:S(2)}) collective-permute-start(f32[6,16,8,384]{3,2,1,0:T(8,128)S(1)} %get-tuple-element.33), channel_id=1, source_target_pairs={{0,1},{1,0},{2,3},{3,2},{4,5},{5,4},{6,7},{7,6},{8,9},{9,8},{10,11... | collective-permute-start | bytes 3538952 | tf_op jit(solution)/shard_map/ppermute | solution.py:607
  32.4 4.9 %collective-permute-done.7.refs_3_ = f32[2,16,8,384]{3,2,1,0:T(8,128)S(1)} collective-permute-done((f32[2,16,8,384]{3,2,1,0:T(8,128)S(1)}, f32[2,16,8,384]{3,2,1,0:T(8,128)S(1)}, u32[]{:S(2)}, u32[]{:S(2)}) %collective-permute-start.7) | collective-permute-done | bytes 393248 | tf_op jit(solution)/shard_map/ppermute | solution.py:624
  37.4 6.1 %collective-permute-done.6.refs_2_ = f32[2,16,8,384]{3,2,1,0:T(8,128)S(1)} collective-permute-done((f32[2,16,8,384]{3,2,1,0:T(8,128)S(1)}, f32[2,16,8,384]{3,2,1,0:T(8,128)S(1)}, u32[]{:S(2)}, u32[]{:S(2)}) %collective-permute-start.6) | collective-permute-done | bytes 393248 | tf_op jit(solution)/shard_map/ppermute | solution.py:624
  43.5 0.0 collective-permute-done.5.refs_1_
  43.5 0.5 shard_map.87
  44.0 2.4 %shard_map.86.east = f32[7,4,16,8,384]{4,3,2,1,0:T(8,128)S(1)} custom-call(f32[2,16,8,384]{3,2,1,0:T(8,128)S(1)} %shard_map.83.refs_6_.refs_0_, f32[2,16,8,384]{3,2,1,0:T(8,128)S(1)} %collective-permute-done.5.refs_1_, f32[2,16,8,384]{3,2,1,0:T(8,128)S(1)} %collective-permute-done.6.refs_2_, f32[2,16,8,384]{3,2,1,0:T(8,128)S(1)} %collective-permute-done.7.refs_3_), custom_call_target="tpu_custom_call" | custom-call | flops 10000000000 | bytes 100000 | tf_op jit(solution)/shard_map/pallas_call | solution.py:592
  46.4 0.0 collective-permute-done.3.from_z
  46.5 0.0 collective-permute-done.4.from_c
  46.5 1.5 %shard_map.85 = (f32[7,4,16,8,384]{4,3,2,1,0:T(8,128)S(1)}, f32[3,16,8,384]{3,2,1,0:T(8,128)S(1)}) custom-call(f32[4,16,8,384]{3,2,1,0:T(8,128)S(1)} %get-tuple-element.34.north, f32[6,16,8,384]{3,2,1,0:T(8,128)S(1)} %collective-permute-done.3.from_z, f32[6,16,8,384]{3,2,1,0:T(8,128)S(1)} %collective-permute-done.4.from_c), custom_call_target="tpu_custom_call" | custom-call | flops 1500000000 | bytes 100000 | tf_op jit(solution)/shard_map/pallas_call | solution.py:592
  48.0 3.9 %shard_map.88 = (f32[4,16,8,384]{3,2,1,0:T(8,128)S(1)}, f32[3,16,8,384]{3,2,1,0:T(8,128)S(1)}, f32[3,16,8,384]{3,2,1,0:T(8,128)S(1)}) custom-call(f32[4,16,8,384]{3,2,1,0:T(8,128)S(1)} %get-tuple-element.31.field, f32[6,16,8,384]{3,2,1,0:T(8,128)S(1)} %collective-permute-done.3.from_z, f32[6,16,8,384]{3,2,1,0:T(8,128)S(1)} %collective-permute-done.4.from_c, ...), custom_call_target="tpu_custom_call" | custom-call | flops 6000000000 | bytes 100000 | tf_op jit(solution)/shard_map/pallas_call | solution.py:592
  51.9 4.1 %collective-permute-start.8 = (f32[3,16,8,384]{3,2,1,0:T(8,128)S(1)}, f32[3,16,8,384]{3,2,1,0:T(8,128)S(1)}, u32[]{:S(2)}, u32[]{:S(2)}) collective-permute-start(f32[3,16,8,384]{3,2,1,0:T(8,128)S(1)} %get-tuple-element.41), channel_id=1, source_target_pairs={{1,2},{2,1},{3,4},{4,3},{5,6},{6,5},{9,10},{10,9},{11,12},{12,11},... | collective-permute-start | bytes 1769480 | tf_op jit(solution)/shard_map/ppermute | solution.py:606
  56.0 0.1 collective-permute-start.9
  56.1 7.5 %collective-permute-done.8.from_z = f32[3,16,8,384]{3,2,1,0:T(8,128)S(1)} collective-permute-done((f32[3,16,8,384]{3,2,1,0:T(8,128)S(1)}, f32[3,16,8,384]{3,2,1,0:T(8,128)S(1)}, u32[]{:S(2)}, u32[]{:S(2)}) %collective-permute-start.8) | collective-permute-done | bytes 589856 | tf_op jit(solution)/shard_map/ppermute | solution.py:606
  63.5 0.0 collective-permute-done.9.from_c
  63.6 3.0 %shard_map.89 = (f32[4,4,8,384]{3,2,1,0:T(8,128)S(1)}, f32[4,4,8,384]{3,2,1,0:T(8,128)S(1)}, f32[4,4,8,384]{3,2,1,0:T(8,128)S(1)}, f32[4,4,8,384]{3,2,1,0:T(8,128)S(1)}) custom-call(f32[4,16,8,384]{3,2,1,0:T(8,128)S(1)} %get-tuple-element.40.field, f32[3,16,8,384]{3,2,1,0:T(8,128)S(1)} %collective-permute-done.8.from_z, ...), custom_call_target="tpu_custom_call" | custom-call | flops 3500000000 | bytes 100000 | tf_op jit(solution)/shard_map/pallas_call | solution.py:592
  66.6 1.3 %collective-permute-start.10 = (f32[4,4,8,384]{3,2,1,0:T(8,128)S(1)}, f32[4,4,8,384]{3,2,1,0:T(8,128)S(1)}, u32[]{:S(2)}, u32[]{:S(2)}) collective-permute-start(f32[4,4,8,384]{3,2,1,0:T(8,128)S(1)} %get-tuple-element.44), channel_id=1, source_target_pairs={{0,8},{8,0},{16,24},{24,16},{1,9},{9,1},{17,25},{25,17},{2,10},{10... | collective-permute-start | bytes 589832 | tf_op jit(solution)/shard_map/ppermute | solution.py:624
  67.9 0.8 collective-permute-start.11
  68.7 1.5 %collective-permute-start.12 = (f32[4,4,8,384]{3,2,1,0:T(8,128)S(1)}, f32[4,4,8,384]{3,2,1,0:T(8,128)S(1)}, u32[]{:S(2)}, u32[]{:S(2)}) collective-permute-start(f32[4,4,8,384]{3,2,1,0:T(8,128)S(1)} %get-tuple-element.46), channel_id=1, source_target_pairs={{0,24},{8,16},{16,8},{24,0},{1,25},{9,17},{17,9},{25,1},{2,26},{10... | collective-permute-start | bytes 589832 | tf_op jit(solution)/shard_map/ppermute | solution.py:624
  70.2 4.3 %collective-permute-done.10.refs_1_ = f32[4,4,8,384]{3,2,1,0:T(8,128)S(1)} collective-permute-done((f32[4,4,8,384]{3,2,1,0:T(8,128)S(1)}, f32[4,4,8,384]{3,2,1,0:T(8,128)S(1)}, u32[]{:S(2)}, u32[]{:S(2)}) %collective-permute-start.10) | collective-permute-done | bytes 196640 | tf_op jit(solution)/shard_map/ppermute | solution.py:624
  74.5 0.6 collective-permute-done.11.refs_2_
  75.1 3.3 %collective-permute-done.12.refs_3_ = f32[4,4,8,384]{3,2,1,0:T(8,128)S(1)} collective-permute-done((f32[4,4,8,384]{3,2,1,0:T(8,128)S(1)}, f32[4,4,8,384]{3,2,1,0:T(8,128)S(1)}, u32[]{:S(2)}, u32[]{:S(2)}) %collective-permute-start.12) | collective-permute-done | bytes 196640 | tf_op jit(solution)/shard_map/ppermute | solution.py:624
  78.4 1.4 %shard_map.90 = f32[4,360,128]{2,1,0:T(8,128)} custom-call(f32[4,4,8,384]{3,2,1,0:T(8,128)S(1)} %get-tuple-element.43.refs_0_, f32[4,4,8,384]{3,2,1,0:T(8,128)S(1)} %collective-permute-done.10.refs_1_, f32[4,4,8,384]{3,2,1,0:T(8,128)S(1)} %collective-permute-done.11.refs_2_, f32[4,4,8,384]{3,2,1,0:T(8,128)S(1)} %collective-permute-done.12.refs_3_), custom_call_target="tpu_custom_call" | custom-call | flops 1000000000 | bytes 100000 | tf_op jit(solution)/shard_map/pallas_call | solution.py:592
Async XLA Ops:
  0.0 27.9 %copy-start.1 = (bf16[2,768,384]{2,1,0:T(8,128)(2,1)S(1)}, bf16[2,768,384]{2,1,0:T(8,128)(2,1)}, u32[]{:S(2)}) copy-start(bf16[2,768,384]{2,1,0:T(8,128)(2,1)} %constant.4.clone.refs_4_.refs_0_) | copy-start | bytes 3538948
  2.8 25.1 %copy-start = (bf16[2,768,384]{2,1,0:T(8,128)(2,1)S(1)}, bf16[2,768,384]{2,1,0:T(8,128)(2,1)}, u32[]{:S(2)}) copy-start(bf16[2,768,384]{2,1,0:T(8,128)(2,1)} %constant.5.clone.refs_5_.refs_1_) | copy-start | bytes 3538948
  2.8 12.1 %collective-permute-start = (f32[8,4,8,384]{3,2,1,0:T(8,128)S(1)}, f32[8,4,8,384]{3,2,1,0:T(8,128)S(1)}, u32[]{:S(2)}, u32[]{:S(2)}) collective-permute-start(f32[8,4,8,384]{3,2,1,0:T(8,128)S(1)} %get-tuple-element.27), channel_id=1, source_target_pairs={{0,8},{8,0},{16,24},{24,16},{1,9},{9,1},{17,25},{25,17},{2,10},{10... | collective-permute-start | bytes 1179656 | tf_op jit(solution)/shard_map/ppermute | solution.py:624
  4.4 19.0 %collective-permute-start.1 = (f32[8,4,8,384]{3,2,1,0:T(8,128)S(1)}, f32[8,4,8,384]{3,2,1,0:T(8,128)S(1)}, u32[]{:S(2)}, u32[]{:S(2)}) collective-permute-start(f32[8,4,8,384]{3,2,1,0:T(8,128)S(1)} %get-tuple-element.28), channel_id=1, source_target_pairs={{0,16},{8,24},{16,0},{24,8},{1,17},{9,25},{17,1},{25,9},{2,18},{10... | collective-permute-start | bytes 1179656 | tf_op jit(solution)/shard_map/ppermute | solution.py:624
  5.9 17.5 %collective-permute-start.2 = (f32[8,4,8,384]{3,2,1,0:T(8,128)S(1)}, f32[8,4,8,384]{3,2,1,0:T(8,128)S(1)}, u32[]{:S(2)}, u32[]{:S(2)}) collective-permute-start(f32[8,4,8,384]{3,2,1,0:T(8,128)S(1)} %get-tuple-element.29), channel_id=1, source_target_pairs={{0,24},{8,16},{16,8},{24,0},{1,25},{9,17},{17,9},{25,1},{2,26},{10... | collective-permute-start | bytes 1179656 | tf_op jit(solution)/shard_map/ppermute | solution.py:624
  24.3 13.0 %collective-permute-start.7 = (f32[2,16,8,384]{3,2,1,0:T(8,128)S(1)}, f32[2,16,8,384]{3,2,1,0:T(8,128)S(1)}, u32[]{:S(2)}, u32[]{:S(2)}) collective-permute-start(f32[2,16,8,384]{3,2,1,0:T(8,128)S(1)} %shard_map.83.refs_6_.refs_0_), channel_id=1, source_target_pairs={{0,24},{8,16},{16,8},{24,0},{1,25},{9,17},{17,9},{25,1},{2,26},{10... | collective-permute-start | bytes 1179656 | tf_op jit(solution)/shard_map/ppermute | solution.py:624
  25.9 17.6 %collective-permute-start.6 = (f32[2,16,8,384]{3,2,1,0:T(8,128)S(1)}, f32[2,16,8,384]{3,2,1,0:T(8,128)S(1)}, u32[]{:S(2)}, u32[]{:S(2)}) collective-permute-start(f32[2,16,8,384]{3,2,1,0:T(8,128)S(1)} %shard_map.83.refs_6_.refs_0_), channel_id=1, source_target_pairs={{0,16},{8,24},{16,0},{24,8},{1,17},{9,25},{17,1},{25,9},{2,18},{10... | collective-permute-start | bytes 1179656 | tf_op jit(solution)/shard_map/ppermute | solution.py:624
  27.1 16.4 %collective-permute-start.5 = (f32[2,16,8,384]{3,2,1,0:T(8,128)S(1)}, f32[2,16,8,384]{3,2,1,0:T(8,128)S(1)}, u32[]{:S(2)}, u32[]{:S(2)}) collective-permute-start(f32[2,16,8,384]{3,2,1,0:T(8,128)S(1)} %shard_map.83.refs_6_.refs_0_), channel_id=1, source_target_pairs={{0,8},{8,0},{16,24},{24,16},{1,9},{9,1},{17,25},{25,17},{2,10},{10... | collective-permute-start | bytes 1179656 | tf_op jit(solution)/shard_map/ppermute | solution.py:624
  28.7 17.7 %collective-permute-start.3 = (f32[6,16,8,384]{3,2,1,0:T(8,128)S(1)}, f32[6,16,8,384]{3,2,1,0:T(8,128)S(1)}, u32[]{:S(2)}, u32[]{:S(2)}) collective-permute-start(f32[6,16,8,384]{3,2,1,0:T(8,128)S(1)} %get-tuple-element.32), channel_id=1, source_target_pairs={{1,2},{2,1},{3,4},{4,3},{5,6},{6,5},{9,10},{10,9},{11,12},{12,11},... | collective-permute-start | bytes 3538952 | tf_op jit(solution)/shard_map/ppermute | solution.py:606
  30.7 15.7 %collective-permute-start.4 = (f32[6,16,8,384]{3,2,1,0:T(8,128)S(1)}, f32[6,16,8,384]{3,2,1,0:T(8,128)S(1)}, u32[]{:S(2)}, u32[]{:S(2)}) collective-permute-start(f32[6,16,8,384]{3,2,1,0:T(8,128)S(1)} %get-tuple-element.33), channel_id=1, source_target_pairs={{0,1},{1,0},{2,3},{3,2},{4,5},{5,4},{6,7},{7,6},{8,9},{9,8},{10,11... | collective-permute-start | bytes 3538952 | tf_op jit(solution)/shard_map/ppermute | solution.py:607
  51.9 11.7 %collective-permute-start.8 = (f32[3,16,8,384]{3,2,1,0:T(8,128)S(1)}, f32[3,16,8,384]{3,2,1,0:T(8,128)S(1)}, u32[]{:S(2)}, u32[]{:S(2)}) collective-permute-start(f32[3,16,8,384]{3,2,1,0:T(8,128)S(1)} %get-tuple-element.41), channel_id=1, source_target_pairs={{1,2},{2,1},{3,4},{4,3},{5,6},{6,5},{9,10},{10,9},{11,12},{12,11},... | collective-permute-start | bytes 1769480 | tf_op jit(solution)/shard_map/ppermute | solution.py:606
  56.0 7.6 %collective-permute-start.9 = (f32[3,16,8,384]{3,2,1,0:T(8,128)S(1)}, f32[3,16,8,384]{3,2,1,0:T(8,128)S(1)}, u32[]{:S(2)}, u32[]{:S(2)}) collective-permute-start(f32[3,16,8,384]{3,2,1,0:T(8,128)S(1)} %get-tuple-element.42), channel_id=1, source_target_pairs={{0,1},{1,0},{2,3},{3,2},{4,5},{5,4},{6,7},{7,6},{8,9},{9,8},{10,11... | collective-permute-start | bytes 1769480 | tf_op jit(solution)/shard_map/ppermute | solution.py:607
  66.6 7.9 %collective-permute-start.10 = (f32[4,4,8,384]{3,2,1,0:T(8,128)S(1)}, f32[4,4,8,384]{3,2,1,0:T(8,128)S(1)}, u32[]{:S(2)}, u32[]{:S(2)}) collective-permute-start(f32[4,4,8,384]{3,2,1,0:T(8,128)S(1)} %get-tuple-element.44), channel_id=1, source_target_pairs={{0,8},{8,0},{16,24},{24,16},{1,9},{9,1},{17,25},{25,17},{2,10},{10... | collective-permute-start | bytes 589832 | tf_op jit(solution)/shard_map/ppermute | solution.py:624
  67.9 7.2 %collective-permute-start.11 = (f32[4,4,8,384]{3,2,1,0:T(8,128)S(1)}, f32[4,4,8,384]{3,2,1,0:T(8,128)S(1)}, u32[]{:S(2)}, u32[]{:S(2)}) collective-permute-start(f32[4,4,8,384]{3,2,1,0:T(8,128)S(1)} %get-tuple-element.45), channel_id=1, source_target_pairs={{0,16},{8,24},{16,0},{24,8},{1,17},{9,25},{17,1},{25,9},{2,18},{10... | collective-permute-start | bytes 589832 | tf_op jit(solution)/shard_map/ppermute | solution.py:624
  68.7 9.7 %collective-permute-start.12 = (f32[4,4,8,384]{3,2,1,0:T(8,128)S(1)}, f32[4,4,8,384]{3,2,1,0:T(8,128)S(1)}, u32[]{:S(2)}, u32[]{:S(2)}) collective-permute-start(f32[4,4,8,384]{3,2,1,0:T(8,128)S(1)} %get-tuple-element.46), channel_id=1, source_target_pairs={{0,24},{8,16},{16,8},{24,0},{1,25},{9,17},{17,9},{25,1},{2,26},{10... | collective-permute-start | bytes 589832 | tf_op jit(solution)/shard_map/ppermute | solution.py:624

commit v4 on v3

--- a/solution.py
+++ b/solution.py
@@ -372,7 +372,7 @@
             before = now
         return 0
 
-    lax.fori_loop(0, groups, body, 0, unroll=2)
+    lax.fori_loop(0, groups, body, 0, unroll=4)
 
 
 def meridional_pass(field, before, after, north, out):
@@ -393,7 +393,7 @@
             out[r, i] = total[r]
         return 0
 
-    lax.fori_loop(0, groups, body, 0, unroll=2)
+    lax.fori_loop(0, groups, body, 0, unroll=4)
 
 
 def pole_pass(field, ghosts, out):
@@ -414,7 +414,7 @@
                 out[second, i] = out[second, i] + ghosts[2, j] * near
                 return 0
 
-            lax.fori_loop(0, groups, body, 0, unroll=2)
+            lax.fori_loop(0, groups, body, 0, unroll=4)
 
 
 def widen(values, width):
@@ -449,7 +449,7 @@
             emit(r, q, tile, total)
         return 0
 
-    lax.fori_loop(0, rows * tiles, body, 0, unroll=2)
+    lax.fori_loop(0, rows * tiles, body, 0, unroll=4)
 
 
 def east_factors(width, courant, out):
@@ -465,7 +465,7 @@
                 out[m + HALO, r, q * tiles + tile] = stencil(w.get(1 - m), w.get(-m), m)
         return 0
 
-    lax.fori_loop(0, rows * tiles, body, 0, unroll=2)
+    lax.fori_loop(0, rows * tiles, body, 0, unroll=4)
 
 
 def solve_pass(field, g, a, h):
@@ -480,7 +480,7 @@
             field[r, q * tiles + tile] = x[tile]
         return 0
 
-    lax.fori_loop(0, rows * QUARTERS, body, 0, unroll=2)
+    lax.fori_loop(0, rows * QUARTERS, body, 0, unroll=4)
 
 
 def place(pieces, tiles, direct, out):

time: 80.4 us -> 80 us (level)
    ppermute x2, starting transfers between devices: 6.11 us -> 3.9 us  [lat_exchange(): from_z = lax.ppermute(edge_z, 'lat', pairs(1))]
    ppermute x2, starting transfers between devices: 1.73 us -> 3.43 us  [lat_exchange(): from_c = lax.ppermute(edge_c, 'lat', pairs(0))]
where the time goes in v4:
time: 80 us; the launch traced here: 79.1 us
  waiting for transfers between devices  44.1 us (55%)
  starting transfers between devices  18 us (22%)
  Pallas kernels  16.9 us (21%)
    ppermute x9, waiting for transfers between devices, on_device(): lax.ppermute(x, 'lon', [(i, i ^ s) for i in range(parts)])  36.5 us
    pallas_call x9, Pallas kernels, call(): pl.pallas_call(kernel, out_shape=[jax.ShapeDtypeStruct(s, f32) if isinsta...  16.9 us
    ppermute x9, starting transfers between devices, on_device(): lax.ppermute(x, 'lon', [(i, i ^ s) for i in range(parts)])  10.7 us
    ppermute x2, waiting for transfers between devices, lat_exchange(): from_z = lax.ppermute(edge_z, 'lat', pairs(1))  7.53 us
    ppermute x2, starting transfers between devices, lat_exchange(): from_z = lax.ppermute(edge_z, 'lat', pairs(1))  3.9 us
    ppermute x2, starting transfers between devices, lat_exchange(): from_c = lax.ppermute(edge_c, 'lat', pairs(0))  3.43 us
  transfers between devices with their start and end apart: 13, of which 8 were waited for; matrix products, arithmetic and copies ran while one was open for 0% of the time, Pallas kernels for 5%

profile of v4, /device:TPU:8, one launch (start us, length us, event | category | flops | bytes accessed | tf_op | source)
XLA Modules:
  0.0 79.1 jit_solution(8907535662086265700)
XLA Ops:
  0.0 0.0 copy-start.1
  0.0 2.8 %shard_map.82 = (f32[8,4,8,384]{3,2,1,0:T(8,128)S(1)}, f32[8,4,8,384]{3,2,1,0:T(8,128)S(1)}, f32[8,4,8,384]{3,2,1,0:T(8,128)S(1)}, f32[8,4,8,384]{3,2,1,0:T(8,128)S(1)}, f32[4,4,8,384]{3,2,1,0:T(8,128)S(1)}) custom-call(f32[4,360,128]{2,1,0:T(8,128)} %sens.1, f32[31,4,360]{2,1,0:T(4,128)} %bitcast.5, f32[4,32,360]{2,1,0:T(8,128)} %bitcast.4), custom_call_target="tpu_custom_call" | custom-call | flops 3000000000 | bytes 100000 | tf_op jit(solution)/shard_map/pallas_call | solution.py:592
  2.8 0.0 copy-start
  2.8 1.6 %collective-permute-start = (f32[8,4,8,384]{3,2,1,0:T(8,128)S(1)}, f32[8,4,8,384]{3,2,1,0:T(8,128)S(1)}, u32[]{:S(2)}, u32[]{:S(2)}) collective-permute-start(f32[8,4,8,384]{3,2,1,0:T(8,128)S(1)} %get-tuple-element.27), channel_id=1, source_target_pairs={{0,8},{8,0},{16,24},{24,16},{1,9},{9,1},{17,25},{25,17},{2,10},{10... | collective-permute-start | bytes 1179656 | tf_op jit(solution)/shard_map/ppermute | solution.py:624
  4.4 1.5 %collective-permute-start.1 = (f32[8,4,8,384]{3,2,1,0:T(8,128)S(1)}, f32[8,4,8,384]{3,2,1,0:T(8,128)S(1)}, u32[]{:S(2)}, u32[]{:S(2)}) collective-permute-start(f32[8,4,8,384]{3,2,1,0:T(8,128)S(1)} %get-tuple-element.28), channel_id=1, source_target_pairs={{0,16},{8,24},{16,0},{24,8},{1,17},{9,25},{17,1},{25,9},{2,18},{10... | collective-permute-start | bytes 1179656 | tf_op jit(solution)/shard_map/ppermute | solution.py:624
  5.9 0.5 collective-permute-start.2
  6.4 8.5 %collective-permute-done.refs_0_.refs_1_ = f32[8,4,8,384]{3,2,1,0:T(8,128)S(1)} collective-permute-done((f32[8,4,8,384]{3,2,1,0:T(8,128)S(1)}, f32[8,4,8,384]{3,2,1,0:T(8,128)S(1)}, u32[]{:S(2)}, u32[]{:S(2)}) %collective-permute-start) | collective-permute-done | bytes 393248 | tf_op jit(solution)/shard_map/ppermute | solution.py:624
  14.9 8.5 %collective-permute-done.1.refs_1_.refs_2_ = f32[8,4,8,384]{3,2,1,0:T(8,128)S(1)} collective-permute-done((f32[8,4,8,384]{3,2,1,0:T(8,128)S(1)}, f32[8,4,8,384]{3,2,1,0:T(8,128)S(1)}, u32[]{:S(2)}, u32[]{:S(2)}) %collective-permute-start.1) | collective-permute-done | bytes 393248 | tf_op jit(solution)/shard_map/ppermute | solution.py:624
  23.4 0.0 collective-permute-done.2.refs_2_.refs_3_
  23.4 0.9 %shard_map.83.refs_6_.refs_0_ = f32[2,16,8,384]{3,2,1,0:T(8,128)S(1)} custom-call(f32[4,4,8,384]{3,2,1,0:T(8,128)S(1)} %get-tuple-element.30.h, f32[8,4,8,384]{3,2,1,0:T(8,128)S(1)} %collective-permute-done.refs_0_.refs_1_, f32[8,4,8,384]{3,2,1,0:T(8,128)S(1)} %collective-permute-done.1.refs_1_.refs_2_, ...), custom_call_target="tpu_custom_call" | custom-call | flops 500000000 | bytes 100000 | tf_op jit(solution)/shard_map/pallas_call | solution.py:592
  24.3 1.6 %collective-permute-start.7 = (f32[2,16,8,384]{3,2,1,0:T(8,128)S(1)}, f32[2,16,8,384]{3,2,1,0:T(8,128)S(1)}, u32[]{:S(2)}, u32[]{:S(2)}) collective-permute-start(f32[2,16,8,384]{3,2,1,0:T(8,128)S(1)} %shard_map.83.refs_6_.refs_0_), channel_id=1, source_target_pairs={{0,24},{8,16},{16,8},{24,0},{1,25},{9,17},{17,9},{25,1},{2,26},{10... | collective-permute-start | bytes 1179656 | tf_op jit(solution)/shard_map/ppermute | solution.py:624
  25.9 1.2 %collective-permute-start.6 = (f32[2,16,8,384]{3,2,1,0:T(8,128)S(1)}, f32[2,16,8,384]{3,2,1,0:T(8,128)S(1)}, u32[]{:S(2)}, u32[]{:S(2)}) collective-permute-start(f32[2,16,8,384]{3,2,1,0:T(8,128)S(1)} %shard_map.83.refs_6_.refs_0_), channel_id=1, source_target_pairs={{0,16},{8,24},{16,0},{24,8},{1,17},{9,25},{17,1},{25,9},{2,18},{10... | collective-permute-start | bytes 1179656 | tf_op jit(solution)/shard_map/ppermute | solution.py:624
  27.1 0.8 %collective-permute-start.5 = (f32[2,16,8,384]{3,2,1,0:T(8,128)S(1)}, f32[2,16,8,384]{3,2,1,0:T(8,128)S(1)}, u32[]{:S(2)}, u32[]{:S(2)}) collective-permute-start(f32[2,16,8,384]{3,2,1,0:T(8,128)S(1)} %shard_map.83.refs_6_.refs_0_), channel_id=1, source_target_pairs={{0,8},{8,0},{16,24},{24,16},{1,9},{9,1},{17,25},{25,17},{2,10},{10... | collective-permute-start | bytes 1179656 | tf_op jit(solution)/shard_map/ppermute | solution.py:624
  27.9 0.0 copy-done.1
  27.9 0.0 copy-done
  27.9 0.8 %shard_map.84 = (f32[4,16,8,384]{3,2,1,0:T(8,128)S(1)}, f32[4,16,8,384]{3,2,1,0:T(8,128)S(1)}, f32[6,16,8,384]{3,2,1,0:T(8,128)S(1)}, f32[6,16,8,384]{3,2,1,0:T(8,128)S(1)}) custom-call(f32[8,4,8,384]{3,2,1,0:T(8,128)S(1)} %get-tuple-element.26.refs_0_, f32[8,4,8,384]{3,2,1,0:T(8,128)S(1)} %collective-permute-done.refs_0_.refs_1_, ...), custom_call_target="tpu_custom_call" | custom-call | flops 2500000000 | bytes 100000 | tf_op jit(solution)/shard_map/pallas_call | solution.py:592
  28.7 1.9 %collective-permute-start.3 = (f32[6,16,8,384]{3,2,1,0:T(8,128)S(1)}, f32[6,16,8,384]{3,2,1,0:T(8,128)S(1)}, u32[]{:S(2)}, u32[]{:S(2)}) collective-permute-start(f32[6,16,8,384]{3,2,1,0:T(8,128)S(1)} %get-tuple-element.32), channel_id=1, source_target_pairs={{1,2},{2,1},{3,4},{4,3},{5,6},{6,5},{9,10},{10,9},{11,12},{12,11},... | collective-permute-start | bytes 3538952 | tf_op jit(solution)/shard_map/ppermute | solution.py:606
  30.7 1.7 %collective-permute-start.4 = (f32[6,16,8,384]{3,2,1,0:T(8,128)S(1)}, f32[6,16,8,384]{3,2,1,0:T(8,128)S(1)}, u32[]{:S(2)}, u32[]{:S(2)}) collective-permute-start(f32[6,16,8,384]{3,2,1,0:T(8,128)S(1)} %get-tuple-element.33), channel_id=1, source_target_pairs={{0,1},{1,0},{2,3},{3,2},{4,5},{5,4},{6,7},{7,6},{8,9},{9,8},{10,11... | collective-permute-start | bytes 3538952 | tf_op jit(solution)/shard_map/ppermute | solution.py:607
  32.4 4.9 %collective-permute-done.7.refs_3_ = f32[2,16,8,384]{3,2,1,0:T(8,128)S(1)} collective-permute-done((f32[2,16,8,384]{3,2,1,0:T(8,128)S(1)}, f32[2,16,8,384]{3,2,1,0:T(8,128)S(1)}, u32[]{:S(2)}, u32[]{:S(2)}) %collective-permute-start.7) | collective-permute-done | bytes 393248 | tf_op jit(solution)/shard_map/ppermute | solution.py:624
  37.4 6.1 %collective-permute-done.6.refs_2_ = f32[2,16,8,384]{3,2,1,0:T(8,128)S(1)} collective-permute-done((f32[2,16,8,384]{3,2,1,0:T(8,128)S(1)}, f32[2,16,8,384]{3,2,1,0:T(8,128)S(1)}, u32[]{:S(2)}, u32[]{:S(2)}) %collective-permute-start.6) | collective-permute-done | bytes 393248 | tf_op jit(solution)/shard_map/ppermute | solution.py:624
  43.5 0.0 collective-permute-done.5.refs_1_
  43.5 0.5 shard_map.87
  44.0 2.3 %shard_map.86.east = f32[7,4,16,8,384]{4,3,2,1,0:T(8,128)S(1)} custom-call(f32[2,16,8,384]{3,2,1,0:T(8,128)S(1)} %shard_map.83.refs_6_.refs_0_, f32[2,16,8,384]{3,2,1,0:T(8,128)S(1)} %collective-permute-done.5.refs_1_, f32[2,16,8,384]{3,2,1,0:T(8,128)S(1)} %collective-permute-done.6.refs_2_, f32[2,16,8,384]{3,2,1,0:T(8,128)S(1)} %collective-permute-done.7.refs_3_), custom_call_target="tpu_custom_call" | custom-call | flops 10000000000 | bytes 100000 | tf_op jit(solution)/shard_map/pallas_call | solution.py:592
  46.4 0.0 collective-permute-done.3.from_z
  46.4 0.0 collective-permute-done.4.from_c
  46.4 1.5 %shard_map.85 = (f32[7,4,16,8,384]{4,3,2,1,0:T(8,128)S(1)}, f32[3,16,8,384]{3,2,1,0:T(8,128)S(1)}) custom-call(f32[4,16,8,384]{3,2,1,0:T(8,128)S(1)} %get-tuple-element.34.north, f32[6,16,8,384]{3,2,1,0:T(8,128)S(1)} %collective-permute-done.3.from_z, f32[6,16,8,384]{3,2,1,0:T(8,128)S(1)} %collective-permute-done.4.from_c), custom_call_target="tpu_custom_call" | custom-call | flops 1500000000 | bytes 100000 | tf_op jit(solution)/shard_map/pallas_call | solution.py:592
  47.9 3.7 %shard_map.88 = (f32[4,16,8,384]{3,2,1,0:T(8,128)S(1)}, f32[3,16,8,384]{3,2,1,0:T(8,128)S(1)}, f32[3,16,8,384]{3,2,1,0:T(8,128)S(1)}) custom-call(f32[4,16,8,384]{3,2,1,0:T(8,128)S(1)} %get-tuple-element.31.field, f32[6,16,8,384]{3,2,1,0:T(8,128)S(1)} %collective-permute-done.3.from_z, f32[6,16,8,384]{3,2,1,0:T(8,128)S(1)} %collective-permute-done.4.from_c, ...), custom_call_target="tpu_custom_call" | custom-call | flops 6000000000 | bytes 100000 | tf_op jit(solution)/shard_map/pallas_call | solution.py:592
  51.6 2.0 %collective-permute-start.8 = (f32[3,16,8,384]{3,2,1,0:T(8,128)S(1)}, f32[3,16,8,384]{3,2,1,0:T(8,128)S(1)}, u32[]{:S(2)}, u32[]{:S(2)}) collective-permute-start(f32[3,16,8,384]{3,2,1,0:T(8,128)S(1)} %get-tuple-element.41), channel_id=1, source_target_pairs={{1,2},{2,1},{3,4},{4,3},{5,6},{6,5},{9,10},{10,9},{11,12},{12,11},... | collective-permute-start | bytes 1769480 | tf_op jit(solution)/shard_map/ppermute | solution.py:606
  53.6 1.7 %collective-permute-start.9 = (f32[3,16,8,384]{3,2,1,0:T(8,128)S(1)}, f32[3,16,8,384]{3,2,1,0:T(8,128)S(1)}, u32[]{:S(2)}, u32[]{:S(2)}) collective-permute-start(f32[3,16,8,384]{3,2,1,0:T(8,128)S(1)} %get-tuple-element.42), channel_id=1, source_target_pairs={{0,1},{1,0},{2,3},{3,2},{4,5},{5,4},{6,7},{7,6},{8,9},{9,8},{10,11... | collective-permute-start | bytes 1769480 | tf_op jit(solution)/shard_map/ppermute | solution.py:607
  55.3 7.5 %collective-permute-done.8.from_z = f32[3,16,8,384]{3,2,1,0:T(8,128)S(1)} collective-permute-done((f32[3,16,8,384]{3,2,1,0:T(8,128)S(1)}, f32[3,16,8,384]{3,2,1,0:T(8,128)S(1)}, u32[]{:S(2)}, u32[]{:S(2)}) %collective-permute-start.8) | collective-permute-done | bytes 589856 | tf_op jit(solution)/shard_map/ppermute | solution.py:606
  62.8 0.0 collective-permute-done.9.from_c
  62.8 2.9 %shard_map.89 = (f32[4,4,8,384]{3,2,1,0:T(8,128)S(1)}, f32[4,4,8,384]{3,2,1,0:T(8,128)S(1)}, f32[4,4,8,384]{3,2,1,0:T(8,128)S(1)}, f32[4,4,8,384]{3,2,1,0:T(8,128)S(1)}) custom-call(f32[4,16,8,384]{3,2,1,0:T(8,128)S(1)} %get-tuple-element.40.field, f32[3,16,8,384]{3,2,1,0:T(8,128)S(1)} %collective-permute-done.8.from_z, ...), custom_call_target="tpu_custom_call" | custom-call | flops 3500000000 | bytes 100000 | tf_op jit(solution)/shard_map/pallas_call | solution.py:592
  65.7 1.1 %collective-permute-start.10 = (f32[4,4,8,384]{3,2,1,0:T(8,128)S(1)}, f32[4,4,8,384]{3,2,1,0:T(8,128)S(1)}, u32[]{:S(2)}, u32[]{:S(2)}) collective-permute-start(f32[4,4,8,384]{3,2,1,0:T(8,128)S(1)} %get-tuple-element.44), channel_id=1, source_target_pairs={{0,8},{8,0},{16,24},{24,16},{1,9},{9,1},{17,25},{25,17},{2,10},{10... | collective-permute-start | bytes 589832 | tf_op jit(solution)/shard_map/ppermute | solution.py:624
  66.8 1.0 %collective-permute-start.11 = (f32[4,4,8,384]{3,2,1,0:T(8,128)S(1)}, f32[4,4,8,384]{3,2,1,0:T(8,128)S(1)}, u32[]{:S(2)}, u32[]{:S(2)}) collective-permute-start(f32[4,4,8,384]{3,2,1,0:T(8,128)S(1)} %get-tuple-element.45), channel_id=1, source_target_pairs={{0,16},{8,24},{16,0},{24,8},{1,17},{9,25},{17,1},{25,9},{2,18},{10... | collective-permute-start | bytes 589832 | tf_op jit(solution)/shard_map/ppermute | solution.py:624
  67.8 1.4 %collective-permute-start.12 = (f32[4,4,8,384]{3,2,1,0:T(8,128)S(1)}, f32[4,4,8,384]{3,2,1,0:T(8,128)S(1)}, u32[]{:S(2)}, u32[]{:S(2)}) collective-permute-start(f32[4,4,8,384]{3,2,1,0:T(8,128)S(1)} %get-tuple-element.46), channel_id=1, source_target_pairs={{0,24},{8,16},{16,8},{24,0},{1,25},{9,17},{17,9},{25,1},{2,26},{10... | collective-permute-start | bytes 589832 | tf_op jit(solution)/shard_map/ppermute | solution.py:624
  69.2 4.3 %collective-permute-done.10.refs_1_ = f32[4,4,8,384]{3,2,1,0:T(8,128)S(1)} collective-permute-done((f32[4,4,8,384]{3,2,1,0:T(8,128)S(1)}, f32[4,4,8,384]{3,2,1,0:T(8,128)S(1)}, u32[]{:S(2)}, u32[]{:S(2)}) %collective-permute-start.10) | collective-permute-done | bytes 196640 | tf_op jit(solution)/shard_map/ppermute | solution.py:624
  73.5 2.7 %collective-permute-done.11.refs_2_ = f32[4,4,8,384]{3,2,1,0:T(8,128)S(1)} collective-permute-done((f32[4,4,8,384]{3,2,1,0:T(8,128)S(1)}, f32[4,4,8,384]{3,2,1,0:T(8,128)S(1)}, u32[]{:S(2)}, u32[]{:S(2)}) %collective-permute-start.11) | collective-permute-done | bytes 196640 | tf_op jit(solution)/shard_map/ppermute | solution.py:624
  76.2 1.5 %collective-permute-done.12.refs_3_ = f32[4,4,8,384]{3,2,1,0:T(8,128)S(1)} collective-permute-done((f32[4,4,8,384]{3,2,1,0:T(8,128)S(1)}, f32[4,4,8,384]{3,2,1,0:T(8,128)S(1)}, u32[]{:S(2)}, u32[]{:S(2)}) %collective-permute-start.12) | collective-permute-done | bytes 196640 | tf_op jit(solution)/shard_map/ppermute | solution.py:624
  77.7 1.4 %shard_map.90 = f32[4,360,128]{2,1,0:T(8,128)} custom-call(f32[4,4,8,384]{3,2,1,0:T(8,128)S(1)} %get-tuple-element.43.refs_0_, f32[4,4,8,384]{3,2,1,0:T(8,128)S(1)} %collective-permute-done.10.refs_1_, f32[4,4,8,384]{3,2,1,0:T(8,128)S(1)} %collective-permute-done.11.refs_2_, f32[4,4,8,384]{3,2,1,0:T(8,128)S(1)} %collective-permute-done.12.refs_3_), custom_call_target="tpu_custom_call" | custom-call | flops 1000000000 | bytes 100000 | tf_op jit(solution)/shard_map/pallas_call | solution.py:592
Async XLA Ops:
  0.0 27.9 %copy-start.1 = (bf16[2,768,384]{2,1,0:T(8,128)(2,1)S(1)}, bf16[2,768,384]{2,1,0:T(8,128)(2,1)}, u32[]{:S(2)}) copy-start(bf16[2,768,384]{2,1,0:T(8,128)(2,1)} %constant.4.clone.refs_4_.refs_0_) | copy-start | bytes 3538948
  2.8 25.1 %copy-start = (bf16[2,768,384]{2,1,0:T(8,128)(2,1)S(1)}, bf16[2,768,384]{2,1,0:T(8,128)(2,1)}, u32[]{:S(2)}) copy-start(bf16[2,768,384]{2,1,0:T(8,128)(2,1)} %constant.5.clone.refs_5_.refs_1_) | copy-start | bytes 3538948
  2.8 12.1 %collective-permute-start = (f32[8,4,8,384]{3,2,1,0:T(8,128)S(1)}, f32[8,4,8,384]{3,2,1,0:T(8,128)S(1)}, u32[]{:S(2)}, u32[]{:S(2)}) collective-permute-start(f32[8,4,8,384]{3,2,1,0:T(8,128)S(1)} %get-tuple-element.27), channel_id=1, source_target_pairs={{0,8},{8,0},{16,24},{24,16},{1,9},{9,1},{17,25},{25,17},{2,10},{10... | collective-permute-start | bytes 1179656 | tf_op jit(solution)/shard_map/ppermute | solution.py:624
  4.4 19.0 %collective-permute-start.1 = (f32[8,4,8,384]{3,2,1,0:T(8,128)S(1)}, f32[8,4,8,384]{3,2,1,0:T(8,128)S(1)}, u32[]{:S(2)}, u32[]{:S(2)}) collective-permute-start(f32[8,4,8,384]{3,2,1,0:T(8,128)S(1)} %get-tuple-element.28), channel_id=1, source_target_pairs={{0,16},{8,24},{16,0},{24,8},{1,17},{9,25},{17,1},{25,9},{2,18},{10... | collective-permute-start | bytes 1179656 | tf_op jit(solution)/shard_map/ppermute | solution.py:624
  5.9 17.5 %collective-permute-start.2 = (f32[8,4,8,384]{3,2,1,0:T(8,128)S(1)}, f32[8,4,8,384]{3,2,1,0:T(8,128)S(1)}, u32[]{:S(2)}, u32[]{:S(2)}) collective-permute-start(f32[8,4,8,384]{3,2,1,0:T(8,128)S(1)} %get-tuple-element.29), channel_id=1, source_target_pairs={{0,24},{8,16},{16,8},{24,0},{1,25},{9,17},{17,9},{25,1},{2,26},{10... | collective-permute-start | bytes 1179656 | tf_op jit(solution)/shard_map/ppermute | solution.py:624
  24.3 13.0 %collective-permute-start.7 = (f32[2,16,8,384]{3,2,1,0:T(8,128)S(1)}, f32[2,16,8,384]{3,2,1,0:T(8,128)S(1)}, u32[]{:S(2)}, u32[]{:S(2)}) collective-permute-start(f32[2,16,8,384]{3,2,1,0:T(8,128)S(1)} %shard_map.83.refs_6_.refs_0_), channel_id=1, source_target_pairs={{0,24},{8,16},{16,8},{24,0},{1,25},{9,17},{17,9},{25,1},{2,26},{10... | collective-permute-start | bytes 1179656 | tf_op jit(solution)/shard_map/ppermute | solution.py:624
  25.9 17.6 %collective-permute-start.6 = (f32[2,16,8,384]{3,2,1,0:T(8,128)S(1)}, f32[2,16,8,384]{3,2,1,0:T(8,128)S(1)}, u32[]{:S(2)}, u32[]{:S(2)}) collective-permute-start(f32[2,16,8,384]{3,2,1,0:T(8,128)S(1)} %shard_map.83.refs_6_.refs_0_), channel_id=1, source_target_pairs={{0,16},{8,24},{16,0},{24,8},{1,17},{9,25},{17,1},{25,9},{2,18},{10... | collective-permute-start | bytes 1179656 | tf_op jit(solution)/shard_map/ppermute | solution.py:624
  27.1 16.4 %collective-permute-start.5 = (f32[2,16,8,384]{3,2,1,0:T(8,128)S(1)}, f32[2,16,8,384]{3,2,1,0:T(8,128)S(1)}, u32[]{:S(2)}, u32[]{:S(2)}) collective-permute-start(f32[2,16,8,384]{3,2,1,0:T(8,128)S(1)} %shard_map.83.refs_6_.refs_0_), channel_id=1, source_target_pairs={{0,8},{8,0},{16,24},{24,16},{1,9},{9,1},{17,25},{25,17},{2,10},{10... | collective-permute-start | bytes 1179656 | tf_op jit(solution)/shard_map/ppermute | solution.py:624
  28.7 17.6 %collective-permute-start.3 = (f32[6,16,8,384]{3,2,1,0:T(8,128)S(1)}, f32[6,16,8,384]{3,2,1,0:T(8,128)S(1)}, u32[]{:S(2)}, u32[]{:S(2)}) collective-permute-start(f32[6,16,8,384]{3,2,1,0:T(8,128)S(1)} %get-tuple-element.32), channel_id=1, source_target_pairs={{1,2},{2,1},{3,4},{4,3},{5,6},{6,5},{9,10},{10,9},{11,12},{12,11},... | collective-permute-start | bytes 3538952 | tf_op jit(solution)/shard_map/ppermute | solution.py:606
  30.7 15.7 %collective-permute-start.4 = (f32[6,16,8,384]{3,2,1,0:T(8,128)S(1)}, f32[6,16,8,384]{3,2,1,0:T(8,128)S(1)}, u32[]{:S(2)}, u32[]{:S(2)}) collective-permute-start(f32[6,16,8,384]{3,2,1,0:T(8,128)S(1)} %get-tuple-element.33), channel_id=1, source_target_pairs={{0,1},{1,0},{2,3},{3,2},{4,5},{5,4},{6,7},{7,6},{8,9},{9,8},{10,11... | collective-permute-start | bytes 3538952 | tf_op jit(solution)/shard_map/ppermute | solution.py:607
  51.6 11.2 %collective-permute-start.8 = (f32[3,16,8,384]{3,2,1,0:T(8,128)S(1)}, f32[3,16,8,384]{3,2,1,0:T(8,128)S(1)}, u32[]{:S(2)}, u32[]{:S(2)}) collective-permute-start(f32[3,16,8,384]{3,2,1,0:T(8,128)S(1)} %get-tuple-element.41), channel_id=1, source_target_pairs={{1,2},{2,1},{3,4},{4,3},{5,6},{6,5},{9,10},{10,9},{11,12},{12,11},... | collective-permute-start | bytes 1769480 | tf_op jit(solution)/shard_map/ppermute | solution.py:606
  53.6 9.2 %collective-permute-start.9 = (f32[3,16,8,384]{3,2,1,0:T(8,128)S(1)}, f32[3,16,8,384]{3,2,1,0:T(8,128)S(1)}, u32[]{:S(2)}, u32[]{:S(2)}) collective-permute-start(f32[3,16,8,384]{3,2,1,0:T(8,128)S(1)} %get-tuple-element.42), channel_id=1, source_target_pairs={{0,1},{1,0},{2,3},{3,2},{4,5},{5,4},{6,7},{7,6},{8,9},{9,8},{10,11... | collective-permute-start | bytes 1769480 | tf_op jit(solution)/shard_map/ppermute | solution.py:607
  65.7 7.8 %collective-permute-start.10 = (f32[4,4,8,384]{3,2,1,0:T(8,128)S(1)}, f32[4,4,8,384]{3,2,1,0:T(8,128)S(1)}, u32[]{:S(2)}, u32[]{:S(2)}) collective-permute-start(f32[4,4,8,384]{3,2,1,0:T(8,128)S(1)} %get-tuple-element.44), channel_id=1, source_target_pairs={{0,8},{8,0},{16,24},{24,16},{1,9},{9,1},{17,25},{25,17},{2,10},{10... | collective-permute-start | bytes 589832 | tf_op jit(solution)/shard_map/ppermute | solution.py:624
  66.8 9.4 %collective-permute-start.11 = (f32[4,4,8,384]{3,2,1,0:T(8,128)S(1)}, f32[4,4,8,384]{3,2,1,0:T(8,128)S(1)}, u32[]{:S(2)}, u32[]{:S(2)}) collective-permute-start(f32[4,4,8,384]{3,2,1,0:T(8,128)S(1)} %get-tuple-element.45), channel_id=1, source_target_pairs={{0,16},{8,24},{16,0},{24,8},{1,17},{9,25},{17,1},{25,9},{2,18},{10... | collective-permute-start | bytes 589832 | tf_op jit(solution)/shard_map/ppermute | solution.py:624
  67.8 9.9 %collective-permute-start.12 = (f32[4,4,8,384]{3,2,1,0:T(8,128)S(1)}, f32[4,4,8,384]{3,2,1,0:T(8,128)S(1)}, u32[]{:S(2)}, u32[]{:S(2)}) collective-permute-start(f32[4,4,8,384]{3,2,1,0:T(8,128)S(1)} %get-tuple-element.46), channel_id=1, source_target_pairs={{0,24},{8,16},{16,8},{24,0},{1,25},{9,17},{17,9},{25,1},{2,26},{10... | collective-permute-start | bytes 589832 | tf_op jit(solution)/shard_map/ppermute | solution.py:624

commit v5 on v4

--- a/solution.py
+++ b/solution.py
@@ -55,7 +55,9 @@
 
 def product(high, low, t_high, t_low, side):
     dot = lambda x, t: lax.dot_general(x, t, (((1,), (side,)), ((), ())), preferred_element_type=f32)
-    return dot(high, t_high) + dot(low, t_high) + dot(high, t_low)
+    n = high.shape[0]
+    both = dot(jnp.concatenate([high, low], axis=0), t_high)
+    return both[:n] + both[n:] + dot(high, t_low)
 
 
 def column_factors(mix_at, levels, shape, store):

time: 80 us -> 79.9 us (level)
    ppermute x2, starting transfers between devices: 3.9 us -> 5.69 us  [lat_exchange(): from_z = lax.ppermute(edge_z, 'lat', pairs(1))]
    ppermute x2, starting transfers between devices: 3.43 us -> 1.82 us  [lat_exchange(): from_c = lax.ppermute(edge_c, 'lat', pairs(0))]
where the time goes in v5:
time: 79.9 us; the launch traced here: 79.2 us
  waiting for transfers between devices  44 us (55%)
  starting transfers between devices  18.2 us (23%)
  Pallas kernels  16.9 us (21%)
    ppermute x9, waiting for transfers between devices, on_device(): lax.ppermute(x, 'lon', [(i, i ^ s) for i in range(parts)])  36.5 us
    pallas_call x9, Pallas kernels, call(): pl.pallas_call(kernel, out_shape=[jax.ShapeDtypeStruct(s, f32) if isinsta...  16.9 us
    ppermute x9, starting transfers between devices, on_device(): lax.ppermute(x, 'lon', [(i, i ^ s) for i in range(parts)])  10.7 us
    ppermute x2, waiting for transfers between devices, lat_exchange(): from_z = lax.ppermute(edge_z, 'lat', pairs(1))  7.48 us
    ppermute x2, starting transfers between devices, lat_exchange(): from_z = lax.ppermute(edge_z, 'lat', pairs(1))  5.69 us
    ppermute x2, starting transfers between devices, lat_exchange(): from_c = lax.ppermute(edge_c, 'lat', pairs(0))  1.82 us
  transfers between devices with their start and end apart: 13, of which 8 were waited for; matrix products, arithmetic and copies ran while one was open for 0% of the time, Pallas kernels for 5%

profile of v5, /device:TPU:8, one launch (start us, length us, event | category | flops | bytes accessed | tf_op | source)
XLA Modules:
  0.0 79.2 jit_solution(14844250382748845773)
XLA Ops:
  0.0 0.0 copy-start.1
  0.0 2.8 %shard_map.82 = (f32[8,4,8,384]{3,2,1,0:T(8,128)S(1)}, f32[8,4,8,384]{3,2,1,0:T(8,128)S(1)}, f32[8,4,8,384]{3,2,1,0:T(8,128)S(1)}, f32[8,4,8,384]{3,2,1,0:T(8,128)S(1)}, f32[4,4,8,384]{3,2,1,0:T(8,128)S(1)}) custom-call(f32[4,360,128]{2,1,0:T(8,128)} %sens.1, f32[31,4,360]{2,1,0:T(4,128)} %bitcast.5, f32[4,32,360]{2,1,0:T(8,128)} %bitcast.4), custom_call_target="tpu_custom_call" | custom-call | flops 3000000000 | bytes 100000 | tf_op jit(solution)/shard_map/pallas_call | solution.py:594
  2.8 0.0 copy-start
  2.8 1.6 %collective-permute-start = (f32[8,4,8,384]{3,2,1,0:T(8,128)S(1)}, f32[8,4,8,384]{3,2,1,0:T(8,128)S(1)}, u32[]{:S(2)}, u32[]{:S(2)}) collective-permute-start(f32[8,4,8,384]{3,2,1,0:T(8,128)S(1)} %get-tuple-element.27), channel_id=1, source_target_pairs={{0,8},{8,0},{16,24},{24,16},{1,9},{9,1},{17,25},{25,17},{2,10},{10... | collective-permute-start | bytes 1179656 | tf_op jit(solution)/shard_map/ppermute | solution.py:626
  4.4 1.5 %collective-permute-start.1 = (f32[8,4,8,384]{3,2,1,0:T(8,128)S(1)}, f32[8,4,8,384]{3,2,1,0:T(8,128)S(1)}, u32[]{:S(2)}, u32[]{:S(2)}) collective-permute-start(f32[8,4,8,384]{3,2,1,0:T(8,128)S(1)} %get-tuple-element.28), channel_id=1, source_target_pairs={{0,16},{8,24},{16,0},{24,8},{1,17},{9,25},{17,1},{25,9},{2,18},{10... | collective-permute-start | bytes 1179656 | tf_op jit(solution)/shard_map/ppermute | solution.py:626
  5.9 0.5 collective-permute-start.2
  6.4 8.5 %collective-permute-done.refs_0_.refs_1_ = f32[8,4,8,384]{3,2,1,0:T(8,128)S(1)} collective-permute-done((f32[8,4,8,384]{3,2,1,0:T(8,128)S(1)}, f32[8,4,8,384]{3,2,1,0:T(8,128)S(1)}, u32[]{:S(2)}, u32[]{:S(2)}) %collective-permute-start) | collective-permute-done | bytes 393248 | tf_op jit(solution)/shard_map/ppermute | solution.py:626
  14.9 8.5 %collective-permute-done.1.refs_1_.refs_2_ = f32[8,4,8,384]{3,2,1,0:T(8,128)S(1)} collective-permute-done((f32[8,4,8,384]{3,2,1,0:T(8,128)S(1)}, f32[8,4,8,384]{3,2,1,0:T(8,128)S(1)}, u32[]{:S(2)}, u32[]{:S(2)}) %collective-permute-start.1) | collective-permute-done | bytes 393248 | tf_op jit(solution)/shard_map/ppermute | solution.py:626
  23.4 0.0 collective-permute-done.2.refs_2_.refs_3_
  23.4 0.9 %shard_map.83.refs_6_.refs_0_ = f32[2,16,8,384]{3,2,1,0:T(8,128)S(1)} custom-call(f32[4,4,8,384]{3,2,1,0:T(8,128)S(1)} %get-tuple-element.30.h, f32[8,4,8,384]{3,2,1,0:T(8,128)S(1)} %collective-permute-done.refs_0_.refs_1_, f32[8,4,8,384]{3,2,1,0:T(8,128)S(1)} %collective-permute-done.1.refs_1_.refs_2_, ...), custom_call_target="tpu_custom_call" | custom-call | flops 500000000 | bytes 100000 | tf_op jit(solution)/shard_map/pallas_call | solution.py:594
  24.3 1.6 %collective-permute-start.7 = (f32[2,16,8,384]{3,2,1,0:T(8,128)S(1)}, f32[2,16,8,384]{3,2,1,0:T(8,128)S(1)}, u32[]{:S(2)}, u32[]{:S(2)}) collective-permute-start(f32[2,16,8,384]{3,2,1,0:T(8,128)S(1)} %shard_map.83.refs_6_.refs_0_), channel_id=1, source_target_pairs={{0,24},{8,16},{16,8},{24,0},{1,25},{9,17},{17,9},{25,1},{2,26},{10... | collective-permute-start | bytes 1179656 | tf_op jit(solution)/shard_map/ppermute | solution.py:626
  25.9 1.2 %collective-permute-start.6 = (f32[2,16,8,384]{3,2,1,0:T(8,128)S(1)}, f32[2,16,8,384]{3,2,1,0:T(8,128)S(1)}, u32[]{:S(2)}, u32[]{:S(2)}) collective-permute-start(f32[2,16,8,384]{3,2,1,0:T(8,128)S(1)} %shard_map.83.refs_6_.refs_0_), channel_id=1, source_target_pairs={{0,16},{8,24},{16,0},{24,8},{1,17},{9,25},{17,1},{25,9},{2,18},{10... | collective-permute-start | bytes 1179656 | tf_op jit(solution)/shard_map/ppermute | solution.py:626
  27.1 0.8 %collective-permute-start.5 = (f32[2,16,8,384]{3,2,1,0:T(8,128)S(1)}, f32[2,16,8,384]{3,2,1,0:T(8,128)S(1)}, u32[]{:S(2)}, u32[]{:S(2)}) collective-permute-start(f32[2,16,8,384]{3,2,1,0:T(8,128)S(1)} %shard_map.83.refs_6_.refs_0_), channel_id=1, source_target_pairs={{0,8},{8,0},{16,24},{24,16},{1,9},{9,1},{17,25},{25,17},{2,10},{10... | collective-permute-start | bytes 1179656 | tf_op jit(solution)/shard_map/ppermute | solution.py:626
  27.9 0.0 copy-done.1
  27.9 0.0 copy-done
  27.9 0.8 %shard_map.84 = (f32[4,16,8,384]{3,2,1,0:T(8,128)S(1)}, f32[4,16,8,384]{3,2,1,0:T(8,128)S(1)}, f32[6,16,8,384]{3,2,1,0:T(8,128)S(1)}, f32[6,16,8,384]{3,2,1,0:T(8,128)S(1)}) custom-call(f32[8,4,8,384]{3,2,1,0:T(8,128)S(1)} %get-tuple-element.26.refs_0_, f32[8,4,8,384]{3,2,1,0:T(8,128)S(1)} %collective-permute-done.refs_0_.refs_1_, ...), custom_call_target="tpu_custom_call" | custom-call | flops 2500000000 | bytes 100000 | tf_op jit(solution)/shard_map/pallas_call | solution.py:594
  28.7 1.9 %collective-permute-start.3 = (f32[6,16,8,384]{3,2,1,0:T(8,128)S(1)}, f32[6,16,8,384]{3,2,1,0:T(8,128)S(1)}, u32[]{:S(2)}, u32[]{:S(2)}) collective-permute-start(f32[6,16,8,384]{3,2,1,0:T(8,128)S(1)} %get-tuple-element.32), channel_id=1, source_target_pairs={{1,2},{2,1},{3,4},{4,3},{5,6},{6,5},{9,10},{10,9},{11,12},{12,11},... | collective-permute-start | bytes 3538952 | tf_op jit(solution)/shard_map/ppermute | solution.py:608
  30.7 1.7 %collective-permute-start.4 = (f32[6,16,8,384]{3,2,1,0:T(8,128)S(1)}, f32[6,16,8,384]{3,2,1,0:T(8,128)S(1)}, u32[]{:S(2)}, u32[]{:S(2)}) collective-permute-start(f32[6,16,8,384]{3,2,1,0:T(8,128)S(1)} %get-tuple-element.33), channel_id=1, source_target_pairs={{0,1},{1,0},{2,3},{3,2},{4,5},{5,4},{6,7},{7,6},{8,9},{9,8},{10,11... | collective-permute-start | bytes 3538952 | tf_op jit(solution)/shard_map/ppermute | solution.py:609
  32.4 4.9 %collective-permute-done.7.refs_3_ = f32[2,16,8,384]{3,2,1,0:T(8,128)S(1)} collective-permute-done((f32[2,16,8,384]{3,2,1,0:T(8,128)S(1)}, f32[2,16,8,384]{3,2,1,0:T(8,128)S(1)}, u32[]{:S(2)}, u32[]{:S(2)}) %collective-permute-start.7) | collective-permute-done | bytes 393248 | tf_op jit(solution)/shard_map/ppermute | solution.py:626
  37.4 6.1 %collective-permute-done.6.refs_2_ = f32[2,16,8,384]{3,2,1,0:T(8,128)S(1)} collective-permute-done((f32[2,16,8,384]{3,2,1,0:T(8,128)S(1)}, f32[2,16,8,384]{3,2,1,0:T(8,128)S(1)}, u32[]{:S(2)}, u32[]{:S(2)}) %collective-permute-start.6) | collective-permute-done | bytes 393248 | tf_op jit(solution)/shard_map/ppermute | solution.py:626
  43.5 0.0 collective-permute-done.5.refs_1_
  43.5 0.5 shard_map.87
  44.0 2.3 %shard_map.86.east = f32[7,4,16,8,384]{4,3,2,1,0:T(8,128)S(1)} custom-call(f32[2,16,8,384]{3,2,1,0:T(8,128)S(1)} %shard_map.83.refs_6_.refs_0_, f32[2,16,8,384]{3,2,1,0:T(8,128)S(1)} %collective-permute-done.5.refs_1_, f32[2,16,8,384]{3,2,1,0:T(8,128)S(1)} %collective-permute-done.6.refs_2_, f32[2,16,8,384]{3,2,1,0:T(8,128)S(1)} %collective-permute-done.7.refs_3_), custom_call_target="tpu_custom_call" | custom-call | flops 10000000000 | bytes 100000 | tf_op jit(solution)/shard_map/pallas_call | solution.py:594
  46.4 0.0 collective-permute-done.3.from_z
  46.4 0.0 collective-permute-done.4.from_c
  46.4 1.5 %shard_map.85 = (f32[7,4,16,8,384]{4,3,2,1,0:T(8,128)S(1)}, f32[3,16,8,384]{3,2,1,0:T(8,128)S(1)}) custom-call(f32[4,16,8,384]{3,2,1,0:T(8,128)S(1)} %get-tuple-element.34.north, f32[6,16,8,384]{3,2,1,0:T(8,128)S(1)} %collective-permute-done.3.from_z, f32[6,16,8,384]{3,2,1,0:T(8,128)S(1)} %collective-permute-done.4.from_c), custom_call_target="tpu_custom_call" | custom-call | flops 1500000000 | bytes 100000 | tf_op jit(solution)/shard_map/pallas_call | solution.py:594
  47.9 3.7 %shard_map.88 = (f32[4,16,8,384]{3,2,1,0:T(8,128)S(1)}, f32[3,16,8,384]{3,2,1,0:T(8,128)S(1)}, f32[3,16,8,384]{3,2,1,0:T(8,128)S(1)}) custom-call(f32[4,16,8,384]{3,2,1,0:T(8,128)S(1)} %get-tuple-element.31.field, f32[6,16,8,384]{3,2,1,0:T(8,128)S(1)} %collective-permute-done.3.from_z, f32[6,16,8,384]{3,2,1,0:T(8,128)S(1)} %collective-permute-done.4.from_c, ...), custom_call_target="tpu_custom_call" | custom-call | flops 6000000000 | bytes 100000 | tf_op jit(solution)/shard_map/pallas_call | solution.py:594
  51.6 3.8 %collective-permute-start.8 = (f32[3,16,8,384]{3,2,1,0:T(8,128)S(1)}, f32[3,16,8,384]{3,2,1,0:T(8,128)S(1)}, u32[]{:S(2)}, u32[]{:S(2)}) collective-permute-start(f32[3,16,8,384]{3,2,1,0:T(8,128)S(1)} %get-tuple-element.41), channel_id=1, source_target_pairs={{1,2},{2,1},{3,4},{4,3},{5,6},{6,5},{9,10},{10,9},{11,12},{12,11},... | collective-permute-start | bytes 1769480 | tf_op jit(solution)/shard_map/ppermute | solution.py:608
  55.4 0.1 collective-permute-start.9
  55.4 7.5 %collective-permute-done.8.from_z = f32[3,16,8,384]{3,2,1,0:T(8,128)S(1)} collective-permute-done((f32[3,16,8,384]{3,2,1,0:T(8,128)S(1)}, f32[3,16,8,384]{3,2,1,0:T(8,128)S(1)}, u32[]{:S(2)}, u32[]{:S(2)}) %collective-permute-start.8) | collective-permute-done | bytes 589856 | tf_op jit(solution)/shard_map/ppermute | solution.py:608
  62.9 0.0 collective-permute-done.9.from_c
  62.9 2.9 %shard_map.89 = (f32[4,4,8,384]{3,2,1,0:T(8,128)S(1)}, f32[4,4,8,384]{3,2,1,0:T(8,128)S(1)}, f32[4,4,8,384]{3,2,1,0:T(8,128)S(1)}, f32[4,4,8,384]{3,2,1,0:T(8,128)S(1)}) custom-call(f32[4,16,8,384]{3,2,1,0:T(8,128)S(1)} %get-tuple-element.40.field, f32[3,16,8,384]{3,2,1,0:T(8,128)S(1)} %collective-permute-done.8.from_z, ...), custom_call_target="tpu_custom_call" | custom-call | flops 3500000000 | bytes 100000 | tf_op jit(solution)/shard_map/pallas_call | solution.py:594
  65.8 1.1 %collective-permute-start.10 = (f32[4,4,8,384]{3,2,1,0:T(8,128)S(1)}, f32[4,4,8,384]{3,2,1,0:T(8,128)S(1)}, u32[]{:S(2)}, u32[]{:S(2)}) collective-permute-start(f32[4,4,8,384]{3,2,1,0:T(8,128)S(1)} %get-tuple-element.44), channel_id=1, source_target_pairs={{0,8},{8,0},{16,24},{24,16},{1,9},{9,1},{17,25},{25,17},{2,10},{10... | collective-permute-start | bytes 589832 | tf_op jit(solution)/shard_map/ppermute | solution.py:626
  66.9 1.0 %collective-permute-start.11 = (f32[4,4,8,384]{3,2,1,0:T(8,128)S(1)}, f32[4,4,8,384]{3,2,1,0:T(8,128)S(1)}, u32[]{:S(2)}, u32[]{:S(2)}) collective-permute-start(f32[4,4,8,384]{3,2,1,0:T(8,128)S(1)} %get-tuple-element.45), channel_id=1, source_target_pairs={{0,16},{8,24},{16,0},{24,8},{1,17},{9,25},{17,1},{25,9},{2,18},{10... | collective-permute-start | bytes 589832 | tf_op jit(solution)/shard_map/ppermute | solution.py:626
  67.9 1.5 %collective-permute-start.12 = (f32[4,4,8,384]{3,2,1,0:T(8,128)S(1)}, f32[4,4,8,384]{3,2,1,0:T(8,128)S(1)}, u32[]{:S(2)}, u32[]{:S(2)}) collective-permute-start(f32[4,4,8,384]{3,2,1,0:T(8,128)S(1)} %get-tuple-element.46), channel_id=1, source_target_pairs={{0,24},{8,16},{16,8},{24,0},{1,25},{9,17},{17,9},{25,1},{2,26},{10... | collective-permute-start | bytes 589832 | tf_op jit(solution)/shard_map/ppermute | solution.py:626
  69.4 4.3 %collective-permute-done.10.refs_1_ = f32[4,4,8,384]{3,2,1,0:T(8,128)S(1)} collective-permute-done((f32[4,4,8,384]{3,2,1,0:T(8,128)S(1)}, f32[4,4,8,384]{3,2,1,0:T(8,128)S(1)}, u32[]{:S(2)}, u32[]{:S(2)}) %collective-permute-start.10) | collective-permute-done | bytes 196640 | tf_op jit(solution)/shard_map/ppermute | solution.py:626
  73.6 0.7 collective-permute-done.11.refs_2_
  74.3 3.4 %collective-permute-done.12.refs_3_ = f32[4,4,8,384]{3,2,1,0:T(8,128)S(1)} collective-permute-done((f32[4,4,8,384]{3,2,1,0:T(8,128)S(1)}, f32[4,4,8,384]{3,2,1,0:T(8,128)S(1)}, u32[]{:S(2)}, u32[]{:S(2)}) %collective-permute-start.12) | collective-permute-done | bytes 196640 | tf_op jit(solution)/shard_map/ppermute | solution.py:626
  77.8 1.4 %shard_map.90 = f32[4,360,128]{2,1,0:T(8,128)} custom-call(f32[4,4,8,384]{3,2,1,0:T(8,128)S(1)} %get-tuple-element.43.refs_0_, f32[4,4,8,384]{3,2,1,0:T(8,128)S(1)} %collective-permute-done.10.refs_1_, f32[4,4,8,384]{3,2,1,0:T(8,128)S(1)} %collective-permute-done.11.refs_2_, f32[4,4,8,384]{3,2,1,0:T(8,128)S(1)} %collective-permute-done.12.refs_3_), custom_call_target="tpu_custom_call" | custom-call | flops 1000000000 | bytes 100000 | tf_op jit(solution)/shard_map/pallas_call | solution.py:594
Async XLA Ops:
  0.0 27.9 %copy-start.1 = (bf16[2,768,384]{2,1,0:T(8,128)(2,1)S(1)}, bf16[2,768,384]{2,1,0:T(8,128)(2,1)}, u32[]{:S(2)}) copy-start(bf16[2,768,384]{2,1,0:T(8,128)(2,1)} %constant.4.clone.refs_4_.refs_0_) | copy-start | bytes 3538948
  2.8 25.1 %copy-start = (bf16[2,768,384]{2,1,0:T(8,128)(2,1)S(1)}, bf16[2,768,384]{2,1,0:T(8,128)(2,1)}, u32[]{:S(2)}) copy-start(bf16[2,768,384]{2,1,0:T(8,128)(2,1)} %constant.5.clone.refs_5_.refs_1_) | copy-start | bytes 3538948
  2.8 12.1 %collective-permute-start = (f32[8,4,8,384]{3,2,1,0:T(8,128)S(1)}, f32[8,4,8,384]{3,2,1,0:T(8,128)S(1)}, u32[]{:S(2)}, u32[]{:S(2)}) collective-permute-start(f32[8,4,8,384]{3,2,1,0:T(8,128)S(1)} %get-tuple-element.27), channel_id=1, source_target_pairs={{0,8},{8,0},{16,24},{24,16},{1,9},{9,1},{17,25},{25,17},{2,10},{10... | collective-permute-start | bytes 1179656 | tf_op jit(solution)/shard_map/ppermute | solution.py:626
  4.4 19.0 %collective-permute-start.1 = (f32[8,4,8,384]{3,2,1,0:T(8,128)S(1)}, f32[8,4,8,384]{3,2,1,0:T(8,128)S(1)}, u32[]{:S(2)}, u32[]{:S(2)}) collective-permute-start(f32[8,4,8,384]{3,2,1,0:T(8,128)S(1)} %get-tuple-element.28), channel_id=1, source_target_pairs={{0,16},{8,24},{16,0},{24,8},{1,17},{9,25},{17,1},{25,9},{2,18},{10... | collective-permute-start | bytes 1179656 | tf_op jit(solution)/shard_map/ppermute | solution.py:626
  5.9 17.5 %collective-permute-start.2 = (f32[8,4,8,384]{3,2,1,0:T(8,128)S(1)}, f32[8,4,8,384]{3,2,1,0:T(8,128)S(1)}, u32[]{:S(2)}, u32[]{:S(2)}) collective-permute-start(f32[8,4,8,384]{3,2,1,0:T(8,128)S(1)} %get-tuple-element.29), channel_id=1, source_target_pairs={{0,24},{8,16},{16,8},{24,0},{1,25},{9,17},{17,9},{25,1},{2,26},{10... | collective-permute-start | bytes 1179656 | tf_op jit(solution)/shard_map/ppermute | solution.py:626
  24.3 13.0 %collective-permute-start.7 = (f32[2,16,8,384]{3,2,1,0:T(8,128)S(1)}, f32[2,16,8,384]{3,2,1,0:T(8,128)S(1)}, u32[]{:S(2)}, u32[]{:S(2)}) collective-permute-start(f32[2,16,8,384]{3,2,1,0:T(8,128)S(1)} %shard_map.83.refs_6_.refs_0_), channel_id=1, source_target_pairs={{0,24},{8,16},{16,8},{24,0},{1,25},{9,17},{17,9},{25,1},{2,26},{10... | collective-permute-start | bytes 1179656 | tf_op jit(solution)/shard_map/ppermute | solution.py:626
  25.9 17.6 %collective-permute-start.6 = (f32[2,16,8,384]{3,2,1,0:T(8,128)S(1)}, f32[2,16,8,384]{3,2,1,0:T(8,128)S(1)}, u32[]{:S(2)}, u32[]{:S(2)}) collective-permute-start(f32[2,16,8,384]{3,2,1,0:T(8,128)S(1)} %shard_map.83.refs_6_.refs_0_), channel_id=1, source_target_pairs={{0,16},{8,24},{16,0},{24,8},{1,17},{9,25},{17,1},{25,9},{2,18},{10... | collective-permute-start | bytes 1179656 | tf_op jit(solution)/shard_map/ppermute | solution.py:626
  27.1 16.4 %collective-permute-start.5 = (f32[2,16,8,384]{3,2,1,0:T(8,128)S(1)}, f32[2,16,8,384]{3,2,1,0:T(8,128)S(1)}, u32[]{:S(2)}, u32[]{:S(2)}) collective-permute-start(f32[2,16,8,384]{3,2,1,0:T(8,128)S(1)} %shard_map.83.refs_6_.refs_0_), channel_id=1, source_target_pairs={{0,8},{8,0},{16,24},{24,16},{1,9},{9,1},{17,25},{25,17},{2,10},{10... | collective-permute-start | bytes 1179656 | tf_op jit(solution)/shard_map/ppermute | solution.py:626
  28.7 17.6 %collective-permute-start.3 = (f32[6,16,8,384]{3,2,1,0:T(8,128)S(1)}, f32[6,16,8,384]{3,2,1,0:T(8,128)S(1)}, u32[]{:S(2)}, u32[]{:S(2)}) collective-permute-start(f32[6,16,8,384]{3,2,1,0:T(8,128)S(1)} %get-tuple-element.32), channel_id=1, source_target_pairs={{1,2},{2,1},{3,4},{4,3},{5,6},{6,5},{9,10},{10,9},{11,12},{12,11},... | collective-permute-start | bytes 3538952 | tf_op jit(solution)/shard_map/ppermute | solution.py:608
  30.7 15.7 %collective-permute-start.4 = (f32[6,16,8,384]{3,2,1,0:T(8,128)S(1)}, f32[6,16,8,384]{3,2,1,0:T(8,128)S(1)}, u32[]{:S(2)}, u32[]{:S(2)}) collective-permute-start(f32[6,16,8,384]{3,2,1,0:T(8,128)S(1)} %get-tuple-element.33), channel_id=1, source_target_pairs={{0,1},{1,0},{2,3},{3,2},{4,5},{5,4},{6,7},{7,6},{8,9},{9,8},{10,11... | collective-permute-start | bytes 3538952 | tf_op jit(solution)/shard_map/ppermute | solution.py:609
  51.6 11.3 %collective-permute-start.8 = (f32[3,16,8,384]{3,2,1,0:T(8,128)S(1)}, f32[3,16,8,384]{3,2,1,0:T(8,128)S(1)}, u32[]{:S(2)}, u32[]{:S(2)}) collective-permute-start(f32[3,16,8,384]{3,2,1,0:T(8,128)S(1)} %get-tuple-element.41), channel_id=1, source_target_pairs={{1,2},{2,1},{3,4},{4,3},{5,6},{6,5},{9,10},{10,9},{11,12},{12,11},... | collective-permute-start | bytes 1769480 | tf_op jit(solution)/shard_map/ppermute | solution.py:608
  55.4 7.6 %collective-permute-start.9 = (f32[3,16,8,384]{3,2,1,0:T(8,128)S(1)}, f32[3,16,8,384]{3,2,1,0:T(8,128)S(1)}, u32[]{:S(2)}, u32[]{:S(2)}) collective-permute-start(f32[3,16,8,384]{3,2,1,0:T(8,128)S(1)} %get-tuple-element.42), channel_id=1, source_target_pairs={{0,1},{1,0},{2,3},{3,2},{4,5},{5,4},{6,7},{7,6},{8,9},{9,8},{10,11... | collective-permute-start | bytes 1769480 | tf_op jit(solution)/shard_map/ppermute | solution.py:609
  65.8 7.8 %collective-permute-start.10 = (f32[4,4,8,384]{3,2,1,0:T(8,128)S(1)}, f32[4,4,8,384]{3,2,1,0:T(8,128)S(1)}, u32[]{:S(2)}, u32[]{:S(2)}) collective-permute-start(f32[4,4,8,384]{3,2,1,0:T(8,128)S(1)} %get-tuple-element.44), channel_id=1, source_target_pairs={{0,8},{8,0},{16,24},{24,16},{1,9},{9,1},{17,25},{25,17},{2,10},{10... | collective-permute-start | bytes 589832 | tf_op jit(solution)/shard_map/ppermute | solution.py:626
  66.9 7.5 %collective-permute-start.11 = (f32[4,4,8,384]{3,2,1,0:T(8,128)S(1)}, f32[4,4,8,384]{3,2,1,0:T(8,128)S(1)}, u32[]{:S(2)}, u32[]{:S(2)}) collective-permute-start(f32[4,4,8,384]{3,2,1,0:T(8,128)S(1)} %get-tuple-element.45), channel_id=1, source_target_pairs={{0,16},{8,24},{16,0},{24,8},{1,17},{9,25},{17,1},{25,9},{2,18},{10... | collective-permute-start | bytes 589832 | tf_op jit(solution)/shard_map/ppermute | solution.py:626
  67.9 9.9 %collective-permute-start.12 = (f32[4,4,8,384]{3,2,1,0:T(8,128)S(1)}, f32[4,4,8,384]{3,2,1,0:T(8,128)S(1)}, u32[]{:S(2)}, u32[]{:S(2)}) collective-permute-start(f32[4,4,8,384]{3,2,1,0:T(8,128)S(1)} %get-tuple-element.46), channel_id=1, source_target_pairs={{0,24},{8,16},{16,8},{24,0},{1,25},{9,17},{17,9},{25,1},{2,26},{10... | collective-permute-start | bytes 589832 | tf_op jit(solution)/shard_map/ppermute | solution.py:626

commit v6 on v5

--- a/solution.py
+++ b/solution.py
@@ -602,6 +602,21 @@
     )(*args, *outside)
 
 
+def nothing_kernel(*refs):
+    pass
+
+
+def held_until(x, *after):
+    return pl.pallas_call(
+        nothing_kernel,
+        out_shape=jax.ShapeDtypeStruct(x.shape, x.dtype),
+        in_specs=[pl.BlockSpec(memory_space=pltpu.VMEM)] * (1 + len(after)),
+        out_specs=pl.BlockSpec(memory_space=pltpu.VMEM),
+        input_output_aliases={0: 0},
+        compiler_params=pltpu.CompilerParams(vmem_limit_bytes=16 * 2**20),
+    )(x, *after)
+
+
 def lat_exchange(edge_z, edge_c):
     count = lax.axis_size("lat")
     pairs = lambda start: [p for i in range(start, count - 1, 2) for p in ((i, i + 1), (i + 1, i))]
@@ -673,10 +688,11 @@
         partial(pack_both_kernel, tiles),
         [(2, rows * tiles, SUB, piece)],
         [east_t.shape, turned, pltpu.SemaphoreType.DMA((rows,))],
-        h_piece, *pieces[1:],
+        h_piece,
         outside=[east_t],
         us=PACK_US,
     )
+    both = held_until(both, *pieces[1:])
     both_pieces = gather(both)
     both_edge = (2 * HALO,) + full[1:]
     state, north, edge_z, edge_c = call(

time: 79.9 us -> 79.3 us (level)
  waiting for transfers between devices: 44 us -> 43 us
    ppermute x2, starting transfers between devices: 5.69 us -> 3.9 us  [lat_exchange(): from_z = lax.ppermute(edge_z, 'lat', pairs(1))]
    ppermute x2, starting transfers between devices: 1.82 us -> 3.43 us  [lat_exchange(): from_c = lax.ppermute(edge_c, 'lat', pairs(0))]
    ppermute x9, waiting for transfers between devices: 36.5 us -> 35.5 us  [on_device(): lax.ppermute(x, 'lon', [(i, i ^ s) for i in range(parts)])]
  transfers between devices with their start and end apart: 13 -> 13, of which waited for: 8 -> 8; matrix products, arithmetic and copies ran while one was open for 0% -> 0% of each run, Pallas kernels for 5% -> 6%
where the time goes in v6:
time: 79.3 us; the launch traced here: 78 us
  waiting for transfers between devices  43 us (54%)
  starting transfers between devices  17.9 us (23%)
  Pallas kernels  16.9 us (21%)
    ppermute x9, waiting for transfers between devices, on_device(): lax.ppermute(x, 'lon', [(i, i ^ s) for i in range(parts)])  35.5 us
    pallas_call x9, Pallas kernels, call(): pl.pallas_call(kernel, out_shape=[jax.ShapeDtypeStruct(s, f32) if isinsta...  16.9 us
    ppermute x9, starting transfers between devices, on_device(): lax.ppermute(x, 'lon', [(i, i ^ s) for i in range(parts)])  10.6 us
    ppermute x2, waiting for transfers between devices, lat_exchange(): from_z = lax.ppermute(edge_z, 'lat', pairs(1))  7.53 us
    ppermute x2, starting transfers between devices, lat_exchange(): from_z = lax.ppermute(edge_z, 'lat', pairs(1))  3.9 us
    ppermute x2, starting transfers between devices, lat_exchange(): from_c = lax.ppermute(edge_c, 'lat', pairs(0))  3.43 us
  transfers between devices with their start and end apart: 13, of which 8 were waited for; matrix products, arithmetic and copies ran while one was open for 0% of the time, Pallas kernels for 6%

profile of v6, /device:TPU:8, one launch (start us, length us, event | category | flops | bytes accessed | tf_op | source)
XLA Modules:
  0.0 78.0 jit_solution(17021092135474021004)
XLA Ops:
  0.0 2.7 %shard_map.82 = (f32[8,4,8,384]{3,2,1,0:T(8,128)S(1)}, f32[8,4,8,384]{3,2,1,0:T(8,128)S(1)}, f32[8,4,8,384]{3,2,1,0:T(8,128)S(1)}, f32[8,4,8,384]{3,2,1,0:T(8,128)S(1)}, f32[4,4,8,384]{3,2,1,0:T(8,128)S(1)}) custom-call(f32[4,360,128]{2,1,0:T(8,128)} %sens.1, f32[31,4,360]{2,1,0:T(4,128)} %bitcast.5, f32[4,32,360]{2,1,0:T(8,128)} %bitcast.3), custom_call_target="tpu_custom_call" | custom-call | flops 3000000000 | bytes 100000 | tf_op jit(solution)/shard_map/pallas_call | solution.py:594
  2.7 1.6 %collective-permute-start = (f32[8,4,8,384]{3,2,1,0:T(8,128)S(1)}, f32[8,4,8,384]{3,2,1,0:T(8,128)S(1)}, u32[]{:S(2)}, u32[]{:S(2)}) collective-permute-start(f32[8,4,8,384]{3,2,1,0:T(8,128)S(1)} %get-tuple-element.27), channel_id=1, source_target_pairs={{0,8},{8,0},{16,24},{24,16},{1,9},{9,1},{17,25},{25,17},{2,10},{10... | collective-permute-start | bytes 1179656 | tf_op jit(solution)/shard_map/ppermute | solution.py:641
  4.3 1.5 %collective-permute-start.1 = (f32[8,4,8,384]{3,2,1,0:T(8,128)S(1)}, f32[8,4,8,384]{3,2,1,0:T(8,128)S(1)}, u32[]{:S(2)}, u32[]{:S(2)}) collective-permute-start(f32[8,4,8,384]{3,2,1,0:T(8,128)S(1)} %get-tuple-element.28), channel_id=1, source_target_pairs={{0,16},{8,24},{16,0},{24,8},{1,17},{9,25},{17,1},{25,9},{2,18},{10... | collective-permute-start | bytes 1179656 | tf_op jit(solution)/shard_map/ppermute | solution.py:641
  5.8 0.5 collective-permute-start.2
  6.3 0.0 copy-start.1
  6.3 1.0 %shard_map.83.refs_0_ = f32[2,16,8,384]{3,2,1,0:T(8,128)S(1)} custom-call(f32[4,4,8,384]{3,2,1,0:T(8,128)S(1)} %get-tuple-element.30.h, f32[4,32,360]{2,1,0:T(8,128)} %bitcast.4), custom_call_target="tpu_custom_call" | custom-call | flops 500000000 | bytes 100000 | tf_op jit(solution)/shard_map/pallas_call | solution.py:594
  7.3 0.0 copy-start
  7.3 7.5 %collective-permute-done.refs_1_ = f32[8,4,8,384]{3,2,1,0:T(8,128)S(1)} collective-permute-done((f32[8,4,8,384]{3,2,1,0:T(8,128)S(1)}, f32[8,4,8,384]{3,2,1,0:T(8,128)S(1)}, u32[]{:S(2)}, u32[]{:S(2)}) %collective-permute-start) | collective-permute-done | bytes 393248 | tf_op jit(solution)/shard_map/ppermute | solution.py:641
  14.8 8.5 %collective-permute-done.1.refs_2_ = f32[8,4,8,384]{3,2,1,0:T(8,128)S(1)} collective-permute-done((f32[8,4,8,384]{3,2,1,0:T(8,128)S(1)}, f32[8,4,8,384]{3,2,1,0:T(8,128)S(1)}, u32[]{:S(2)}, u32[]{:S(2)}) %collective-permute-start.1) | collective-permute-done | bytes 393248 | tf_op jit(solution)/shard_map/ppermute | solution.py:641
  23.3 0.0 collective-permute-done.2.refs_3_
  23.3 1.5 %collective-permute-start.7 = (f32[2,16,8,384]{3,2,1,0:T(8,128)S(1)}, f32[2,16,8,384]{3,2,1,0:T(8,128)S(1)}, u32[]{:S(2)}, u32[]{:S(2)}) collective-permute-start(f32[2,16,8,384]{3,2,1,0:T(8,128)S(1)} %shard_map.84.refs_6_.refs_0_), channel_id=1, source_target_pairs={{0,24},{8,16},{16,8},{24,0},{1,25},{9,17},{17,9},{25,1},{2,26},{10... | collective-permute-start | bytes 1179656 | tf_op jit(solution)/shard_map/ppermute | solution.py:641
  24.8 1.2 %collective-permute-start.6 = (f32[2,16,8,384]{3,2,1,0:T(8,128)S(1)}, f32[2,16,8,384]{3,2,1,0:T(8,128)S(1)}, u32[]{:S(2)}, u32[]{:S(2)}) collective-permute-start(f32[2,16,8,384]{3,2,1,0:T(8,128)S(1)} %shard_map.84.refs_6_.refs_0_), channel_id=1, source_target_pairs={{0,16},{8,24},{16,0},{24,8},{1,17},{9,25},{17,1},{25,9},{2,18},{10... | collective-permute-start | bytes 1179656 | tf_op jit(solution)/shard_map/ppermute | solution.py:641
  26.0 0.8 %collective-permute-start.5 = (f32[2,16,8,384]{3,2,1,0:T(8,128)S(1)}, f32[2,16,8,384]{3,2,1,0:T(8,128)S(1)}, u32[]{:S(2)}, u32[]{:S(2)}) collective-permute-start(f32[2,16,8,384]{3,2,1,0:T(8,128)S(1)} %shard_map.84.refs_6_.refs_0_), channel_id=1, source_target_pairs={{0,8},{8,0},{16,24},{24,16},{1,9},{9,1},{17,25},{25,17},{2,10},{10... | collective-permute-start | bytes 1179656 | tf_op jit(solution)/shard_map/ppermute | solution.py:641
  26.8 0.0 copy-done.1
  26.8 0.0 copy-done
  26.8 0.8 %shard_map.85 = (f32[4,16,8,384]{3,2,1,0:T(8,128)S(1)}, f32[4,16,8,384]{3,2,1,0:T(8,128)S(1)}, f32[6,16,8,384]{3,2,1,0:T(8,128)S(1)}, f32[6,16,8,384]{3,2,1,0:T(8,128)S(1)}) custom-call(f32[8,4,8,384]{3,2,1,0:T(8,128)S(1)} %get-tuple-element.26.refs_0_, f32[8,4,8,384]{3,2,1,0:T(8,128)S(1)} %collective-permute-done.refs_1_, ...), custom_call_target="tpu_custom_call" | custom-call | flops 2500000000 | bytes 100000 | tf_op jit(solution)/shard_map/pallas_call | solution.py:594
  27.6 1.9 %collective-permute-start.3 = (f32[6,16,8,384]{3,2,1,0:T(8,128)S(1)}, f32[6,16,8,384]{3,2,1,0:T(8,128)S(1)}, u32[]{:S(2)}, u32[]{:S(2)}) collective-permute-start(f32[6,16,8,384]{3,2,1,0:T(8,128)S(1)} %get-tuple-element.32), channel_id=1, source_target_pairs={{1,2},{2,1},{3,4},{4,3},{5,6},{6,5},{9,10},{10,9},{11,12},{12,11},... | collective-permute-start | bytes 3538952 | tf_op jit(solution)/shard_map/ppermute | solution.py:623
  29.6 1.7 %collective-permute-start.4 = (f32[6,16,8,384]{3,2,1,0:T(8,128)S(1)}, f32[6,16,8,384]{3,2,1,0:T(8,128)S(1)}, u32[]{:S(2)}, u32[]{:S(2)}) collective-permute-start(f32[6,16,8,384]{3,2,1,0:T(8,128)S(1)} %get-tuple-element.33), channel_id=1, source_target_pairs={{0,1},{1,0},{2,3},{3,2},{4,5},{5,4},{6,7},{7,6},{8,9},{9,8},{10,11... | collective-permute-start | bytes 3538952 | tf_op jit(solution)/shard_map/ppermute | solution.py:624
  31.3 4.9 %collective-permute-done.7.refs_3_ = f32[2,16,8,384]{3,2,1,0:T(8,128)S(1)} collective-permute-done((f32[2,16,8,384]{3,2,1,0:T(8,128)S(1)}, f32[2,16,8,384]{3,2,1,0:T(8,128)S(1)}, u32[]{:S(2)}, u32[]{:S(2)}) %collective-permute-start.7) | collective-permute-done | bytes 393248 | tf_op jit(solution)/shard_map/ppermute | solution.py:641
  36.3 6.1 %collective-permute-done.6.refs_2_ = f32[2,16,8,384]{3,2,1,0:T(8,128)S(1)} collective-permute-done((f32[2,16,8,384]{3,2,1,0:T(8,128)S(1)}, f32[2,16,8,384]{3,2,1,0:T(8,128)S(1)}, u32[]{:S(2)}, u32[]{:S(2)}) %collective-permute-start.6) | collective-permute-done | bytes 393248 | tf_op jit(solution)/shard_map/ppermute | solution.py:641
  42.4 0.0 collective-permute-done.5.refs_1_
  42.4 0.5 shard_map.88
  42.9 2.3 %shard_map.87.east = f32[7,4,16,8,384]{4,3,2,1,0:T(8,128)S(1)} custom-call(f32[2,16,8,384]{3,2,1,0:T(8,128)S(1)} %shard_map.84.refs_6_.refs_0_, f32[2,16,8,384]{3,2,1,0:T(8,128)S(1)} %collective-permute-done.5.refs_1_, f32[2,16,8,384]{3,2,1,0:T(8,128)S(1)} %collective-permute-done.6.refs_2_, f32[2,16,8,384]{3,2,1,0:T(8,128)S(1)} %collective-permute-done.7.refs_3_), custom_call_target="tpu_custom_call" | custom-call | flops 10000000000 | bytes 100000 | tf_op jit(solution)/shard_map/pallas_call | solution.py:594
  45.3 0.0 collective-permute-done.3.from_z
  45.3 0.0 collective-permute-done.4.from_c
  45.3 1.5 %shard_map.86 = (f32[7,4,16,8,384]{4,3,2,1,0:T(8,128)S(1)}, f32[3,16,8,384]{3,2,1,0:T(8,128)S(1)}) custom-call(f32[4,16,8,384]{3,2,1,0:T(8,128)S(1)} %get-tuple-element.34.north, f32[6,16,8,384]{3,2,1,0:T(8,128)S(1)} %collective-permute-done.3.from_z, f32[6,16,8,384]{3,2,1,0:T(8,128)S(1)} %collective-permute-done.4.from_c), custom_call_target="tpu_custom_call" | custom-call | flops 1500000000 | bytes 100000 | tf_op jit(solution)/shard_map/pallas_call | solution.py:594
  46.8 3.7 %shard_map.89 = (f32[4,16,8,384]{3,2,1,0:T(8,128)S(1)}, f32[3,16,8,384]{3,2,1,0:T(8,128)S(1)}, f32[3,16,8,384]{3,2,1,0:T(8,128)S(1)}) custom-call(f32[4,16,8,384]{3,2,1,0:T(8,128)S(1)} %get-tuple-element.31.field, f32[6,16,8,384]{3,2,1,0:T(8,128)S(1)} %collective-permute-done.3.from_z, f32[6,16,8,384]{3,2,1,0:T(8,128)S(1)} %collective-permute-done.4.from_c, ...), custom_call_target="tpu_custom_call" | custom-call | flops 6000000000 | bytes 100000 | tf_op jit(solution)/shard_map/pallas_call | solution.py:594
  50.5 2.0 %collective-permute-start.8 = (f32[3,16,8,384]{3,2,1,0:T(8,128)S(1)}, f32[3,16,8,384]{3,2,1,0:T(8,128)S(1)}, u32[]{:S(2)}, u32[]{:S(2)}) collective-permute-start(f32[3,16,8,384]{3,2,1,0:T(8,128)S(1)} %get-tuple-element.41), channel_id=1, source_target_pairs={{1,2},{2,1},{3,4},{4,3},{5,6},{6,5},{9,10},{10,9},{11,12},{12,11},... | collective-permute-start | bytes 1769480 | tf_op jit(solution)/shard_map/ppermute | solution.py:623
  52.5 1.7 %collective-permute-start.9 = (f32[3,16,8,384]{3,2,1,0:T(8,128)S(1)}, f32[3,16,8,384]{3,2,1,0:T(8,128)S(1)}, u32[]{:S(2)}, u32[]{:S(2)}) collective-permute-start(f32[3,16,8,384]{3,2,1,0:T(8,128)S(1)} %get-tuple-element.42), channel_id=1, source_target_pairs={{0,1},{1,0},{2,3},{3,2},{4,5},{5,4},{6,7},{7,6},{8,9},{9,8},{10,11... | collective-permute-start | bytes 1769480 | tf_op jit(solution)/shard_map/ppermute | solution.py:624
  54.2 7.5 %collective-permute-done.8.from_z = f32[3,16,8,384]{3,2,1,0:T(8,128)S(1)} collective-permute-done((f32[3,16,8,384]{3,2,1,0:T(8,128)S(1)}, f32[3,16,8,384]{3,2,1,0:T(8,128)S(1)}, u32[]{:S(2)}, u32[]{:S(2)}) %collective-permute-start.8) | collective-permute-done | bytes 589856 | tf_op jit(solution)/shard_map/ppermute | solution.py:623
  61.7 0.0 collective-permute-done.9.from_c
  61.7 2.9 %shard_map.90 = (f32[4,4,8,384]{3,2,1,0:T(8,128)S(1)}, f32[4,4,8,384]{3,2,1,0:T(8,128)S(1)}, f32[4,4,8,384]{3,2,1,0:T(8,128)S(1)}, f32[4,4,8,384]{3,2,1,0:T(8,128)S(1)}) custom-call(f32[4,16,8,384]{3,2,1,0:T(8,128)S(1)} %get-tuple-element.40.field, f32[3,16,8,384]{3,2,1,0:T(8,128)S(1)} %collective-permute-done.8.from_z, ...), custom_call_target="tpu_custom_call" | custom-call | flops 3500000000 | bytes 100000 | tf_op jit(solution)/shard_map/pallas_call | solution.py:594
  64.6 1.1 %collective-permute-start.10 = (f32[4,4,8,384]{3,2,1,0:T(8,128)S(1)}, f32[4,4,8,384]{3,2,1,0:T(8,128)S(1)}, u32[]{:S(2)}, u32[]{:S(2)}) collective-permute-start(f32[4,4,8,384]{3,2,1,0:T(8,128)S(1)} %get-tuple-element.44), channel_id=1, source_target_pairs={{0,8},{8,0},{16,24},{24,16},{1,9},{9,1},{17,25},{25,17},{2,10},{10... | collective-permute-start | bytes 589832 | tf_op jit(solution)/shard_map/ppermute | solution.py:641
  65.7 1.0 %collective-permute-start.11 = (f32[4,4,8,384]{3,2,1,0:T(8,128)S(1)}, f32[4,4,8,384]{3,2,1,0:T(8,128)S(1)}, u32[]{:S(2)}, u32[]{:S(2)}) collective-permute-start(f32[4,4,8,384]{3,2,1,0:T(8,128)S(1)} %get-tuple-element.45), channel_id=1, source_target_pairs={{0,16},{8,24},{16,0},{24,8},{1,17},{9,25},{17,1},{25,9},{2,18},{10... | collective-permute-start | bytes 589832 | tf_op jit(solution)/shard_map/ppermute | solution.py:641
  66.7 1.4 %collective-permute-start.12 = (f32[4,4,8,384]{3,2,1,0:T(8,128)S(1)}, f32[4,4,8,384]{3,2,1,0:T(8,128)S(1)}, u32[]{:S(2)}, u32[]{:S(2)}) collective-permute-start(f32[4,4,8,384]{3,2,1,0:T(8,128)S(1)} %get-tuple-element.46), channel_id=1, source_target_pairs={{0,24},{8,16},{16,8},{24,0},{1,25},{9,17},{17,9},{25,1},{2,26},{10... | collective-permute-start | bytes 589832 | tf_op jit(solution)/shard_map/ppermute | solution.py:641
  68.1 4.3 %collective-permute-done.10.refs_1_ = f32[4,4,8,384]{3,2,1,0:T(8,128)S(1)} collective-permute-done((f32[4,4,8,384]{3,2,1,0:T(8,128)S(1)}, f32[4,4,8,384]{3,2,1,0:T(8,128)S(1)}, u32[]{:S(2)}, u32[]{:S(2)}) %collective-permute-start.10) | collective-permute-done | bytes 196640 | tf_op jit(solution)/shard_map/ppermute | solution.py:641
  72.4 2.7 %collective-permute-done.11.refs_2_ = f32[4,4,8,384]{3,2,1,0:T(8,128)S(1)} collective-permute-done((f32[4,4,8,384]{3,2,1,0:T(8,128)S(1)}, f32[4,4,8,384]{3,2,1,0:T(8,128)S(1)}, u32[]{:S(2)}, u32[]{:S(2)}) %collective-permute-start.11) | collective-permute-done | bytes 196640 | tf_op jit(solution)/shard_map/ppermute | solution.py:641
  75.1 1.5 %collective-permute-done.12.refs_3_ = f32[4,4,8,384]{3,2,1,0:T(8,128)S(1)} collective-permute-done((f32[4,4,8,384]{3,2,1,0:T(8,128)S(1)}, f32[4,4,8,384]{3,2,1,0:T(8,128)S(1)}, u32[]{:S(2)}, u32[]{:S(2)}) %collective-permute-start.12) | collective-permute-done | bytes 196640 | tf_op jit(solution)/shard_map/ppermute | solution.py:641
  76.6 1.4 %shard_map.91 = f32[4,360,128]{2,1,0:T(8,128)} custom-call(f32[4,4,8,384]{3,2,1,0:T(8,128)S(1)} %get-tuple-element.43.refs_0_, f32[4,4,8,384]{3,2,1,0:T(8,128)S(1)} %collective-permute-done.10.refs_1_, f32[4,4,8,384]{3,2,1,0:T(8,128)S(1)} %collective-permute-done.11.refs_2_, f32[4,4,8,384]{3,2,1,0:T(8,128)S(1)} %collective-permute-done.12.refs_3_), custom_call_target="tpu_custom_call" | custom-call | flops 1000000000 | bytes 100000 | tf_op jit(solution)/shard_map/pallas_call | solution.py:594
  (1 shorter events, 0.0 us)
Async XLA Ops:
  2.7 12.1 %collective-permute-start = (f32[8,4,8,384]{3,2,1,0:T(8,128)S(1)}, f32[8,4,8,384]{3,2,1,0:T(8,128)S(1)}, u32[]{:S(2)}, u32[]{:S(2)}) collective-permute-start(f32[8,4,8,384]{3,2,1,0:T(8,128)S(1)} %get-tuple-element.27), channel_id=1, source_target_pairs={{0,8},{8,0},{16,24},{24,16},{1,9},{9,1},{17,25},{25,17},{2,10},{10... | collective-permute-start | bytes 1179656 | tf_op jit(solution)/shard_map/ppermute | solution.py:641
  4.3 19.0 %collective-permute-start.1 = (f32[8,4,8,384]{3,2,1,0:T(8,128)S(1)}, f32[8,4,8,384]{3,2,1,0:T(8,128)S(1)}, u32[]{:S(2)}, u32[]{:S(2)}) collective-permute-start(f32[8,4,8,384]{3,2,1,0:T(8,128)S(1)} %get-tuple-element.28), channel_id=1, source_target_pairs={{0,16},{8,24},{16,0},{24,8},{1,17},{9,25},{17,1},{25,9},{2,18},{10... | collective-permute-start | bytes 1179656 | tf_op jit(solution)/shard_map/ppermute | solution.py:641
  5.8 17.5 %collective-permute-start.2 = (f32[8,4,8,384]{3,2,1,0:T(8,128)S(1)}, f32[8,4,8,384]{3,2,1,0:T(8,128)S(1)}, u32[]{:S(2)}, u32[]{:S(2)}) collective-permute-start(f32[8,4,8,384]{3,2,1,0:T(8,128)S(1)} %get-tuple-element.29), channel_id=1, source_target_pairs={{0,24},{8,16},{16,8},{24,0},{1,25},{9,17},{17,9},{25,1},{2,26},{10... | collective-permute-start | bytes 1179656 | tf_op jit(solution)/shard_map/ppermute | solution.py:641
  6.3 20.5 %copy-start.1 = (bf16[2,768,384]{2,1,0:T(8,128)(2,1)S(1)}, bf16[2,768,384]{2,1,0:T(8,128)(2,1)}, u32[]{:S(2)}) copy-start(bf16[2,768,384]{2,1,0:T(8,128)(2,1)} %constant.4.clone.refs_4_.refs_0_) | copy-start | bytes 3538948
  7.3 19.5 %copy-start = (bf16[2,768,384]{2,1,0:T(8,128)(2,1)S(1)}, bf16[2,768,384]{2,1,0:T(8,128)(2,1)}, u32[]{:S(2)}) copy-start(bf16[2,768,384]{2,1,0:T(8,128)(2,1)} %constant.5.clone.refs_5_.refs_1_) | copy-start | bytes 3538948
  23.3 13.0 %collective-permute-start.7 = (f32[2,16,8,384]{3,2,1,0:T(8,128)S(1)}, f32[2,16,8,384]{3,2,1,0:T(8,128)S(1)}, u32[]{:S(2)}, u32[]{:S(2)}) collective-permute-start(f32[2,16,8,384]{3,2,1,0:T(8,128)S(1)} %shard_map.84.refs_6_.refs_0_), channel_id=1, source_target_pairs={{0,24},{8,16},{16,8},{24,0},{1,25},{9,17},{17,9},{25,1},{2,26},{10... | collective-permute-start | bytes 1179656 | tf_op jit(solution)/shard_map/ppermute | solution.py:641
  24.8 17.6 %collective-permute-start.6 = (f32[2,16,8,384]{3,2,1,0:T(8,128)S(1)}, f32[2,16,8,384]{3,2,1,0:T(8,128)S(1)}, u32[]{:S(2)}, u32[]{:S(2)}) collective-permute-start(f32[2,16,8,384]{3,2,1,0:T(8,128)S(1)} %shard_map.84.refs_6_.refs_0_), channel_id=1, source_target_pairs={{0,16},{8,24},{16,0},{24,8},{1,17},{9,25},{17,1},{25,9},{2,18},{10... | collective-permute-start | bytes 1179656 | tf_op jit(solution)/shard_map/ppermute | solution.py:641
  26.0 16.4 %collective-permute-start.5 = (f32[2,16,8,384]{3,2,1,0:T(8,128)S(1)}, f32[2,16,8,384]{3,2,1,0:T(8,128)S(1)}, u32[]{:S(2)}, u32[]{:S(2)}) collective-permute-start(f32[2,16,8,384]{3,2,1,0:T(8,128)S(1)} %shard_map.84.refs_6_.refs_0_), channel_id=1, source_target_pairs={{0,8},{8,0},{16,24},{24,16},{1,9},{9,1},{17,25},{25,17},{2,10},{10... | collective-permute-start | bytes 1179656 | tf_op jit(solution)/shard_map/ppermute | solution.py:641
  27.6 17.6 %collective-permute-start.3 = (f32[6,16,8,384]{3,2,1,0:T(8,128)S(1)}, f32[6,16,8,384]{3,2,1,0:T(8,128)S(1)}, u32[]{:S(2)}, u32[]{:S(2)}) collective-permute-start(f32[6,16,8,384]{3,2,1,0:T(8,128)S(1)} %get-tuple-element.32), channel_id=1, source_target_pairs={{1,2},{2,1},{3,4},{4,3},{5,6},{6,5},{9,10},{10,9},{11,12},{12,11},... | collective-permute-start | bytes 3538952 | tf_op jit(solution)/shard_map/ppermute | solution.py:623
  29.6 15.7 %collective-permute-start.4 = (f32[6,16,8,384]{3,2,1,0:T(8,128)S(1)}, f32[6,16,8,384]{3,2,1,0:T(8,128)S(1)}, u32[]{:S(2)}, u32[]{:S(2)}) collective-permute-start(f32[6,16,8,384]{3,2,1,0:T(8,128)S(1)} %get-tuple-element.33), channel_id=1, source_target_pairs={{0,1},{1,0},{2,3},{3,2},{4,5},{5,4},{6,7},{7,6},{8,9},{9,8},{10,11... | collective-permute-start | bytes 3538952 | tf_op jit(solution)/shard_map/ppermute | solution.py:624
  50.5 11.2 %collective-permute-start.8 = (f32[3,16,8,384]{3,2,1,0:T(8,128)S(1)}, f32[3,16,8,384]{3,2,1,0:T(8,128)S(1)}, u32[]{:S(2)}, u32[]{:S(2)}) collective-permute-start(f32[3,16,8,384]{3,2,1,0:T(8,128)S(1)} %get-tuple-element.41), channel_id=1, source_target_pairs={{1,2},{2,1},{3,4},{4,3},{5,6},{6,5},{9,10},{10,9},{11,12},{12,11},... | collective-permute-start | bytes 1769480 | tf_op jit(solution)/shard_map/ppermute | solution.py:623
  52.5 9.2 %collective-permute-start.9 = (f32[3,16,8,384]{3,2,1,0:T(8,128)S(1)}, f32[3,16,8,384]{3,2,1,0:T(8,128)S(1)}, u32[]{:S(2)}, u32[]{:S(2)}) collective-permute-start(f32[3,16,8,384]{3,2,1,0:T(8,128)S(1)} %get-tuple-element.42), channel_id=1, source_target_pairs={{0,1},{1,0},{2,3},{3,2},{4,5},{5,4},{6,7},{7,6},{8,9},{9,8},{10,11... | collective-permute-start | bytes 1769480 | tf_op jit(solution)/shard_map/ppermute | solution.py:624
  64.6 7.8 %collective-permute-start.10 = (f32[4,4,8,384]{3,2,1,0:T(8,128)S(1)}, f32[4,4,8,384]{3,2,1,0:T(8,128)S(1)}, u32[]{:S(2)}, u32[]{:S(2)}) collective-permute-start(f32[4,4,8,384]{3,2,1,0:T(8,128)S(1)} %get-tuple-element.44), channel_id=1, source_target_pairs={{0,8},{8,0},{16,24},{24,16},{1,9},{9,1},{17,25},{25,17},{2,10},{10... | collective-permute-start | bytes 589832 | tf_op jit(solution)/shard_map/ppermute | solution.py:641
  65.7 9.4 %collective-permute-start.11 = (f32[4,4,8,384]{3,2,1,0:T(8,128)S(1)}, f32[4,4,8,384]{3,2,1,0:T(8,128)S(1)}, u32[]{:S(2)}, u32[]{:S(2)}) collective-permute-start(f32[4,4,8,384]{3,2,1,0:T(8,128)S(1)} %get-tuple-element.45), channel_id=1, source_target_pairs={{0,16},{8,24},{16,0},{24,8},{1,17},{9,25},{17,1},{25,9},{2,18},{10... | collective-permute-start | bytes 589832 | tf_op jit(solution)/shard_map/ppermute | solution.py:641
  66.7 9.9 %collective-permute-start.12 = (f32[4,4,8,384]{3,2,1,0:T(8,128)S(1)}, f32[4,4,8,384]{3,2,1,0:T(8,128)S(1)}, u32[]{:S(2)}, u32[]{:S(2)}) collective-permute-start(f32[4,4,8,384]{3,2,1,0:T(8,128)S(1)} %get-tuple-element.46), channel_id=1, source_target_pairs={{0,24},{8,16},{16,8},{24,0},{1,25},{9,17},{17,9},{25,1},{2,26},{10... | collective-permute-start | bytes 589832 | tf_op jit(solution)/shard_map/ppermute | solution.py:641

commit v7 on v6

--- a/solution.py
+++ b/solution.py
@@ -715,7 +715,7 @@
         us=10.0,
     )
     north, ghosts = call(
-        north_factor_kernel, [(2 * HALO + 1,) + full, (3,) + full[1:]], [], north, *edges, us=1.5
+        north_factor_kernel, [(2 * HALO + 1,) + full, (3,) + full[1:]], [], north, *edges, us=0.2
     )
     for substep in range(SUBSTEPS - 1):
         state, edge_z, edge_c = call(

time: 79.3 us -> 79.3 us (level)
    ppermute x2, starting transfers between devices: 3.9 us -> 5.68 us  [lat_exchange(): from_z = lax.ppermute(edge_z, 'lat', pairs(1))]
    ppermute x2, starting transfers between devices: 3.43 us -> 1.82 us  [lat_exchange(): from_c = lax.ppermute(edge_c, 'lat', pairs(0))]
where the time goes in v7:
time: 79.3 us; the launch traced here: 78.1 us
  waiting for transfers between devices  42.9 us (54%)
  starting transfers between devices  18.1 us (23%)
  Pallas kernels  16.9 us (21%)
    ppermute x9, waiting for transfers between devices, on_device(): lax.ppermute(x, 'lon', [(i, i ^ s) for i in range(parts)])  35.5 us
    pallas_call x9, Pallas kernels, call(): pl.pallas_call(kernel, out_shape=[jax.ShapeDtypeStruct(s, f32) if isinsta...  16.9 us
    ppermute x9, starting transfers between devices, on_device(): lax.ppermute(x, 'lon', [(i, i ^ s) for i in range(parts)])  10.6 us
    ppermute x2, waiting for transfers between devices, lat_exchange(): from_z = lax.ppermute(edge_z, 'lat', pairs(1))  7.48 us
    ppermute x2, starting transfers between devices, lat_exchange(): from_z = lax.ppermute(edge_z, 'lat', pairs(1))  5.68 us
    ppermute x2, starting transfers between devices, lat_exchange(): from_c = lax.ppermute(edge_c, 'lat', pairs(0))  1.82 us
  transfers between devices with their start and end apart: 13, of which 8 were waited for; matrix products, arithmetic and copies ran while one was open for 0% of the time, Pallas kernels for 6%

profile of v7, /device:TPU:8, one launch (start us, length us, event | category | flops | bytes accessed | tf_op | source)
XLA Modules:
  0.0 78.1 jit_solution(12527815186413785779)
XLA Ops:
  0.0 2.7 %shard_map.82 = (f32[8,4,8,384]{3,2,1,0:T(8,128)S(1)}, f32[8,4,8,384]{3,2,1,0:T(8,128)S(1)}, f32[8,4,8,384]{3,2,1,0:T(8,128)S(1)}, f32[8,4,8,384]{3,2,1,0:T(8,128)S(1)}, f32[4,4,8,384]{3,2,1,0:T(8,128)S(1)}) custom-call(f32[4,360,128]{2,1,0:T(8,128)} %sens.1, f32[31,4,360]{2,1,0:T(4,128)} %bitcast.5, f32[4,32,360]{2,1,0:T(8,128)} %bitcast.3), custom_call_target="tpu_custom_call" | custom-call | flops 3000000000 | bytes 100000 | tf_op jit(solution)/shard_map/pallas_call | solution.py:594
  2.7 1.6 %collective-permute-start = (f32[8,4,8,384]{3,2,1,0:T(8,128)S(1)}, f32[8,4,8,384]{3,2,1,0:T(8,128)S(1)}, u32[]{:S(2)}, u32[]{:S(2)}) collective-permute-start(f32[8,4,8,384]{3,2,1,0:T(8,128)S(1)} %get-tuple-element.27), channel_id=1, source_target_pairs={{0,8},{8,0},{16,24},{24,16},{1,9},{9,1},{17,25},{25,17},{2,10},{10... | collective-permute-start | bytes 1179656 | tf_op jit(solution)/shard_map/ppermute | solution.py:641
  4.3 1.5 %collective-permute-start.1 = (f32[8,4,8,384]{3,2,1,0:T(8,128)S(1)}, f32[8,4,8,384]{3,2,1,0:T(8,128)S(1)}, u32[]{:S(2)}, u32[]{:S(2)}) collective-permute-start(f32[8,4,8,384]{3,2,1,0:T(8,128)S(1)} %get-tuple-element.28), channel_id=1, source_target_pairs={{0,16},{8,24},{16,0},{24,8},{1,17},{9,25},{17,1},{25,9},{2,18},{10... | collective-permute-start | bytes 1179656 | tf_op jit(solution)/shard_map/ppermute | solution.py:641
  5.8 0.5 collective-permute-start.2
  6.3 0.0 copy-start.1
  6.3 1.0 %shard_map.83.refs_0_ = f32[2,16,8,384]{3,2,1,0:T(8,128)S(1)} custom-call(f32[4,4,8,384]{3,2,1,0:T(8,128)S(1)} %get-tuple-element.30.h, f32[4,32,360]{2,1,0:T(8,128)} %bitcast.4), custom_call_target="tpu_custom_call" | custom-call | flops 500000000 | bytes 100000 | tf_op jit(solution)/shard_map/pallas_call | solution.py:594
  7.3 0.0 copy-start
  7.3 7.5 %collective-permute-done.refs_1_ = f32[8,4,8,384]{3,2,1,0:T(8,128)S(1)} collective-permute-done((f32[8,4,8,384]{3,2,1,0:T(8,128)S(1)}, f32[8,4,8,384]{3,2,1,0:T(8,128)S(1)}, u32[]{:S(2)}, u32[]{:S(2)}) %collective-permute-start) | collective-permute-done | bytes 393248 | tf_op jit(solution)/shard_map/ppermute | solution.py:641
  14.8 8.5 %collective-permute-done.1.refs_2_ = f32[8,4,8,384]{3,2,1,0:T(8,128)S(1)} collective-permute-done((f32[8,4,8,384]{3,2,1,0:T(8,128)S(1)}, f32[8,4,8,384]{3,2,1,0:T(8,128)S(1)}, u32[]{:S(2)}, u32[]{:S(2)}) %collective-permute-start.1) | collective-permute-done | bytes 393248 | tf_op jit(solution)/shard_map/ppermute | solution.py:641
  23.3 0.0 collective-permute-done.2.refs_3_
  23.3 1.5 %collective-permute-start.7 = (f32[2,16,8,384]{3,2,1,0:T(8,128)S(1)}, f32[2,16,8,384]{3,2,1,0:T(8,128)S(1)}, u32[]{:S(2)}, u32[]{:S(2)}) collective-permute-start(f32[2,16,8,384]{3,2,1,0:T(8,128)S(1)} %shard_map.84.refs_6_.refs_0_), channel_id=1, source_target_pairs={{0,24},{8,16},{16,8},{24,0},{1,25},{9,17},{17,9},{25,1},{2,26},{10... | collective-permute-start | bytes 1179656 | tf_op jit(solution)/shard_map/ppermute | solution.py:641
  24.8 1.2 %collective-permute-start.6 = (f32[2,16,8,384]{3,2,1,0:T(8,128)S(1)}, f32[2,16,8,384]{3,2,1,0:T(8,128)S(1)}, u32[]{:S(2)}, u32[]{:S(2)}) collective-permute-start(f32[2,16,8,384]{3,2,1,0:T(8,128)S(1)} %shard_map.84.refs_6_.refs_0_), channel_id=1, source_target_pairs={{0,16},{8,24},{16,0},{24,8},{1,17},{9,25},{17,1},{25,9},{2,18},{10... | collective-permute-start | bytes 1179656 | tf_op jit(solution)/shard_map/ppermute | solution.py:641
  26.0 0.8 %collective-permute-start.5 = (f32[2,16,8,384]{3,2,1,0:T(8,128)S(1)}, f32[2,16,8,384]{3,2,1,0:T(8,128)S(1)}, u32[]{:S(2)}, u32[]{:S(2)}) collective-permute-start(f32[2,16,8,384]{3,2,1,0:T(8,128)S(1)} %shard_map.84.refs_6_.refs_0_), channel_id=1, source_target_pairs={{0,8},{8,0},{16,24},{24,16},{1,9},{9,1},{17,25},{25,17},{2,10},{10... | collective-permute-start | bytes 1179656 | tf_op jit(solution)/shard_map/ppermute | solution.py:641
  26.8 0.0 copy-done.1
  26.8 0.0 copy-done
  26.8 0.8 %shard_map.85 = (f32[4,16,8,384]{3,2,1,0:T(8,128)S(1)}, f32[4,16,8,384]{3,2,1,0:T(8,128)S(1)}, f32[6,16,8,384]{3,2,1,0:T(8,128)S(1)}, f32[6,16,8,384]{3,2,1,0:T(8,128)S(1)}) custom-call(f32[8,4,8,384]{3,2,1,0:T(8,128)S(1)} %get-tuple-element.26.refs_0_, f32[8,4,8,384]{3,2,1,0:T(8,128)S(1)} %collective-permute-done.refs_1_, ...), custom_call_target="tpu_custom_call" | custom-call | flops 2500000000 | bytes 100000 | tf_op jit(solution)/shard_map/pallas_call | solution.py:594
  27.6 1.9 %collective-permute-start.3 = (f32[6,16,8,384]{3,2,1,0:T(8,128)S(1)}, f32[6,16,8,384]{3,2,1,0:T(8,128)S(1)}, u32[]{:S(2)}, u32[]{:S(2)}) collective-permute-start(f32[6,16,8,384]{3,2,1,0:T(8,128)S(1)} %get-tuple-element.32), channel_id=1, source_target_pairs={{1,2},{2,1},{3,4},{4,3},{5,6},{6,5},{9,10},{10,9},{11,12},{12,11},... | collective-permute-start | bytes 3538952 | tf_op jit(solution)/shard_map/ppermute | solution.py:623
  29.6 1.7 %collective-permute-start.4 = (f32[6,16,8,384]{3,2,1,0:T(8,128)S(1)}, f32[6,16,8,384]{3,2,1,0:T(8,128)S(1)}, u32[]{:S(2)}, u32[]{:S(2)}) collective-permute-start(f32[6,16,8,384]{3,2,1,0:T(8,128)S(1)} %get-tuple-element.33), channel_id=1, source_target_pairs={{0,1},{1,0},{2,3},{3,2},{4,5},{5,4},{6,7},{7,6},{8,9},{9,8},{10,11... | collective-permute-start | bytes 3538952 | tf_op jit(solution)/shard_map/ppermute | solution.py:624
  31.3 4.9 %collective-permute-done.7.refs_3_ = f32[2,16,8,384]{3,2,1,0:T(8,128)S(1)} collective-permute-done((f32[2,16,8,384]{3,2,1,0:T(8,128)S(1)}, f32[2,16,8,384]{3,2,1,0:T(8,128)S(1)}, u32[]{:S(2)}, u32[]{:S(2)}) %collective-permute-start.7) | collective-permute-done | bytes 393248 | tf_op jit(solution)/shard_map/ppermute | solution.py:641
  36.3 6.1 %collective-permute-done.6.refs_2_ = f32[2,16,8,384]{3,2,1,0:T(8,128)S(1)} collective-permute-done((f32[2,16,8,384]{3,2,1,0:T(8,128)S(1)}, f32[2,16,8,384]{3,2,1,0:T(8,128)S(1)}, u32[]{:S(2)}, u32[]{:S(2)}) %collective-permute-start.6) | collective-permute-done | bytes 393248 | tf_op jit(solution)/shard_map/ppermute | solution.py:641
  42.4 0.0 collective-permute-done.5.refs_1_
  42.4 0.5 shard_map.88
  42.9 2.3 %shard_map.87.east = f32[7,4,16,8,384]{4,3,2,1,0:T(8,128)S(1)} custom-call(f32[2,16,8,384]{3,2,1,0:T(8,128)S(1)} %shard_map.84.refs_6_.refs_0_, f32[2,16,8,384]{3,2,1,0:T(8,128)S(1)} %collective-permute-done.5.refs_1_, f32[2,16,8,384]{3,2,1,0:T(8,128)S(1)} %collective-permute-done.6.refs_2_, f32[2,16,8,384]{3,2,1,0:T(8,128)S(1)} %collective-permute-done.7.refs_3_), custom_call_target="tpu_custom_call" | custom-call | flops 10000000000 | bytes 100000 | tf_op jit(solution)/shard_map/pallas_call | solution.py:594
  45.3 0.0 collective-permute-done.3.from_z
  45.3 0.0 collective-permute-done.4.from_c
  45.3 1.5 %shard_map.86 = (f32[7,4,16,8,384]{4,3,2,1,0:T(8,128)S(1)}, f32[3,16,8,384]{3,2,1,0:T(8,128)S(1)}) custom-call(f32[4,16,8,384]{3,2,1,0:T(8,128)S(1)} %get-tuple-element.34.north, f32[6,16,8,384]{3,2,1,0:T(8,128)S(1)} %collective-permute-done.3.from_z, f32[6,16,8,384]{3,2,1,0:T(8,128)S(1)} %collective-permute-done.4.from_c), custom_call_target="tpu_custom_call" | custom-call | flops 200000000 | bytes 100000 | tf_op jit(solution)/shard_map/pallas_call | solution.py:594
  46.8 3.7 %shard_map.89 = (f32[4,16,8,384]{3,2,1,0:T(8,128)S(1)}, f32[3,16,8,384]{3,2,1,0:T(8,128)S(1)}, f32[3,16,8,384]{3,2,1,0:T(8,128)S(1)}) custom-call(f32[4,16,8,384]{3,2,1,0:T(8,128)S(1)} %get-tuple-element.31.field, f32[6,16,8,384]{3,2,1,0:T(8,128)S(1)} %collective-permute-done.3.from_z, f32[6,16,8,384]{3,2,1,0:T(8,128)S(1)} %collective-permute-done.4.from_c, ...), custom_call_target="tpu_custom_call" | custom-call | flops 6000000000 | bytes 100000 | tf_op jit(solution)/shard_map/pallas_call | solution.py:594
  50.5 3.8 %collective-permute-start.8 = (f32[3,16,8,384]{3,2,1,0:T(8,128)S(1)}, f32[3,16,8,384]{3,2,1,0:T(8,128)S(1)}, u32[]{:S(2)}, u32[]{:S(2)}) collective-permute-start(f32[3,16,8,384]{3,2,1,0:T(8,128)S(1)} %get-tuple-element.41), channel_id=1, source_target_pairs={{1,2},{2,1},{3,4},{4,3},{5,6},{6,5},{9,10},{10,9},{11,12},{12,11},... | collective-permute-start | bytes 1769480 | tf_op jit(solution)/shard_map/ppermute | solution.py:623
  54.3 0.1 collective-permute-start.9
  54.3 7.5 %collective-permute-done.8.from_z = f32[3,16,8,384]{3,2,1,0:T(8,128)S(1)} collective-permute-done((f32[3,16,8,384]{3,2,1,0:T(8,128)S(1)}, f32[3,16,8,384]{3,2,1,0:T(8,128)S(1)}, u32[]{:S(2)}, u32[]{:S(2)}) %collective-permute-start.8) | collective-permute-done | bytes 589856 | tf_op jit(solution)/shard_map/ppermute | solution.py:623
  61.8 0.0 collective-permute-done.9.from_c
  61.8 2.9 %shard_map.90 = (f32[4,4,8,384]{3,2,1,0:T(8,128)S(1)}, f32[4,4,8,384]{3,2,1,0:T(8,128)S(1)}, f32[4,4,8,384]{3,2,1,0:T(8,128)S(1)}, f32[4,4,8,384]{3,2,1,0:T(8,128)S(1)}) custom-call(f32[4,16,8,384]{3,2,1,0:T(8,128)S(1)} %get-tuple-element.40.field, f32[3,16,8,384]{3,2,1,0:T(8,128)S(1)} %collective-permute-done.8.from_z, ...), custom_call_target="tpu_custom_call" | custom-call | flops 3500000000 | bytes 100000 | tf_op jit(solution)/shard_map/pallas_call | solution.py:594
  64.7 1.1 %collective-permute-start.10 = (f32[4,4,8,384]{3,2,1,0:T(8,128)S(1)}, f32[4,4,8,384]{3,2,1,0:T(8,128)S(1)}, u32[]{:S(2)}, u32[]{:S(2)}) collective-permute-start(f32[4,4,8,384]{3,2,1,0:T(8,128)S(1)} %get-tuple-element.44), channel_id=1, source_target_pairs={{0,8},{8,0},{16,24},{24,16},{1,9},{9,1},{17,25},{25,17},{2,10},{10... | collective-permute-start | bytes 589832 | tf_op jit(solution)/shard_map/ppermute | solution.py:641
  65.8 1.0 %collective-permute-start.11 = (f32[4,4,8,384]{3,2,1,0:T(8,128)S(1)}, f32[4,4,8,384]{3,2,1,0:T(8,128)S(1)}, u32[]{:S(2)}, u32[]{:S(2)}) collective-permute-start(f32[4,4,8,384]{3,2,1,0:T(8,128)S(1)} %get-tuple-element.45), channel_id=1, source_target_pairs={{0,16},{8,24},{16,0},{24,8},{1,17},{9,25},{17,1},{25,9},{2,18},{10... | collective-permute-start | bytes 589832 | tf_op jit(solution)/shard_map/ppermute | solution.py:641
  66.8 1.5 %collective-permute-start.12 = (f32[4,4,8,384]{3,2,1,0:T(8,128)S(1)}, f32[4,4,8,384]{3,2,1,0:T(8,128)S(1)}, u32[]{:S(2)}, u32[]{:S(2)}) collective-permute-start(f32[4,4,8,384]{3,2,1,0:T(8,128)S(1)} %get-tuple-element.46), channel_id=1, source_target_pairs={{0,24},{8,16},{16,8},{24,0},{1,25},{9,17},{17,9},{25,1},{2,26},{10... | collective-permute-start | bytes 589832 | tf_op jit(solution)/shard_map/ppermute | solution.py:641
  68.3 4.3 %collective-permute-done.10.refs_1_ = f32[4,4,8,384]{3,2,1,0:T(8,128)S(1)} collective-permute-done((f32[4,4,8,384]{3,2,1,0:T(8,128)S(1)}, f32[4,4,8,384]{3,2,1,0:T(8,128)S(1)}, u32[]{:S(2)}, u32[]{:S(2)}) %collective-permute-start.10) | collective-permute-done | bytes 196640 | tf_op jit(solution)/shard_map/ppermute | solution.py:641
  72.5 0.7 collective-permute-done.11.refs_2_
  73.2 3.4 %collective-permute-done.12.refs_3_ = f32[4,4,8,384]{3,2,1,0:T(8,128)S(1)} collective-permute-done((f32[4,4,8,384]{3,2,1,0:T(8,128)S(1)}, f32[4,4,8,384]{3,2,1,0:T(8,128)S(1)}, u32[]{:S(2)}, u32[]{:S(2)}) %collective-permute-start.12) | collective-permute-done | bytes 196640 | tf_op jit(solution)/shard_map/ppermute | solution.py:641
  76.6 1.4 %shard_map.91 = f32[4,360,128]{2,1,0:T(8,128)} custom-call(f32[4,4,8,384]{3,2,1,0:T(8,128)S(1)} %get-tuple-element.43.refs_0_, f32[4,4,8,384]{3,2,1,0:T(8,128)S(1)} %collective-permute-done.10.refs_1_, f32[4,4,8,384]{3,2,1,0:T(8,128)S(1)} %collective-permute-done.11.refs_2_, f32[4,4,8,384]{3,2,1,0:T(8,128)S(1)} %collective-permute-done.12.refs_3_), custom_call_target="tpu_custom_call" | custom-call | flops 1000000000 | bytes 100000 | tf_op jit(solution)/shard_map/pallas_call | solution.py:594
  (1 shorter events, 0.0 us)
Async XLA Ops:
  2.7 12.1 %collective-permute-start = (f32[8,4,8,384]{3,2,1,0:T(8,128)S(1)}, f32[8,4,8,384]{3,2,1,0:T(8,128)S(1)}, u32[]{:S(2)}, u32[]{:S(2)}) collective-permute-start(f32[8,4,8,384]{3,2,1,0:T(8,128)S(1)} %get-tuple-element.27), channel_id=1, source_target_pairs={{0,8},{8,0},{16,24},{24,16},{1,9},{9,1},{17,25},{25,17},{2,10},{10... | collective-permute-start | bytes 1179656 | tf_op jit(solution)/shard_map/ppermute | solution.py:641
  4.3 19.0 %collective-permute-start.1 = (f32[8,4,8,384]{3,2,1,0:T(8,128)S(1)}, f32[8,4,8,384]{3,2,1,0:T(8,128)S(1)}, u32[]{:S(2)}, u32[]{:S(2)}) collective-permute-start(f32[8,4,8,384]{3,2,1,0:T(8,128)S(1)} %get-tuple-element.28), channel_id=1, source_target_pairs={{0,16},{8,24},{16,0},{24,8},{1,17},{9,25},{17,1},{25,9},{2,18},{10... | collective-permute-start | bytes 1179656 | tf_op jit(solution)/shard_map/ppermute | solution.py:641
  5.8 17.5 %collective-permute-start.2 = (f32[8,4,8,384]{3,2,1,0:T(8,128)S(1)}, f32[8,4,8,384]{3,2,1,0:T(8,128)S(1)}, u32[]{:S(2)}, u32[]{:S(2)}) collective-permute-start(f32[8,4,8,384]{3,2,1,0:T(8,128)S(1)} %get-tuple-element.29), channel_id=1, source_target_pairs={{0,24},{8,16},{16,8},{24,0},{1,25},{9,17},{17,9},{25,1},{2,26},{10... | collective-permute-start | bytes 1179656 | tf_op jit(solution)/shard_map/ppermute | solution.py:641
  6.3 20.5 %copy-start.1 = (bf16[2,768,384]{2,1,0:T(8,128)(2,1)S(1)}, bf16[2,768,384]{2,1,0:T(8,128)(2,1)}, u32[]{:S(2)}) copy-start(bf16[2,768,384]{2,1,0:T(8,128)(2,1)} %constant.4.clone.refs_4_.refs_0_) | copy-start | bytes 3538948
  7.3 19.5 %copy-start = (bf16[2,768,384]{2,1,0:T(8,128)(2,1)S(1)}, bf16[2,768,384]{2,1,0:T(8,128)(2,1)}, u32[]{:S(2)}) copy-start(bf16[2,768,384]{2,1,0:T(8,128)(2,1)} %constant.5.clone.refs_5_.refs_1_) | copy-start | bytes 3538948
  23.3 13.0 %collective-permute-start.7 = (f32[2,16,8,384]{3,2,1,0:T(8,128)S(1)}, f32[2,16,8,384]{3,2,1,0:T(8,128)S(1)}, u32[]{:S(2)}, u32[]{:S(2)}) collective-permute-start(f32[2,16,8,384]{3,2,1,0:T(8,128)S(1)} %shard_map.84.refs_6_.refs_0_), channel_id=1, source_target_pairs={{0,24},{8,16},{16,8},{24,0},{1,25},{9,17},{17,9},{25,1},{2,26},{10... | collective-permute-start | bytes 1179656 | tf_op jit(solution)/shard_map/ppermute | solution.py:641
  24.8 17.6 %collective-permute-start.6 = (f32[2,16,8,384]{3,2,1,0:T(8,128)S(1)}, f32[2,16,8,384]{3,2,1,0:T(8,128)S(1)}, u32[]{:S(2)}, u32[]{:S(2)}) collective-permute-start(f32[2,16,8,384]{3,2,1,0:T(8,128)S(1)} %shard_map.84.refs_6_.refs_0_), channel_id=1, source_target_pairs={{0,16},{8,24},{16,0},{24,8},{1,17},{9,25},{17,1},{25,9},{2,18},{10... | collective-permute-start | bytes 1179656 | tf_op jit(solution)/shard_map/ppermute | solution.py:641
  26.0 16.4 %collective-permute-start.5 = (f32[2,16,8,384]{3,2,1,0:T(8,128)S(1)}, f32[2,16,8,384]{3,2,1,0:T(8,128)S(1)}, u32[]{:S(2)}, u32[]{:S(2)}) collective-permute-start(f32[2,16,8,384]{3,2,1,0:T(8,128)S(1)} %shard_map.84.refs_6_.refs_0_), channel_id=1, source_target_pairs={{0,8},{8,0},{16,24},{24,16},{1,9},{9,1},{17,25},{25,17},{2,10},{10... | collective-permute-start | bytes 1179656 | tf_op jit(solution)/shard_map/ppermute | solution.py:641
  27.6 17.6 %collective-permute-start.3 = (f32[6,16,8,384]{3,2,1,0:T(8,128)S(1)}, f32[6,16,8,384]{3,2,1,0:T(8,128)S(1)}, u32[]{:S(2)}, u32[]{:S(2)}) collective-permute-start(f32[6,16,8,384]{3,2,1,0:T(8,128)S(1)} %get-tuple-element.32), channel_id=1, source_target_pairs={{1,2},{2,1},{3,4},{4,3},{5,6},{6,5},{9,10},{10,9},{11,12},{12,11},... | collective-permute-start | bytes 3538952 | tf_op jit(solution)/shard_map/ppermute | solution.py:623
  29.6 15.7 %collective-permute-start.4 = (f32[6,16,8,384]{3,2,1,0:T(8,128)S(1)}, f32[6,16,8,384]{3,2,1,0:T(8,128)S(1)}, u32[]{:S(2)}, u32[]{:S(2)}) collective-permute-start(f32[6,16,8,384]{3,2,1,0:T(8,128)S(1)} %get-tuple-element.33), channel_id=1, source_target_pairs={{0,1},{1,0},{2,3},{3,2},{4,5},{5,4},{6,7},{7,6},{8,9},{9,8},{10,11... | collective-permute-start | bytes 3538952 | tf_op jit(solution)/shard_map/ppermute | solution.py:624
  50.5 11.3 %collective-permute-start.8 = (f32[3,16,8,384]{3,2,1,0:T(8,128)S(1)}, f32[3,16,8,384]{3,2,1,0:T(8,128)S(1)}, u32[]{:S(2)}, u32[]{:S(2)}) collective-permute-start(f32[3,16,8,384]{3,2,1,0:T(8,128)S(1)} %get-tuple-element.41), channel_id=1, source_target_pairs={{1,2},{2,1},{3,4},{4,3},{5,6},{6,5},{9,10},{10,9},{11,12},{12,11},... | collective-permute-start | bytes 1769480 | tf_op jit(solution)/shard_map/ppermute | solution.py:623
  54.3 7.6 %collective-permute-start.9 = (f32[3,16,8,384]{3,2,1,0:T(8,128)S(1)}, f32[3,16,8,384]{3,2,1,0:T(8,128)S(1)}, u32[]{:S(2)}, u32[]{:S(2)}) collective-permute-start(f32[3,16,8,384]{3,2,1,0:T(8,128)S(1)} %get-tuple-element.42), channel_id=1, source_target_pairs={{0,1},{1,0},{2,3},{3,2},{4,5},{5,4},{6,7},{7,6},{8,9},{9,8},{10,11... | collective-permute-start | bytes 1769480 | tf_op jit(solution)/shard_map/ppermute | solution.py:624
  64.7 7.8 %collective-permute-start.10 = (f32[4,4,8,384]{3,2,1,0:T(8,128)S(1)}, f32[4,4,8,384]{3,2,1,0:T(8,128)S(1)}, u32[]{:S(2)}, u32[]{:S(2)}) collective-permute-start(f32[4,4,8,384]{3,2,1,0:T(8,128)S(1)} %get-tuple-element.44), channel_id=1, source_target_pairs={{0,8},{8,0},{16,24},{24,16},{1,9},{9,1},{17,25},{25,17},{2,10},{10... | collective-permute-start | bytes 589832 | tf_op jit(solution)/shard_map/ppermute | solution.py:641
  65.8 7.5 %collective-permute-start.11 = (f32[4,4,8,384]{3,2,1,0:T(8,128)S(1)}, f32[4,4,8,384]{3,2,1,0:T(8,128)S(1)}, u32[]{:S(2)}, u32[]{:S(2)}) collective-permute-start(f32[4,4,8,384]{3,2,1,0:T(8,128)S(1)} %get-tuple-element.45), channel_id=1, source_target_pairs={{0,16},{8,24},{16,0},{24,8},{1,17},{9,25},{17,1},{25,9},{2,18},{10... | collective-permute-start | bytes 589832 | tf_op jit(solution)/shard_map/ppermute | solution.py:641
  66.8 9.9 %collective-permute-start.12 = (f32[4,4,8,384]{3,2,1,0:T(8,128)S(1)}, f32[4,4,8,384]{3,2,1,0:T(8,128)S(1)}, u32[]{:S(2)}, u32[]{:S(2)}) collective-permute-start(f32[4,4,8,384]{3,2,1,0:T(8,128)S(1)} %get-tuple-element.46), channel_id=1, source_target_pairs={{0,24},{8,16},{16,8},{24,0},{1,25},{9,17},{17,9},{25,1},{2,26},{10... | collective-permute-start | bytes 589832 | tf_op jit(solution)/shard_map/ppermute | solution.py:641
